TPU v7x, 32 devices: a whole 2x2x4 slice. The times are simulated.
32 devices in a mesh: groups: 2 (over x), tensor: 16 (over z, y, core).
Axes of the slice: x: 2, y: 2, z: 4, core: 2. Of those that a mesh axis runs over, the one named last changes fastest.
Arguments:
- tokens: bfloat16 [4096, 6144], P(('groups', 'tensor')), parts along dimension 0, may hold values from -6 to 6
- expert_ids: int32 [4096, 4], P(('groups', 'tensor')), parts along dimension 0, may hold values from 0 to 15, as said below
- gates: float32 [4096, 4], P(('groups', 'tensor')), parts along dimension 0, may hold values from 0.2 to 1
- gate_weight: bfloat16 [10752, 6144], P('tensor'), may hold values from -0.078125 to 0.078125
- up_weight: bfloat16 [10752, 6144], P('tensor'), may hold values from -0.078125 to 0.078125
- down_weight: bfloat16 [10752, 6144], P('tensor'), may hold values from -0.078125 to 0.078125
Outputs:
- mixed: bfloat16 [4096, 6144], P(('groups', 'tensor')), parts along dimension 0
There are 2 independent parts, one for each index of `groups`. A program takes and returns all parts, laid end to end along the dimension named above; an argument that names none is the same for every part. Nothing has to cross between parts.
Inputs may be any that keep to these rules, and one draw needn't show every extreme that they name: `expert_ids`: each row names 4 different experts. In every block of 128 rows of one index of tensor, expert 0 is named by 2 to 12 rows, and by exactly 12 rows in at least one block.
All inputs are finite; a program needn't handle non-finite values.
Results may differ from a plain program's by a relative error of at most 0.0085.
Values may be sent and summed in bfloat16 or wider, within the bound.
No kernel may reach another device: no remote copies, remote signals or barrier semaphores. Data moves between devices by JAX's collectives and lax.ppermute only.
A program may use at most 128 MiB of HBM per device.

v0:
```python
import jax
import jax.numpy as jnp
from jax import lax
from jax.sharding import PartitionSpec as P

CAP = 12


def body(tokens, expert_ids, gates, gate_weight, up_weight, down_weight):
    expert_hits = expert_ids == 0
    routed = jnp.any(expert_hits, axis=1)
    slot_index = jnp.cumsum(routed.astype(jnp.int32)) - 1
    slot_match = routed[:, None] & (
        slot_index[:, None] == jnp.arange(CAP, dtype=jnp.int32)[None, :]
    )
    chooser = slot_match.astype(jnp.bfloat16)
    slot_rows = lax.dot_general(
        chooser, tokens, (((0,), (0,)), ((), ())), preferred_element_type=jnp.float32
    ).astype(jnp.bfloat16)
    contract = (((1,), (1,)), ((), ()))
    block_rows = lax.all_gather(slot_rows, "tensor", axis=0, tiled=True)
    gate_pre = lax.dot_general(
        block_rows, gate_weight, contract, preferred_element_type=jnp.float32
    )
    up_pre = lax.dot_general(block_rows, up_weight, contract, preferred_element_type=jnp.float32)
    hidden = (jax.nn.silu(gate_pre) * up_pre).astype(jnp.bfloat16)
    columns = lax.all_to_all(down_weight, "tensor", split_axis=1, concat_axis=0, tiled=True)
    partial_value = jnp.dot(
        lax.all_gather(hidden, "tensor", axis=1, tiled=True),
        columns,
        preferred_element_type=jnp.float32,
    )
    expert_out = lax.all_to_all(
        partial_value.astype(jnp.bfloat16), "tensor", split_axis=0, concat_axis=1, tiled=True
    )
    gate_share = jnp.sum(jnp.where(expert_hits, gates, 0.0), axis=1)
    slot_weights = jnp.where(slot_match, gate_share[:, None], 0.0)
    picked = jnp.dot(slot_weights, expert_out.astype(jnp.float32), precision=lax.Precision.HIGHEST)
    return picked.astype(jnp.bfloat16)


def solution(mesh):
    in_specs = (
        P(("groups", "tensor"), None),
        P(("groups", "tensor"), None),
        P(("groups", "tensor"), None),
        P("tensor", None),
        P("tensor", None),
        P("tensor", None),
    )
    out_specs = P(("groups", "tensor"), None)
    return jax.shard_map(body, mesh=mesh, in_specs=in_specs, out_specs=out_specs, check_vma=False)
```

profile of v0, /device:TPU:0, one launch (start us, length us, event | category | flops | bytes accessed | tf_op | source)
XLA Modules:
  0.0 306.5 jit_solution(9653190280220292206)
XLA Ops:
  6.5 0.0 copy-start
  6.5 7.5 %copy.22 = bf16[84,16,8,384]{3,2,0,1:T(8,128)(2,1)} copy(bf16[84,16,8,384]{3,2,1,0:T(8,128)(2,1)} %bitcast.30) | data formatting | bytes 16515072 | tf_op jit(solution)/shard_map/all_to_all | solution.py:27
  14.0 7.6 %all-to-all-start = ((bf16[672,16,384]{2,0,1:T(8,128)(2,1)}), bf16[672,16,384]{2,0,1:T(8,128)(2,1)}, u32[]{:S(2)}, u32[]{:S(2)}) async-start(bf16[672,16,384]{2,0,1:T(8,128)(2,1)} %bitcast.29), calls=%async_computation | async-start | bytes 16515072 | tf_op jit(solution)/shard_map/all_to_all | solution.py:27
  21.6 0.0 all-gather.5.cloned.1.call-start
  21.6 0.0 copy-done.2
  21.7 0.1 copy.15
  21.8 0.2 reduce-window.8
  22.0 0.1 add_reduce_fusion
  22.1 1.1 fusion
  23.2 0.0 all-gather.5.cloned.1.call-update
  23.2 0.0 all-gather.7.cloned.1.call-start
  23.3 140.5 %all-gather.5.cloned.1.call-done = bf16[16,12,6144]{2,1,0:T(8,128)(2,1)} async-done(((bf16[1,12,6144]{2,1,0:T(8,128)(2,1)}), bf16[16,12,6144]{2,1,0:T(8,128)(2,1)}) %all-gather.5.cloned.1.call-update) | async-done | bytes 2359312 | tf_op jit(solution)/shard_map/all_gather | solution.py:21
  163.8 4.2 %reshape.38 = bf16[192,6144]{1,0:T(8,128)(2,1)} reshape(bf16[16,12,6144]{2,1,0:T(8,128)(2,1)} %all-gather.5.cloned.1.call-done) | data formatting | bytes 4718592
  168.1 6.9 %fusion.14 = f32[192,672]{1,0:T(8,128)S(1)} fusion(bf16[192,6144]{1,0:T(8,128)(2,1)} %reshape.38, bf16[672,6144]{1,0:T(8,128)(2,1)} %param.9), kind=kOutput, calls=%fused_computation.22 | convolution fusion | flops 1585446912 | bytes 11132928 | tf_op jit(solution)/shard_map/dot_general | solution.py:22
  175.0 0.0 copy-done.1
  175.0 6.8 %fusion.2 = bf16[1,672,192]{1,2,0:T(8,128)(2,1)} fusion(bf16[192,6144]{1,0:T(8,128)(2,1)S(1)} %copy-done.1, bf16[672,6144]{1,0:T(8,128)(2,1)} %param.10, f32[192,672]{1,0:T(8,128)S(1)} %fusion.14), kind=kOutput, calls=%fused_computation.6 | convolution fusion | flops 1586221056 | bytes 11390976 | tf_op jit(solution)/shard_map/dot_general | solution.py:25
  181.8 0.0 all-gather.7.cloned.1.call-update
  181.8 79.3 %all-gather.7.cloned.1.call-done = bf16[16,672,192]{1,2,0:T(8,128)(2,1)} async-done(((bf16[1,672,192]{1,2,0:T(8,128)(2,1)}), bf16[16,672,192]{1,2,0:T(8,128)(2,1)}) %all-gather.7.cloned.1.call-update) | async-done | bytes 4128784 | tf_op jit(solution)/shard_map/all_gather | solution.py:29
  261.1 7.1 %copy.16 = bf16[16,672,192]{1,0,2:T(8,128)(2,1)} copy(bf16[16,672,192]{1,2,0:T(8,128)(2,1)} %all-gather.7.cloned.1.call-done) | data formatting | bytes 8257536 | tf_op jit(solution)/shard_map/all_gather | solution.py:29
  268.2 9.7 %reshape.40 = bf16[10752,192]{0,1:T(8,128)(2,1)} reshape(bf16[16,672,192]{1,0,2:T(8,128)(2,1)} %copy.16) | data formatting | bytes 8257536
  277.9 0.0 all-to-all-done
  277.9 6.9 %convolution_convert_fusion.2 = bf16[192,384]{1,0:T(8,128)(2,1)S(1)} fusion(bf16[10752,192]{0,1:T(8,128)(2,1)} %reshape.40, bf16[10752,384]{1,0:T(8,128)(2,1)} %bitcast.5), kind=kOutput, calls=%fused_computation.7 | convolution fusion | flops 1585520640 | bytes 12533760 | tf_op jit(solution)/shard_map/dot_general | solution.py:28
  284.9 12.1 %all_to_all.38 = bf16[16,12,384]{2,1,0:T(8,128)(2,1)S(1)} all-to-all(bf16[16,12,384]{2,1,0:T(8,128)(2,1)S(1)} %all_to_all.32), channel_id=1, replica_groups=mesh['groups'=2,'tensor'=16] {'tensor'}, dimensions={0} | all-to-all | bytes 294912 | tf_op jit(solution)/shard_map/all_to_all | solution.py:33
  297.1 2.6 convolution_convert_fusion
  (12 shorter events, 0.2 us)
Async XLA Ops:
  6.5 15.6 %copy-start = (bf16[128,6144]{1,0:T(8,128)(2,1)S(1)}, bf16[128,6144]{1,0:T(8,128)(2,1)}, u32[]{:S(2)}) copy-start(bf16[128,6144]{1,0:T(8,128)(2,1)} %param.6) | copy-start | bytes 4718596
  14.0 7.6 %copy-start.2 = (f32[128,4]{0,1:T(4,128)S(1)}, f32[128,4]{0,1:T(4,128)}, u32[]{:S(2)}) copy-start(f32[128,4]{0,1:T(4,128)} %param.8) | copy-start | bytes 6148
  14.0 7.6 %copy-start.3 = (s32[128,4]{0,1:T(4,128)S(1)}, s32[128,4]{0,1:T(4,128)}, u32[]{:S(2)}) copy-start(s32[128,4]{0,1:T(4,128)} %param.7) | copy-start | bytes 6148
  14.0 263.9 %all-to-all-start = ((bf16[672,16,384]{2,0,1:T(8,128)(2,1)}), bf16[672,16,384]{2,0,1:T(8,128)(2,1)}, u32[]{:S(2)}, u32[]{:S(2)}) async-start(bf16[672,16,384]{2,0,1:T(8,128)(2,1)} %bitcast.29), calls=%async_computation | async-start | bytes 16515072 | tf_op jit(solution)/shard_map/all_to_all | solution.py:27
  21.6 142.2 %all-gather.5.cloned.1.call-start = ((), (), s32[]{:S(2)}) async-start(), calls=%async_computation.2 | async-start | bytes 3342336 | tf_op jit(solution)/shard_map/all_gather | solution.py:21
  23.2 237.9 %all-gather.7.cloned.1.call-start = ((), (), s32[]{:S(2)}) async-start(), calls=%async_computation.3 | async-start | bytes 5013504 | tf_op jit(solution)/shard_map/all_gather | solution.py:29
  168.1 6.9 %copy-start.1 = (bf16[192,6144]{1,0:T(8,128)(2,1)S(1)}, bf16[192,6144]{1,0:T(8,128)(2,1)}, u32[]{:S(2)}) copy-start(bf16[192,6144]{1,0:T(8,128)(2,1)} %reshape.38) | copy-start | bytes 7077892
Sparse Core Ops, SparseCore 0:
  24.7 139.0 all-gather.4
  181.9 79.1 all-gather.6
where the time goes:
time: 307 us; the launch traced here: 306 us
  waiting for transfers between devices  220 us (72%)
  local copies, waits for them, and re-layouts  28.8 us (9%)
  matrix products  24.3 us (8%)
  between operations  13.5 us (4%)
  blocking collectives  12.1 us (4%)
  starting transfers between devices  7.64 us (2%)
    all_gather x1, waiting for transfers between devices, body(): block_rows = lax.all_gather(slot_rows, 'tensor', axis=0, tiled=True)  141 us
    all_gather x1, waiting for transfers between devices, body(): lax.all_gather(hidden, 'tensor', axis=1, tiled=True)  79.3 us
    unnamed x12, local copies, waits for them, and re-layouts  14 us
    all_to_all x1, blocking collectives, body(): lax.all_to_all(partial_value.astype(jnp.bfloat16), 'tensor', split_axis=0...  12.1 us
    all_to_all x1, starting transfers between devices, body(): lax.all_to_all(down_weight, 'tensor', split_axis=1, concat_axis=0, tiled=...  7.56 us
    all_to_all x1, local copies, waits for them, and re-layouts, body(): lax.all_to_all(down_weight, 'tensor', split_axis=1, concat_axis=0, tiled=...  7.47 us
    all_gather x1, local copies, waits for them, and re-layouts, body(): lax.all_gather(hidden, 'tensor', axis=1, tiled=True)  7.07 us
    dot_general x1, matrix products, body(): lax.dot_general(block_rows, gate_weight, contract, preferred_element_type...  6.92 us
  transfers between devices with their start and end apart: 3, of which 2 were waited for; matrix products, arithmetic and copies ran while one was open for 12% of the time, Pallas kernels for 0%

commit v1 on v0

v1 whole, which is shorter than its diff:
```python
import jax
import jax.numpy as jnp
from jax import lax
from jax.experimental import pallas as pl
from jax.experimental.pallas import tpu as pltpu
from jax.sharding import PartitionSpec as P

CAP = 12
PAIR = 2 * CAP
F32 = jnp.float32
BF16 = jnp.bfloat16


def permutations(size):
    chips = size // 2
    order = list(range(0, chips, 2)) + list(range(chips - 1, 0, -2))

    def ring(step):
        pairs = []
        for place, chip in enumerate(order):
            pairs.append((2 * chip, 2 * order[(place + step) % chips]))
            pairs.append((2 * chip + 1, 2 * order[(place - step) % chips] + 1))
        return pairs

    return [(i, i ^ 1) for i in range(size)], ring(1), ring(2)


def halves(width):
    core = lax.rem(lax.axis_index("tensor"), 2)
    half = width // 2
    return core, pl.multiple_of(core * half, 128), pl.multiple_of((1 - core) * half, 128)


def choose(ids, core):
    tokens = ids.shape[1]
    routed = jnp.max(jnp.where(ids == 0, 1.0, 0.0), axis=0, keepdims=True)
    earlier = lax.broadcasted_iota(jnp.int32, (tokens, tokens), 0) < lax.broadcasted_iota(
        jnp.int32, (tokens, tokens), 1
    )
    before = jnp.dot(
        jnp.broadcast_to(routed, (8, tokens)).astype(BF16),
        jnp.where(earlier, 1.0, 0.0).astype(BF16),
        preferred_element_type=F32,
    )[:1]
    row = lax.broadcasted_iota(jnp.int32, (PAIR, tokens), 0) - core * CAP
    return jnp.where((row.astype(F32) == before) & (routed > 0.0), 1.0, 0.0)


def compact_kernel(ids_ref, tokens_ref, out_ref):
    width = tokens_ref.shape[1]
    core, first, second = halves(width)
    chooser = choose(ids_ref[...], core).astype(BF16)
    for place, start in enumerate((first, second)):
        out_ref[place * PAIR : (place + 1) * PAIR, :] = jnp.dot(
            chooser, tokens_ref[:, pl.ds(start, width // 2)], preferred_element_type=F32
        ).astype(BF16)


def hidden_kernel(blocks, *refs):
    firsts, seconds = refs[:blocks], refs[blocks : 2 * blocks]
    gate_ref, up_ref, out_ref, rows_first, rows_second = refs[2 * blocks :]
    units, width = gate_ref.shape
    half = width // 2
    _, first, second = halves(width)
    for j in range(blocks):
        rows_first[j * PAIR : (j + 1) * PAIR, :] = firsts[j][...]
        rows_second[j * PAIR : (j + 1) * PAIR, :] = seconds[j][...]
    contract = (((1,), (1,)), ((), ()))

    def product(weight_ref, start, size):
        return lax.dot_general(
            rows_first[...],
            weight_ref[start : start + size, pl.ds(first, half)],
            contract,
            preferred_element_type=F32,
        ) + lax.dot_general(
            rows_second[...],
            weight_ref[start : start + size, pl.ds(second, half)],
            contract,
            preferred_element_type=F32,
        )

    for start in range(0, units, 256):
        size = min(256, units - start)
        gate = product(gate_ref, start, size)
        up = product(up_ref, start, size)
        out_ref[:, start : start + size] = (gate / (1.0 + jnp.exp(-gate)) * up).astype(BF16)


def down_kernel(which, send_rows, hidden_ref, down_ref, send_ref, keep_ref):
    width = down_ref.shape[1]
    half = width // 2
    start = halves(width)[1 + which]
    tile = half // 3
    for part in range(3):
        columns = pl.ds(pl.multiple_of(start + part * tile, 128), tile)
        value = jnp.dot(hidden_ref[...], down_ref[:, columns], preferred_element_type=F32)
        here = slice(part * tile, (part + 1) * tile)
        send_ref[:, here] = value[:send_rows].astype(BF16)
        keep_ref[:, here] = value[send_rows:]


def mix_kernel(ids_ref, gates_ref, first_ref, second_ref, own_first, own_second, sibling_ref, out_ref):
    width = out_ref.shape[1]
    core, first, second = halves(width)
    ids = ids_ref[...]
    tokens = ids.shape[1]
    chooser = choose(ids, core).astype(BF16)
    share = jnp.sum(jnp.where(ids == 0, gates_ref[...], 0.0), axis=0, keepdims=True)
    share = jnp.broadcast_to(share, (tokens, tokens)).T[:, :1]
    sibling = sibling_ref[...].astype(F32)
    for start, ring_ref, own, other in (
        (first, first_ref, own_first, sibling[PAIR:]),
        (second, second_ref, own_second, sibling[:PAIR]),
    ):
        rows = (ring_ref[...].astype(F32) + own[...] + other).astype(BF16)
        picked = lax.dot_general(
            chooser, rows, (((0,), (0,)), ((), ())), preferred_element_type=F32
        )
        out_ref[:, pl.ds(start, width // 2)] = (share * picked).astype(BF16)


def call(kernel, out_shape, *args, scratch=(), flops=0):
    moved = sum(a.size * a.dtype.itemsize for a in args)
    return pl.pallas_call(
        kernel,
        out_shape=out_shape,
        scratch_shapes=list(scratch),
        compiler_params=pltpu.CompilerParams(vmem_limit_bytes=56 * 2**20),
        cost_estimate=pl.CostEstimate(flops=flops, bytes_accessed=moved, transcendentals=0),
    )(*args)


def body(size, tokens, expert_ids, gates, gate_weight, up_weight, down_weight):
    width = tokens.shape[1]
    half = width // 2
    units = gate_weight.shape[0]
    chips = size // 2
    reach = chips // 2
    rows = chips * PAIR
    pair_core, ring_one, ring_two = permutations(size)

    def swap(a):
        return lax.ppermute(a, "tensor", pair_core)

    def onward(a):
        return lax.ppermute(a, "tensor", ring_one)

    def two_on(a):
        return lax.ppermute(a, "tensor", ring_two)

    struct = jax.ShapeDtypeStruct
    ids = expert_ids.T
    own = call(compact_kernel, struct((2 * PAIR, half), BF16), ids, tokens)
    theirs = swap(own)
    chip_first = own[:PAIR] + theirs[PAIR:]
    chip_second = own[PAIR:] + theirs[:PAIR]

    behind = [(chip_first, chip_second)]
    ahead = [None]
    for _ in range(1, reach):
        first, second = (onward(a) for a in behind[-1])
        behind.append((first, second))
        ahead.append((swap(second), swap(first)))
    far_first = two_on(behind[reach - 2][0])
    far_second = swap(far_first)
    order = behind[1:] + [(far_first, far_second)] + ahead[1:] + [behind[0]]

    hidden = call(
        lambda *refs: hidden_kernel(chips, *refs),
        struct((rows, units), BF16),
        *[a for a, _ in order],
        *[b for _, b in order],
        gate_weight,
        up_weight,
        scratch=[pltpu.VMEM((rows, half), BF16)] * 2,
        flops=4 * rows * units * width,
    )

    def partial_sums(which, send_rows):
        return call(
            lambda *refs: down_kernel(which, send_rows, *refs),
            (struct((send_rows, half), BF16), struct((rows - send_rows, half), F32)),
            hidden,
            down_weight,
            flops=2 * rows * units * half,
        )

    near = (reach - 1) * PAIR
    send_second, keep_second = partial_sums(1, near + PAIR)
    send_first, keep_first = partial_sums(0, near)
    from_first = swap(send_second)
    from_second = swap(send_first)
    keep_far, keep_first = keep_first[:PAIR], keep_first[PAIR:]

    def chip_sum(keep, other, distance):
        here = slice((distance - 1) * PAIR, distance * PAIR)
        return keep[here] + other[here].astype(F32)

    far = two_on((keep_far + from_first[near:].astype(F32)).astype(BF16))
    sum_first = chip_sum(keep_first, from_first, reach - 1)
    sum_second = chip_sum(keep_second, from_second, reach - 1)
    for distance in range(reach - 1, 0, -1):
        first = onward(sum_first.astype(BF16)).astype(F32)
        second = onward(sum_second.astype(BF16)).astype(F32)
        if distance == reach - 1:
            first = first + far.astype(F32)
        if distance > 1:
            sum_first = first + chip_sum(keep_first, from_first, distance - 1)
            sum_second = second + chip_sum(keep_second, from_second, distance - 1)
    own_first, own_second = keep_first[near:], keep_second[near:]
    total = jnp.concatenate([first + own_first, second + own_second]).astype(BF16)
    return call(
        mix_kernel,
        struct(tokens.shape, BF16),
        ids,
        gates.T,
        first.astype(BF16),
        second.astype(BF16),
        own_first,
        own_second,
        swap(total),
    )


def solution(mesh):
    size = mesh.shape["tensor"]
    tokens = P(("groups", "tensor"), None)
    weights = P("tensor", None)
    return jax.shard_map(
        lambda *args: body(size, *args),
        mesh=mesh,
        in_specs=(tokens, tokens, tokens, weights, weights, weights),
        out_specs=tokens,
        check_vma=False,
    )
```

time: 307 us -> 84.2 us (0.27)
  waiting for transfers between devices: 220 us -> 21.2 us
  Pallas kernels: 0 us -> 30.2 us
  local copies, waits for them, and re-layouts: 28.8 us -> 1.43 us
  matrix products: 24.3 us -> 0 us
  starting transfers between devices: 7.64 us -> 27 us
  between operations: 13.5 us -> 0.27 us
  blocking collectives: 12.1 us -> 0 us
  other arithmetic: 0.32 us -> 3.89 us
    all_gather x2 -> x0, waiting for transfers between devices: 220 us -> none  [the longest x1 141 us: body(): block_rows = lax.all_gather(slot_rows, 'tensor', axis=0, tiled=True)]
    pallas_call x0 -> x5, Pallas kernels: none -> 30.2 us  [call(): pl.pallas_call(kernel, out_shape=out_shape, scratch_shapes=list(scratch),...]
    ppermute x0 -> x25, starting transfers between devices: none -> 27 us  [the longest x12 20 us: onward(): return lax.ppermute(a, 'tensor', ring_one)]
    dot_general x5 -> x0, matrix products: 24.3 us -> none  [the longest x1 6.92 us: body(): lax.dot_general(block_rows, gate_weight, contract, preferred_element_type...]
    ppermute x0 -> x25, waiting for transfers between devices: none -> 21.2 us  [the longest x12 11.9 us: onward(): return lax.ppermute(a, 'tensor', ring_one)]
    unnamed x12 -> x42, local copies, waits for them, and re-layouts: 14 us -> 1.43 us
    all_to_all x1 -> x0, blocking collectives: 12.1 us -> none  [body(): lax.all_to_all(partial_value.astype(jnp.bfloat16), 'tensor', split_axis=0...]
    all_to_all x1 -> x0, starting transfers between devices: 7.56 us -> none  [body(): lax.all_to_all(down_weight, 'tensor', split_axis=1, concat_axis=0, tiled=...]
  transfers between devices with their start and end apart: 3 -> 25, of which waited for: 2 -> 12; matrix products, arithmetic and copies ran while one was open for 12% -> 2% of each run, Pallas kernels for 0% -> 7%
where the time goes in v1:
time: 84.2 us; the launch traced here: 84 us
  Pallas kernels  30.2 us (36%)
  starting transfers between devices  27 us (32%)
  waiting for transfers between devices  21.2 us (25%)
  other arithmetic  3.89 us (5%)
  local copies, waits for them, and re-layouts  1.43 us (2%)
    pallas_call x5, Pallas kernels, call(): pl.pallas_call(kernel, out_shape=out_shape, scratch_shapes=list(scratch),...  30.2 us
    ppermute x12, starting transfers between devices, onward(): return lax.ppermute(a, 'tensor', ring_one)  20 us
    ppermute x12, waiting for transfers between devices, onward(): return lax.ppermute(a, 'tensor', ring_one)  11.9 us
    ppermute x2, waiting for transfers between devices, two_on(): return lax.ppermute(a, 'tensor', ring_two)  4.98 us
    ppermute x2, starting transfers between devices, two_on(): return lax.ppermute(a, 'tensor', ring_two)  4.92 us
    ppermute x11, waiting for transfers between devices, swap(): return lax.ppermute(a, 'tensor', pair_core)  4.3 us
    ppermute x11, starting transfers between devices, swap(): return lax.ppermute(a, 'tensor', pair_core)  2.03 us
  transfers between devices with their start and end apart: 25, of which 12 were waited for; matrix products, arithmetic and copies ran while one was open for 2% of the time, Pallas kernels for 7%

profile of v1, /device:TPU:0, one launch (start us, length us, event | category | flops | bytes accessed | tf_op | source)
XLA Modules:
  0.0 84.0 jit_solution(254079521408912855)
XLA Ops:
  0.0 2.6 %shard_map.64 = bf16[48,3072]{1,0:T(8,128)(2,1)} custom-call(s32[4,128]{1,0:T(4,128)} %bitcast.2, bf16[128,6144]{1,0:T(8,128)(2,1)} %tokens_ref.1), custom_call_target="tpu_custom_call" | custom-call | bytes 1574912 | tf_op jit(solution)/shard_map/pallas_call | solution.py:125
  3.1 1.4 %collective-permute-done = bf16[48,3072]{1,0:T(8,128)(2,1)S(1)} collective-permute-done((bf16[48,3072]{1,0:T(8,128)(2,1)}, bf16[48,3072]{1,0:T(8,128)(2,1)S(1)}, u32[]{:S(2)}, u32[]{:S(2)}) %collective-permute-start) | collective-permute-done | bytes 294944 | tf_op jit(solution)/shard_map/ppermute | solution.py:144
  5.5 3.0 %collective-permute-start.1 = (bf16[24,3072]{1,0:T(8,128)(2,1)S(1)}, bf16[24,3072]{1,0:T(8,128)(2,1)S(1)}, u32[]{:S(2)}, u32[]{:S(2)}) collective-permute-start(bf16[24,3072]{1,0:T(8,128)(2,1)S(1)} %get-tuple-element.20.refs_7_), channel_id=1, source_target_pairs={{0,4},{1,3},{4,8},{5,1},{8,12},{9,5},{12,14},{13,9},{14,10},{15,13... | collective-permute-start | bytes 442376 | tf_op jit(solution)/shard_map/ppermute | solution.py:147
  8.5 1.6 %collective-permute-start.5 = (bf16[24,3072]{1,0:T(8,128)(2,1)S(1)}, bf16[24,3072]{1,0:T(8,128)(2,1)S(1)}, u32[]{:S(2)}, u32[]{:S(2)}) collective-permute-start(bf16[24,3072]{1,0:T(8,128)(2,1)S(1)} %get-tuple-element.19.refs_15_), channel_id=1, source_target_pairs={{0,4},{1,3},{4,8},{5,1},{8,12},{9,5},{12,14},{13,9},{14,10},{15,13... | collective-permute-start | bytes 442376 | tf_op jit(solution)/shard_map/ppermute | solution.py:147
  10.1 1.5 %collective-permute-done.1.refs_0_ = bf16[24,3072]{1,0:T(8,128)(2,1)S(1)} collective-permute-done((bf16[24,3072]{1,0:T(8,128)(2,1)S(1)}, bf16[24,3072]{1,0:T(8,128)(2,1)S(1)}, u32[]{:S(2)}, u32[]{:S(2)}) %collective-permute-start.1) | collective-permute-done | bytes 147488 | tf_op jit(solution)/shard_map/ppermute | solution.py:147
  11.6 2.1 %collective-permute-start.2 = (bf16[24,3072]{1,0:T(8,128)(2,1)S(1)}, bf16[24,3072]{1,0:T(8,128)(2,1)S(1)}, u32[]{:S(2)}, u32[]{:S(2)}) collective-permute-start(bf16[24,3072]{1,0:T(8,128)(2,1)S(1)} %collective-permute-done.1.refs_0_), channel_id=1, source_target_pairs={{0,4},{1,3},{4,8},{5,1},{8,12},{9,5},{12,14},{13,9},{14,10},{15,13... | collective-permute-start | bytes 442376 | tf_op jit(solution)/shard_map/ppermute | solution.py:147
  13.7 1.6 %collective-permute-start.7 = (bf16[24,3072]{1,0:T(8,128)(2,1)S(1)}, bf16[24,3072]{1,0:T(8,128)(2,1)S(1)}, u32[]{:S(2)}, u32[]{:S(2)}) collective-permute-start(bf16[24,3072]{1,0:T(8,128)(2,1)S(1)} %collective-permute-done.5.refs_8_), channel_id=1, source_target_pairs={{0,4},{1,3},{4,8},{5,1},{8,12},{9,5},{12,14},{13,9},{14,10},{15,13... | collective-permute-start | bytes 442376 | tf_op jit(solution)/shard_map/ppermute | solution.py:147
  16.7 3.1 %collective-permute-start.4 = (bf16[24,3072]{1,0:T(8,128)(2,1)S(1)}, bf16[24,3072]{1,0:T(8,128)(2,1)S(1)}, u32[]{:S(2)}, u32[]{:S(2)}) collective-permute-start(bf16[24,3072]{1,0:T(8,128)(2,1)S(1)} %collective-permute-done.2.refs_1_), channel_id=1, source_target_pairs={{0,8},{1,7},{4,12},{5,3},{8,14},{9,1},{12,10},{13,5},{14,6},{15,9}... | collective-permute-start | bytes 442376 | tf_op jit(solution)/shard_map/ppermute | solution.py:150
  19.8 1.6 %collective-permute-start.3 = (bf16[24,3072]{1,0:T(8,128)(2,1)S(1)}, bf16[24,3072]{1,0:T(8,128)(2,1)S(1)}, u32[]{:S(2)}, u32[]{:S(2)}) collective-permute-start(bf16[24,3072]{1,0:T(8,128)(2,1)S(1)} %collective-permute-done.2.refs_1_), channel_id=1, source_target_pairs={{0,4},{1,3},{4,8},{5,1},{8,12},{9,5},{12,14},{13,9},{14,10},{15,13... | collective-permute-start | bytes 442376 | tf_op jit(solution)/shard_map/ppermute | solution.py:147
  21.4 1.5 %collective-permute-start.9 = (bf16[24,3072]{1,0:T(8,128)(2,1)S(1)}, bf16[24,3072]{1,0:T(8,128)(2,1)S(1)}, u32[]{:S(2)}, u32[]{:S(2)}) collective-permute-start(bf16[24,3072]{1,0:T(8,128)(2,1)S(1)} %collective-permute-done.7.refs_9_), channel_id=1, source_target_pairs={{0,4},{1,3},{4,8},{5,1},{8,12},{9,5},{12,14},{13,9},{14,10},{15,13... | collective-permute-start | bytes 442376 | tf_op jit(solution)/shard_map/ppermute | solution.py:147
  25.1 1.6 %collective-permute-done.9.refs_10_ = bf16[24,3072]{1,0:T(8,128)(2,1)S(1)} collective-permute-done((bf16[24,3072]{1,0:T(8,128)(2,1)S(1)}, bf16[24,3072]{1,0:T(8,128)(2,1)S(1)}, u32[]{:S(2)}, u32[]{:S(2)}) %collective-permute-start.9) | collective-permute-done | bytes 147488 | tf_op jit(solution)/shard_map/ppermute | solution.py:147
  28.9 12.8 %shard_map.65.refs_0_ = bf16[192,672]{1,0:T(8,128)(2,1)} custom-call(bf16[24,3072]{1,0:T(8,128)(2,1)} %copy-done.7, bf16[24,3072]{1,0:T(8,128)(2,1)} %copy-done.9, bf16[24,3072]{1,0:T(8,128)(2,1)} %copy-done.14, bf16[24,3072]{1,0:T(8,128)(2,1)} %copy-done.13, bf16[24,3072]{1,0:T(8,128)(2,1)} %copy-done.12, bf16[24,3072]{1,0:T(8,128)(2,1)} %copy-done.17, ...), custom_call_target="tpu_custom_call" | custom-call | flops 3170893824 | bytes 18874368 | tf_op jit(solution)/shard_map/pallas_call | solution.py:125
  41.6 5.8 %shard_map.66 = (bf16[72,3072]{1,0:T(8,128)(2,1)}, f32[120,3072]{1,0:T(8,128)}) custom-call(bf16[192,672]{1,0:T(8,128)(2,1)} %shard_map.65.refs_0_, bf16[672,6144]{1,0:T(8,128)(2,1)} %refs_1_.3), custom_call_target="tpu_custom_call" | custom-call | flops 792723456 | bytes 8515584 | tf_op jit(solution)/shard_map/pallas_call | solution.py:125
  47.6 5.8 %shard_map.67 = (bf16[96,3072]{1,0:T(8,128)(2,1)}, f32[96,3072]{1,0:T(8,128)}) custom-call(bf16[192,672]{1,0:T(8,128)(2,1)} %shard_map.65.refs_0_, bf16[672,6144]{1,0:T(8,128)(2,1)} %refs_1_.3), custom_call_target="tpu_custom_call" | custom-call | flops 792723456 | bytes 8515584 | tf_op jit(solution)/shard_map/pallas_call | solution.py:125
  54.8 2.1 %collective-permute-start.21 = (bf16[24,3072]{1,0:T(8,128)(2,1)S(1)}, bf16[24,3072]{1,0:T(8,128)(2,1)S(1)}, u32[]{:S(2)}, u32[]{:S(2)}) collective-permute-start(bf16[24,3072]{1,0:T(8,128)(2,1)S(1)} %add_convert_fusion.4), channel_id=1, source_target_pairs={{0,4},{1,3},{4,8},{5,1},{8,12},{9,5},{12,14},{13,9},{14,10},{15,13... | collective-permute-start | bytes 442376 | tf_op jit(solution)/shard_map/ppermute | solution.py:147
  56.9 2.5 %collective-permute-start.16 = (bf16[24,3072]{1,0:T(8,128)(2,1)S(1)}, bf16[24,3072]{1,0:T(8,128)(2,1)S(1)}, u32[]{:S(2)}, u32[]{:S(2)}) collective-permute-start(bf16[24,3072]{1,0:T(8,128)(2,1)S(1)} %get-tuple-element.13), channel_id=1, source_target_pairs={{0,4},{1,3},{4,8},{5,1},{8,12},{9,5},{12,14},{13,9},{14,10},{15,13... | collective-permute-start | bytes 442376 | tf_op jit(solution)/shard_map/ppermute | solution.py:147
  59.5 1.8 %collective-permute-start.17 = (bf16[24,3072]{1,0:T(8,128)(2,1)S(1)}, bf16[24,3072]{1,0:T(8,128)(2,1)S(1)}, u32[]{:S(2)}, u32[]{:S(2)}) collective-permute-start(bf16[24,3072]{1,0:T(8,128)(2,1)S(1)} %get-tuple-element.14), channel_id=1, source_target_pairs={{0,8},{1,7},{4,12},{5,3},{8,14},{9,1},{12,10},{13,5},{14,6},{15,9}... | collective-permute-start | bytes 442376 | tf_op jit(solution)/shard_map/ppermute | solution.py:150
  62.8 4.4 %collective-permute-done.17 = bf16[24,3072]{1,0:T(8,128)(2,1)S(1)} collective-permute-done((bf16[24,3072]{1,0:T(8,128)(2,1)S(1)}, bf16[24,3072]{1,0:T(8,128)(2,1)S(1)}, u32[]{:S(2)}, u32[]{:S(2)}) %collective-permute-start.17) | collective-permute-done | bytes 147488 | tf_op jit(solution)/shard_map/ppermute | solution.py:150
  67.2 1.6 %collective-permute-start.18 = (bf16[24,3072]{1,0:T(8,128)(2,1)S(1)}, bf16[24,3072]{1,0:T(8,128)(2,1)S(1)}, u32[]{:S(2)}, u32[]{:S(2)}) collective-permute-start(bf16[24,3072]{1,0:T(8,128)(2,1)S(1)} %add_convert_fusion.6), channel_id=1, source_target_pairs={{0,4},{1,3},{4,8},{5,1},{8,12},{9,5},{12,14},{13,9},{14,10},{15,13... | collective-permute-start | bytes 442376 | tf_op jit(solution)/shard_map/ppermute | solution.py:147
  69.0 3.4 %collective-permute-done.18 = bf16[24,3072]{1,0:T(8,128)(2,1)S(1)} collective-permute-done((bf16[24,3072]{1,0:T(8,128)(2,1)S(1)}, bf16[24,3072]{1,0:T(8,128)(2,1)S(1)}, u32[]{:S(2)}, u32[]{:S(2)}) %collective-permute-start.18) | collective-permute-done | bytes 147488 | tf_op jit(solution)/shard_map/ppermute | solution.py:147
  72.5 1.6 %collective-permute-start.19 = (bf16[24,3072]{1,0:T(8,128)(2,1)S(1)}, bf16[24,3072]{1,0:T(8,128)(2,1)S(1)}, u32[]{:S(2)}, u32[]{:S(2)}) collective-permute-start(bf16[24,3072]{1,0:T(8,128)(2,1)S(1)} %add_convert_fusion.5), channel_id=1, source_target_pairs={{0,4},{1,3},{4,8},{5,1},{8,12},{9,5},{12,14},{13,9},{14,10},{15,13... | collective-permute-start | bytes 442376 | tf_op jit(solution)/shard_map/ppermute | solution.py:147
  74.9 2.8 %collective-permute-done.19.first_ref = bf16[24,3072]{1,0:T(8,128)(2,1)S(1)} collective-permute-done((bf16[24,3072]{1,0:T(8,128)(2,1)S(1)}, bf16[24,3072]{1,0:T(8,128)(2,1)S(1)}, u32[]{:S(2)}, u32[]{:S(2)}) %collective-permute-start.19) | collective-permute-done | bytes 147488 | tf_op jit(solution)/shard_map/ppermute | solution.py:147
  78.5 1.6 %collective-permute-done.24.sibling_ref = bf16[48,3072]{1,0:T(8,128)(2,1)S(1)} collective-permute-done((bf16[48,3072]{1,0:T(8,128)(2,1)S(1)}, bf16[48,3072]{1,0:T(8,128)(2,1)S(1)}, u32[]{:S(2)}, u32[]{:S(2)}) %collective-permute-start.24) | collective-permute-done | bytes 294944 | tf_op jit(solution)/shard_map/ppermute | solution.py:144
  80.8 3.2 %shard_map.68 = bf16[128,6144]{1,0:T(8,128)(2,1)} custom-call(s32[4,128]{1,0:T(4,128)} %bitcast.3, f32[4,128]{1,0:T(4,128)} %bitcast.4, bf16[24,3072]{1,0:T(8,128)(2,1)} %copy-done.5, bf16[24,3072]{1,0:T(8,128)(2,1)} %copy-done.4, f32[24,3072]{1,0:T(8,128)} %get-tuple-element.16.own_first, f32[24,3072]{1,0:T(8,128)} %get-tuple-element.18.own_second, ...), custom_call_target="tpu_custom_call" | custom-call | bytes 1183744 | tf_op jit(solution)/shard_map/pallas_call | solution.py:125
  (83 shorter events, 12.8 us)
Async XLA Ops:
  2.6 1.9 %collective-permute-start = (bf16[48,3072]{1,0:T(8,128)(2,1)}, bf16[48,3072]{1,0:T(8,128)(2,1)S(1)}, u32[]{:S(2)}, u32[]{:S(2)}) collective-permute-start(bf16[48,3072]{1,0:T(8,128)(2,1)} %shard_map.64), channel_id=1, source_target_pairs={{0,1},{1,0},{2,3},{3,2},{4,5},{5,4},{6,7},{7,6},{8,9},{9,8},{10,11... | collective-permute-start | bytes 884744 | tf_op jit(solution)/shard_map/ppermute | solution.py:144
  5.5 6.1 %collective-permute-start.1 = (bf16[24,3072]{1,0:T(8,128)(2,1)S(1)}, bf16[24,3072]{1,0:T(8,128)(2,1)S(1)}, u32[]{:S(2)}, u32[]{:S(2)}) collective-permute-start(bf16[24,3072]{1,0:T(8,128)(2,1)S(1)} %get-tuple-element.20.refs_7_), channel_id=1, source_target_pairs={{0,4},{1,3},{4,8},{5,1},{8,12},{9,5},{12,14},{13,9},{14,10},{15,13... | collective-permute-start | bytes 442376 | tf_op jit(solution)/shard_map/ppermute | solution.py:147
  8.5 5.1 %collective-permute-start.5 = (bf16[24,3072]{1,0:T(8,128)(2,1)S(1)}, bf16[24,3072]{1,0:T(8,128)(2,1)S(1)}, u32[]{:S(2)}, u32[]{:S(2)}) collective-permute-start(bf16[24,3072]{1,0:T(8,128)(2,1)S(1)} %get-tuple-element.19.refs_15_), channel_id=1, source_target_pairs={{0,4},{1,3},{4,8},{5,1},{8,12},{9,5},{12,14},{13,9},{14,10},{15,13... | collective-permute-start | bytes 442376 | tf_op jit(solution)/shard_map/ppermute | solution.py:147
  11.6 5.1 %collective-permute-start.2 = (bf16[24,3072]{1,0:T(8,128)(2,1)S(1)}, bf16[24,3072]{1,0:T(8,128)(2,1)S(1)}, u32[]{:S(2)}, u32[]{:S(2)}) collective-permute-start(bf16[24,3072]{1,0:T(8,128)(2,1)S(1)} %collective-permute-done.1.refs_0_), channel_id=1, source_target_pairs={{0,4},{1,3},{4,8},{5,1},{8,12},{9,5},{12,14},{13,9},{14,10},{15,13... | collective-permute-start | bytes 442376 | tf_op jit(solution)/shard_map/ppermute | solution.py:147
  13.7 7.7 %collective-permute-start.7 = (bf16[24,3072]{1,0:T(8,128)(2,1)S(1)}, bf16[24,3072]{1,0:T(8,128)(2,1)S(1)}, u32[]{:S(2)}, u32[]{:S(2)}) collective-permute-start(bf16[24,3072]{1,0:T(8,128)(2,1)S(1)} %collective-permute-done.5.refs_8_), channel_id=1, source_target_pairs={{0,4},{1,3},{4,8},{5,1},{8,12},{9,5},{12,14},{13,9},{14,10},{15,13... | collective-permute-start | bytes 442376 | tf_op jit(solution)/shard_map/ppermute | solution.py:147
  15.3 7.7 %collective-permute-start.12 = (bf16[24,3072]{1,0:T(8,128)(2,1)S(1)}, bf16[24,3072]{1,0:T(8,128)(2,1)S(1)}, u32[]{:S(2)}, u32[]{:S(2)}) collective-permute-start(bf16[24,3072]{1,0:T(8,128)(2,1)S(1)} %collective-permute-done.1.refs_0_), channel_id=1, source_target_pairs={{0,1},{1,0},{2,3},{3,2},{4,5},{5,4},{6,7},{7,6},{8,9},{9,8},{10,11... | collective-permute-start | bytes 442376 | tf_op jit(solution)/shard_map/ppermute | solution.py:144
  15.3 7.7 %collective-permute-start.6 = (bf16[24,3072]{1,0:T(8,128)(2,1)S(1)}, bf16[24,3072]{1,0:T(8,128)(2,1)S(1)}, u32[]{:S(2)}, u32[]{:S(2)}) collective-permute-start(bf16[24,3072]{1,0:T(8,128)(2,1)S(1)} %collective-permute-done.5.refs_8_), channel_id=1, source_target_pairs={{0,1},{1,0},{2,3},{3,2},{4,5},{5,4},{6,7},{7,6},{8,9},{9,8},{10,11... | collective-permute-start | bytes 442376 | tf_op jit(solution)/shard_map/ppermute | solution.py:144
  16.7 7.3 %collective-permute-start.4 = (bf16[24,3072]{1,0:T(8,128)(2,1)S(1)}, bf16[24,3072]{1,0:T(8,128)(2,1)S(1)}, u32[]{:S(2)}, u32[]{:S(2)}) collective-permute-start(bf16[24,3072]{1,0:T(8,128)(2,1)S(1)} %collective-permute-done.2.refs_1_), channel_id=1, source_target_pairs={{0,8},{1,7},{4,12},{5,3},{8,14},{9,1},{12,10},{13,5},{14,6},{15,9}... | collective-permute-start | bytes 442376 | tf_op jit(solution)/shard_map/ppermute | solution.py:150
  19.8 5.3 %collective-permute-start.3 = (bf16[24,3072]{1,0:T(8,128)(2,1)S(1)}, bf16[24,3072]{1,0:T(8,128)(2,1)S(1)}, u32[]{:S(2)}, u32[]{:S(2)}) collective-permute-start(bf16[24,3072]{1,0:T(8,128)(2,1)S(1)} %collective-permute-done.2.refs_1_), channel_id=1, source_target_pairs={{0,4},{1,3},{4,8},{5,1},{8,12},{9,5},{12,14},{13,9},{14,10},{15,13... | collective-permute-start | bytes 442376 | tf_op jit(solution)/shard_map/ppermute | solution.py:147
  21.4 5.3 %collective-permute-start.9 = (bf16[24,3072]{1,0:T(8,128)(2,1)S(1)}, bf16[24,3072]{1,0:T(8,128)(2,1)S(1)}, u32[]{:S(2)}, u32[]{:S(2)}) collective-permute-start(bf16[24,3072]{1,0:T(8,128)(2,1)S(1)} %collective-permute-done.7.refs_9_), channel_id=1, source_target_pairs={{0,4},{1,3},{4,8},{5,1},{8,12},{9,5},{12,14},{13,9},{14,10},{15,13... | collective-permute-start | bytes 442376 | tf_op jit(solution)/shard_map/ppermute | solution.py:147
  22.9 3.8 %collective-permute-start.13 = (bf16[24,3072]{1,0:T(8,128)(2,1)S(1)}, bf16[24,3072]{1,0:T(8,128)(2,1)S(1)}, u32[]{:S(2)}, u32[]{:S(2)}) collective-permute-start(bf16[24,3072]{1,0:T(8,128)(2,1)S(1)} %collective-permute-done.2.refs_1_), channel_id=1, source_target_pairs={{0,1},{1,0},{2,3},{3,2},{4,5},{5,4},{6,7},{7,6},{8,9},{9,8},{10,11... | collective-permute-start | bytes 442376 | tf_op jit(solution)/shard_map/ppermute | solution.py:144
  23.0 3.7 %collective-permute-start.8 = (bf16[24,3072]{1,0:T(8,128)(2,1)S(1)}, bf16[24,3072]{1,0:T(8,128)(2,1)S(1)}, u32[]{:S(2)}, u32[]{:S(2)}) collective-permute-start(bf16[24,3072]{1,0:T(8,128)(2,1)S(1)} %collective-permute-done.7.refs_9_), channel_id=1, source_target_pairs={{0,1},{1,0},{2,3},{3,2},{4,5},{5,4},{6,7},{7,6},{8,9},{9,8},{10,11... | collective-permute-start | bytes 442376 | tf_op jit(solution)/shard_map/ppermute | solution.py:144
  24.1 2.7 %collective-permute-start.11 = (bf16[24,3072]{1,0:T(8,128)(2,1)S(1)}, bf16[24,3072]{1,0:T(8,128)(2,1)S(1)}, u32[]{:S(2)}, u32[]{:S(2)}) collective-permute-start(bf16[24,3072]{1,0:T(8,128)(2,1)S(1)} %collective-permute-done.4.refs_3_), channel_id=1, source_target_pairs={{0,1},{1,0},{2,3},{3,2},{4,5},{5,4},{6,7},{7,6},{8,9},{9,8},{10,11... | collective-permute-start | bytes 442376 | tf_op jit(solution)/shard_map/ppermute | solution.py:144
  25.1 1.6 %collective-permute-start.14 = (bf16[24,3072]{1,0:T(8,128)(2,1)S(1)}, bf16[24,3072]{1,0:T(8,128)(2,1)S(1)}, u32[]{:S(2)}, u32[]{:S(2)}) collective-permute-start(bf16[24,3072]{1,0:T(8,128)(2,1)S(1)} %collective-permute-done.3.refs_2_), channel_id=1, source_target_pairs={{0,1},{1,0},{2,3},{3,2},{4,5},{5,4},{6,7},{7,6},{8,9},{9,8},{10,11... | collective-permute-start | bytes 442376 | tf_op jit(solution)/shard_map/ppermute | solution.py:144
  47.4 6.3 %collective-permute-start.20 = (bf16[72,3072]{1,0:T(8,128)(2,1)}, bf16[72,3072]{1,0:T(8,128)(2,1)S(1)}, u32[]{:S(2)}, u32[]{:S(2)}) collective-permute-start(bf16[72,3072]{1,0:T(8,128)(2,1)} %get-tuple-element.12), channel_id=1, source_target_pairs={{0,1},{1,0},{2,3},{3,2},{4,5},{5,4},{6,7},{7,6},{8,9},{9,8},{10,11... | collective-permute-start | bytes 1327112 | tf_op jit(solution)/shard_map/ppermute | solution.py:144
  53.4 3.5 %collective-permute-start.15 = (bf16[96,3072]{1,0:T(8,128)(2,1)}, bf16[96,3072]{1,0:T(8,128)(2,1)S(1)}, u32[]{:S(2)}, u32[]{:S(2)}) collective-permute-start(bf16[96,3072]{1,0:T(8,128)(2,1)} %get-tuple-element.10), channel_id=1, source_target_pairs={{0,1},{1,0},{2,3},{3,2},{4,5},{5,4},{6,7},{7,6},{8,9},{9,8},{10,11... | collective-permute-start | bytes 1769480 | tf_op jit(solution)/shard_map/ppermute | solution.py:144
  54.8 6.5 %collective-permute-start.21 = (bf16[24,3072]{1,0:T(8,128)(2,1)S(1)}, bf16[24,3072]{1,0:T(8,128)(2,1)S(1)}, u32[]{:S(2)}, u32[]{:S(2)}) collective-permute-start(bf16[24,3072]{1,0:T(8,128)(2,1)S(1)} %add_convert_fusion.4), channel_id=1, source_target_pairs={{0,4},{1,3},{4,8},{5,1},{8,12},{9,5},{12,14},{13,9},{14,10},{15,13... | collective-permute-start | bytes 442376 | tf_op jit(solution)/shard_map/ppermute | solution.py:147
  56.9 5.8 %collective-permute-start.16 = (bf16[24,3072]{1,0:T(8,128)(2,1)S(1)}, bf16[24,3072]{1,0:T(8,128)(2,1)S(1)}, u32[]{:S(2)}, u32[]{:S(2)}) collective-permute-start(bf16[24,3072]{1,0:T(8,128)(2,1)S(1)} %get-tuple-element.13), channel_id=1, source_target_pairs={{0,4},{1,3},{4,8},{5,1},{8,12},{9,5},{12,14},{13,9},{14,10},{15,13... | collective-permute-start | bytes 442376 | tf_op jit(solution)/shard_map/ppermute | solution.py:147
  59.5 7.7 %collective-permute-start.17 = (bf16[24,3072]{1,0:T(8,128)(2,1)S(1)}, bf16[24,3072]{1,0:T(8,128)(2,1)S(1)}, u32[]{:S(2)}, u32[]{:S(2)}) collective-permute-start(bf16[24,3072]{1,0:T(8,128)(2,1)S(1)} %get-tuple-element.14), channel_id=1, source_target_pairs={{0,8},{1,7},{4,12},{5,3},{8,14},{9,1},{12,10},{13,5},{14,6},{15,9}... | collective-permute-start | bytes 442376 | tf_op jit(solution)/shard_map/ppermute | solution.py:150
  61.4 7.5 %collective-permute-start.22 = (bf16[24,3072]{1,0:T(8,128)(2,1)S(1)}, bf16[24,3072]{1,0:T(8,128)(2,1)S(1)}, u32[]{:S(2)}, u32[]{:S(2)}) collective-permute-start(bf16[24,3072]{1,0:T(8,128)(2,1)S(1)} %add_convert_fusion.3), channel_id=1, source_target_pairs={{0,4},{1,3},{4,8},{5,1},{8,12},{9,5},{12,14},{13,9},{14,10},{15,13... | collective-permute-start | bytes 442376 | tf_op jit(solution)/shard_map/ppermute | solution.py:147
  67.2 5.2 %collective-permute-start.18 = (bf16[24,3072]{1,0:T(8,128)(2,1)S(1)}, bf16[24,3072]{1,0:T(8,128)(2,1)S(1)}, u32[]{:S(2)}, u32[]{:S(2)}) collective-permute-start(bf16[24,3072]{1,0:T(8,128)(2,1)S(1)} %add_convert_fusion.6), channel_id=1, source_target_pairs={{0,4},{1,3},{4,8},{5,1},{8,12},{9,5},{12,14},{13,9},{14,10},{15,13... | collective-permute-start | bytes 442376 | tf_op jit(solution)/shard_map/ppermute | solution.py:147
  68.9 5.2 %collective-permute-start.23 = (bf16[24,3072]{1,0:T(8,128)(2,1)S(1)}, bf16[24,3072]{1,0:T(8,128)(2,1)S(1)}, u32[]{:S(2)}, u32[]{:S(2)}) collective-permute-start(bf16[24,3072]{1,0:T(8,128)(2,1)S(1)} %add_convert_fusion.2), channel_id=1, source_target_pairs={{0,4},{1,3},{4,8},{5,1},{8,12},{9,5},{12,14},{13,9},{14,10},{15,13... | collective-permute-start | bytes 442376 | tf_op jit(solution)/shard_map/ppermute | solution.py:147
  72.5 5.2 %collective-permute-start.19 = (bf16[24,3072]{1,0:T(8,128)(2,1)S(1)}, bf16[24,3072]{1,0:T(8,128)(2,1)S(1)}, u32[]{:S(2)}, u32[]{:S(2)}) collective-permute-start(bf16[24,3072]{1,0:T(8,128)(2,1)S(1)} %add_convert_fusion.5), channel_id=1, source_target_pairs={{0,4},{1,3},{4,8},{5,1},{8,12},{9,5},{12,14},{13,9},{14,10},{15,13... | collective-permute-start | bytes 442376 | tf_op jit(solution)/shard_map/ppermute | solution.py:147
  78.5 1.6 %collective-permute-start.24 = (bf16[48,3072]{1,0:T(8,128)(2,1)S(1)}, bf16[48,3072]{1,0:T(8,128)(2,1)S(1)}, u32[]{:S(2)}, u32[]{:S(2)}) collective-permute-start(bf16[48,3072]{1,0:T(8,128)(2,1)S(1)} %pad_maximum_fusion), channel_id=1, source_target_pairs={{0,1},{1,0},{2,3},{3,2},{4,5},{5,4},{6,7},{7,6},{8,9},{9,8},{10,11... | collective-permute-start | bytes 884744 | tf_op jit(solution)/shard_map/ppermute | solution.py:144
  (22 other events, 147.2 us)

commit v2 on v1

--- a/solution.py
+++ b/solution.py
@@ -126,7 +126,7 @@
         kernel,
         out_shape=out_shape,
         scratch_shapes=list(scratch),
-        compiler_params=pltpu.CompilerParams(vmem_limit_bytes=56 * 2**20),
+        compiler_params=pltpu.CompilerParams(vmem_limit_bytes=16 * 2**20),
         cost_estimate=pl.CostEstimate(flops=flops, bytes_accessed=moved, transcendentals=0),
     )(*args)
 

time: 84.2 us -> 68.8 us (0.82)
  Pallas kernels: 30.2 us -> 10 us
  local copies, waits for them, and re-layouts: 1.43 us -> 8.8 us
  other arithmetic: 3.89 us -> 0.44 us
    pallas_call x5, Pallas kernels: 30.2 us -> 10 us  [call(): pl.pallas_call(kernel, out_shape=out_shape, scratch_shapes=list(scratch),...]
    unnamed x42 -> x16, local copies, waits for them, and re-layouts: 1.43 us -> 8.8 us
    another operation x2, other arithmetic: 1.55 us -> 0.06 us
    add x1, other arithmetic: 1.03 us -> 0.03 us  [body(): chip_second = own[PAIR:] + theirs[:PAIR]]
    convert_element_type x3, other arithmetic: 1.1 us -> 0.12 us  [body(): second = onward(sum_second.astype(BF16)).astype(F32)]
    ppermute x12, waiting for transfers between devices: 11.9 us -> 12.9 us  [onward(): return lax.ppermute(a, 'tensor', ring_one)]
  transfers between devices with their start and end apart: 25 -> 25, of which waited for: 12 -> 13; matrix products, arithmetic and copies ran while one was open for 2% -> 1% of each run, Pallas kernels for 7% -> 2%
where the time goes in v2:
time: 68.8 us; the launch traced here: 68.6 us
  starting transfers between devices  27.2 us (40%)
  waiting for transfers between devices  22 us (32%)
  Pallas kernels  10 us (15%)
  local copies, waits for them, and re-layouts  8.8 us (13%)
    ppermute x12, starting transfers between devices, onward(): return lax.ppermute(a, 'tensor', ring_one)  19.4 us
    ppermute x12, waiting for transfers between devices, onward(): return lax.ppermute(a, 'tensor', ring_one)  12.9 us
    pallas_call x5, Pallas kernels, call(): pl.pallas_call(kernel, out_shape=out_shape, scratch_shapes=list(scratch),...  10 us
    unnamed x16, local copies, waits for them, and re-layouts  8.8 us
    ppermute x2, starting transfers between devices, two_on(): return lax.ppermute(a, 'tensor', ring_two)  5.54 us
    ppermute x2, waiting for transfers between devices, two_on(): return lax.ppermute(a, 'tensor', ring_two)  4.79 us
    ppermute x11, waiting for transfers between devices, swap(): return lax.ppermute(a, 'tensor', pair_core)  4.26 us
    ppermute x11, starting transfers between devices, swap(): return lax.ppermute(a, 'tensor', pair_core)  2.26 us
  transfers between devices with their start and end apart: 25, of which 13 were waited for; matrix products, arithmetic and copies ran while one was open for 1% of the time, Pallas kernels for 2%

profile of v2, /device:TPU:0, one launch (start us, length us, event | category | flops | bytes accessed | tf_op | source)
XLA Modules:
  0.0 68.6 jit_solution(75830826653372786)
XLA Ops:
  0.0 1.4 %copy-done.2 = bf16[128,6144]{1,0:T(8,128)(2,1)S(1)} copy-done((bf16[128,6144]{1,0:T(8,128)(2,1)S(1)}, bf16[128,6144]{1,0:T(8,128)(2,1)}, u32[]{:S(2)}) %copy-start.2) | copy-done | bytes 1572888
  4.3 3.0 %collective-permute-start.1 = (bf16[24,3072]{1,0:T(8,128)(2,1)S(1)}, bf16[24,3072]{1,0:T(8,128)(2,1)S(1)}, u32[]{:S(2)}, u32[]{:S(2)}) collective-permute-start(bf16[24,3072]{1,0:T(8,128)(2,1)S(1)} %get-tuple-element.20.refs_7_), channel_id=1, source_target_pairs={{0,4},{1,3},{4,8},{5,1},{8,12},{9,5},{12,14},{13,9},{14,10},{15,13... | collective-permute-start | bytes 442376 | tf_op jit(solution)/shard_map/ppermute | solution.py:147
  7.3 1.6 %collective-permute-start.5 = (bf16[24,3072]{1,0:T(8,128)(2,1)S(1)}, bf16[24,3072]{1,0:T(8,128)(2,1)S(1)}, u32[]{:S(2)}, u32[]{:S(2)}) collective-permute-start(bf16[24,3072]{1,0:T(8,128)(2,1)S(1)} %get-tuple-element.19.refs_15_), channel_id=1, source_target_pairs={{0,4},{1,3},{4,8},{5,1},{8,12},{9,5},{12,14},{13,9},{14,10},{15,13... | collective-permute-start | bytes 442376 | tf_op jit(solution)/shard_map/ppermute | solution.py:147
  8.9 1.5 %collective-permute-done.1.refs_0_ = bf16[24,3072]{1,0:T(8,128)(2,1)S(1)} collective-permute-done((bf16[24,3072]{1,0:T(8,128)(2,1)S(1)}, bf16[24,3072]{1,0:T(8,128)(2,1)S(1)}, u32[]{:S(2)}, u32[]{:S(2)}) %collective-permute-start.1) | collective-permute-done | bytes 147488 | tf_op jit(solution)/shard_map/ppermute | solution.py:147
  10.4 2.1 %collective-permute-start.2 = (bf16[24,3072]{1,0:T(8,128)(2,1)S(1)}, bf16[24,3072]{1,0:T(8,128)(2,1)S(1)}, u32[]{:S(2)}, u32[]{:S(2)}) collective-permute-start(bf16[24,3072]{1,0:T(8,128)(2,1)S(1)} %collective-permute-done.1.refs_0_), channel_id=1, source_target_pairs={{0,4},{1,3},{4,8},{5,1},{8,12},{9,5},{12,14},{13,9},{14,10},{15,13... | collective-permute-start | bytes 442376 | tf_op jit(solution)/shard_map/ppermute | solution.py:147
  12.5 1.6 %collective-permute-start.7 = (bf16[24,3072]{1,0:T(8,128)(2,1)S(1)}, bf16[24,3072]{1,0:T(8,128)(2,1)S(1)}, u32[]{:S(2)}, u32[]{:S(2)}) collective-permute-start(bf16[24,3072]{1,0:T(8,128)(2,1)S(1)} %collective-permute-done.5.refs_8_), channel_id=1, source_target_pairs={{0,4},{1,3},{4,8},{5,1},{8,12},{9,5},{12,14},{13,9},{14,10},{15,13... | collective-permute-start | bytes 442376 | tf_op jit(solution)/shard_map/ppermute | solution.py:147
  15.5 3.1 %collective-permute-start.4 = (bf16[24,3072]{1,0:T(8,128)(2,1)S(1)}, bf16[24,3072]{1,0:T(8,128)(2,1)S(1)}, u32[]{:S(2)}, u32[]{:S(2)}) collective-permute-start(bf16[24,3072]{1,0:T(8,128)(2,1)S(1)} %collective-permute-done.2.refs_1_), channel_id=1, source_target_pairs={{0,8},{1,7},{4,12},{5,3},{8,14},{9,1},{12,10},{13,5},{14,6},{15,9}... | collective-permute-start | bytes 442376 | tf_op jit(solution)/shard_map/ppermute | solution.py:150
  18.6 1.6 %collective-permute-start.3 = (bf16[24,3072]{1,0:T(8,128)(2,1)S(1)}, bf16[24,3072]{1,0:T(8,128)(2,1)S(1)}, u32[]{:S(2)}, u32[]{:S(2)}) collective-permute-start(bf16[24,3072]{1,0:T(8,128)(2,1)S(1)} %collective-permute-done.2.refs_1_), channel_id=1, source_target_pairs={{0,4},{1,3},{4,8},{5,1},{8,12},{9,5},{12,14},{13,9},{14,10},{15,13... | collective-permute-start | bytes 442376 | tf_op jit(solution)/shard_map/ppermute | solution.py:147
  20.2 1.5 %collective-permute-start.9 = (bf16[24,3072]{1,0:T(8,128)(2,1)S(1)}, bf16[24,3072]{1,0:T(8,128)(2,1)S(1)}, u32[]{:S(2)}, u32[]{:S(2)}) collective-permute-start(bf16[24,3072]{1,0:T(8,128)(2,1)S(1)} %collective-permute-done.7.refs_9_), channel_id=1, source_target_pairs={{0,4},{1,3},{4,8},{5,1},{8,12},{9,5},{12,14},{13,9},{14,10},{15,13... | collective-permute-start | bytes 442376 | tf_op jit(solution)/shard_map/ppermute | solution.py:147
  23.9 1.6 %collective-permute-done.9.refs_10_ = bf16[24,3072]{1,0:T(8,128)(2,1)S(1)} collective-permute-done((bf16[24,3072]{1,0:T(8,128)(2,1)S(1)}, bf16[24,3072]{1,0:T(8,128)(2,1)S(1)}, u32[]{:S(2)}, u32[]{:S(2)}) %collective-permute-start.9) | collective-permute-done | bytes 147488 | tf_op jit(solution)/shard_map/ppermute | solution.py:147
  25.5 1.3 %collective-permute-done.10.refs_6_ = bf16[24,3072]{1,0:T(8,128)(2,1)S(1)} collective-permute-done((bf16[24,3072]{1,0:T(8,128)(2,1)S(1)}, bf16[24,3072]{1,0:T(8,128)(2,1)S(1)}, u32[]{:S(2)}, u32[]{:S(2)}) %collective-permute-start.10) | collective-permute-done | bytes 147488 | tf_op jit(solution)/shard_map/ppermute | solution.py:144
  26.8 3.3 %copy-done = bf16[672,6144]{1,0:T(8,128)(2,1)S(1)} copy-done((bf16[672,6144]{1,0:T(8,128)(2,1)S(1)}, bf16[672,6144]{1,0:T(8,128)(2,1)}, u32[]{:S(2)}) %copy-start) | copy-done | bytes 8257560
  30.2 3.3 %copy-done.1 = bf16[672,6144]{1,0:T(8,128)(2,1)S(1)} copy-done((bf16[672,6144]{1,0:T(8,128)(2,1)S(1)}, bf16[672,6144]{1,0:T(8,128)(2,1)}, u32[]{:S(2)}) %copy-start.1) | copy-done | bytes 8257560
  33.5 5.5 %shard_map.65.refs_0_ = bf16[192,672]{1,0:T(8,128)(2,1)S(1)} custom-call(bf16[24,3072]{1,0:T(8,128)(2,1)S(1)} %collective-permute-done.1.refs_0_, bf16[24,3072]{1,0:T(8,128)(2,1)S(1)} %collective-permute-done.2.refs_1_, bf16[24,3072]{1,0:T(8,128)(2,1)S(1)} %collective-permute-done.3.refs_2_, bf16[24,3072]{1,0:T(8,128)(2,1)S(1)} %collective-permute-done.4.refs_3_, ...), custom_call_target="tpu_custom_call" | custom-call | flops 3170893824 | bytes 18874368 | tf_op jit(solution)/shard_map/pallas_call | solution.py:125
  42.1 2.1 %collective-permute-start.21 = (bf16[24,3072]{1,0:T(8,128)(2,1)S(1)}, bf16[24,3072]{1,0:T(8,128)(2,1)S(1)}, u32[]{:S(2)}, u32[]{:S(2)}) collective-permute-start(bf16[24,3072]{1,0:T(8,128)(2,1)S(1)} %add_convert_fusion.4), channel_id=1, source_target_pairs={{0,4},{1,3},{4,8},{5,1},{8,12},{9,5},{12,14},{13,9},{14,10},{15,13... | collective-permute-start | bytes 442376 | tf_op jit(solution)/shard_map/ppermute | solution.py:147
  44.2 2.5 %collective-permute-start.16 = (bf16[24,3072]{1,0:T(8,128)(2,1)S(1)}, bf16[24,3072]{1,0:T(8,128)(2,1)S(1)}, u32[]{:S(2)}, u32[]{:S(2)}) collective-permute-start(bf16[24,3072]{1,0:T(8,128)(2,1)S(1)} %get-tuple-element.13), channel_id=1, source_target_pairs={{0,4},{1,3},{4,8},{5,1},{8,12},{9,5},{12,14},{13,9},{14,10},{15,13... | collective-permute-start | bytes 442376 | tf_op jit(solution)/shard_map/ppermute | solution.py:147
  46.8 2.4 %collective-permute-start.17 = (bf16[24,3072]{1,0:T(8,128)(2,1)S(1)}, bf16[24,3072]{1,0:T(8,128)(2,1)S(1)}, u32[]{:S(2)}, u32[]{:S(2)}) collective-permute-start(bf16[24,3072]{1,0:T(8,128)(2,1)S(1)} %get-tuple-element.14), channel_id=1, source_target_pairs={{0,8},{1,7},{4,12},{5,3},{8,14},{9,1},{12,10},{13,5},{14,6},{15,9}... | collective-permute-start | bytes 442376 | tf_op jit(solution)/shard_map/ppermute | solution.py:150
  50.3 4.2 %collective-permute-done.17 = bf16[24,3072]{1,0:T(8,128)(2,1)S(1)} collective-permute-done((bf16[24,3072]{1,0:T(8,128)(2,1)S(1)}, bf16[24,3072]{1,0:T(8,128)(2,1)S(1)}, u32[]{:S(2)}, u32[]{:S(2)}) %collective-permute-start.17) | collective-permute-done | bytes 147488 | tf_op jit(solution)/shard_map/ppermute | solution.py:150
  54.5 1.6 %collective-permute-start.18 = (bf16[24,3072]{1,0:T(8,128)(2,1)S(1)}, bf16[24,3072]{1,0:T(8,128)(2,1)S(1)}, u32[]{:S(2)}, u32[]{:S(2)}) collective-permute-start(bf16[24,3072]{1,0:T(8,128)(2,1)S(1)} %add_convert_fusion.6), channel_id=1, source_target_pairs={{0,4},{1,3},{4,8},{5,1},{8,12},{9,5},{12,14},{13,9},{14,10},{15,13... | collective-permute-start | bytes 442376 | tf_op jit(solution)/shard_map/ppermute | solution.py:147
  56.3 3.4 %collective-permute-done.18 = bf16[24,3072]{1,0:T(8,128)(2,1)S(1)} collective-permute-done((bf16[24,3072]{1,0:T(8,128)(2,1)S(1)}, bf16[24,3072]{1,0:T(8,128)(2,1)S(1)}, u32[]{:S(2)}, u32[]{:S(2)}) %collective-permute-start.18) | collective-permute-done | bytes 147488 | tf_op jit(solution)/shard_map/ppermute | solution.py:147
  59.8 1.6 %collective-permute-start.19 = (bf16[24,3072]{1,0:T(8,128)(2,1)S(1)}, bf16[24,3072]{1,0:T(8,128)(2,1)S(1)}, u32[]{:S(2)}, u32[]{:S(2)}) collective-permute-start(bf16[24,3072]{1,0:T(8,128)(2,1)S(1)} %add_convert_fusion.5), channel_id=1, source_target_pairs={{0,4},{1,3},{4,8},{5,1},{8,12},{9,5},{12,14},{13,9},{14,10},{15,13... | collective-permute-start | bytes 442376 | tf_op jit(solution)/shard_map/ppermute | solution.py:147
  61.4 3.5 %collective-permute-done.19.first_ref = bf16[24,3072]{1,0:T(8,128)(2,1)S(1)} collective-permute-done((bf16[24,3072]{1,0:T(8,128)(2,1)S(1)}, bf16[24,3072]{1,0:T(8,128)(2,1)S(1)}, u32[]{:S(2)}, u32[]{:S(2)}) %collective-permute-start.19) | collective-permute-done | bytes 147488 | tf_op jit(solution)/shard_map/ppermute | solution.py:147
  65.1 1.6 %collective-permute-done.24.sibling_ref = bf16[48,3072]{1,0:T(8,128)(2,1)S(1)} collective-permute-done((bf16[48,3072]{1,0:T(8,128)(2,1)S(1)}, bf16[48,3072]{1,0:T(8,128)(2,1)S(1)}, u32[]{:S(2)}, u32[]{:S(2)}) %collective-permute-start.24) | collective-permute-done | bytes 294944 | tf_op jit(solution)/shard_map/ppermute | solution.py:144
  66.7 1.9 %shard_map.68 = bf16[128,6144]{1,0:T(8,128)(2,1)} custom-call(s32[4,128]{1,0:T(4,128)S(1)} %bitcast.5, f32[4,128]{1,0:T(4,128)S(1)} %bitcast.6, bf16[24,3072]{1,0:T(8,128)(2,1)S(1)} %collective-permute-done.19.first_ref, bf16[24,3072]{1,0:T(8,128)(2,1)S(1)} %collective-permute-done.23.second_ref, f32[24,3072]{1,0:T(8,128)S(1)} %get-tuple-element.16.own_first, ...), custom_call_target="tpu_custom_call" | custom-call | bytes 1183744 | tf_op jit(solution)/shard_map/pallas_call | solution.py:125
  (58 shorter events, 11.1 us)
Async XLA Ops:
  2.6 1.7 %collective-permute-start = (bf16[48,3072]{1,0:T(8,128)(2,1)S(1)}, bf16[48,3072]{1,0:T(8,128)(2,1)S(1)}, u32[]{:S(2)}, u32[]{:S(2)}) collective-permute-start(bf16[48,3072]{1,0:T(8,128)(2,1)S(1)} %shard_map.64), channel_id=1, source_target_pairs={{0,1},{1,0},{2,3},{3,2},{4,5},{5,4},{6,7},{7,6},{8,9},{9,8},{10,11... | collective-permute-start | bytes 884744 | tf_op jit(solution)/shard_map/ppermute | solution.py:144
  4.3 6.1 %collective-permute-start.1 = (bf16[24,3072]{1,0:T(8,128)(2,1)S(1)}, bf16[24,3072]{1,0:T(8,128)(2,1)S(1)}, u32[]{:S(2)}, u32[]{:S(2)}) collective-permute-start(bf16[24,3072]{1,0:T(8,128)(2,1)S(1)} %get-tuple-element.20.refs_7_), channel_id=1, source_target_pairs={{0,4},{1,3},{4,8},{5,1},{8,12},{9,5},{12,14},{13,9},{14,10},{15,13... | collective-permute-start | bytes 442376 | tf_op jit(solution)/shard_map/ppermute | solution.py:147
  7.3 5.1 %collective-permute-start.5 = (bf16[24,3072]{1,0:T(8,128)(2,1)S(1)}, bf16[24,3072]{1,0:T(8,128)(2,1)S(1)}, u32[]{:S(2)}, u32[]{:S(2)}) collective-permute-start(bf16[24,3072]{1,0:T(8,128)(2,1)S(1)} %get-tuple-element.19.refs_15_), channel_id=1, source_target_pairs={{0,4},{1,3},{4,8},{5,1},{8,12},{9,5},{12,14},{13,9},{14,10},{15,13... | collective-permute-start | bytes 442376 | tf_op jit(solution)/shard_map/ppermute | solution.py:147
  10.4 5.1 %collective-permute-start.2 = (bf16[24,3072]{1,0:T(8,128)(2,1)S(1)}, bf16[24,3072]{1,0:T(8,128)(2,1)S(1)}, u32[]{:S(2)}, u32[]{:S(2)}) collective-permute-start(bf16[24,3072]{1,0:T(8,128)(2,1)S(1)} %collective-permute-done.1.refs_0_), channel_id=1, source_target_pairs={{0,4},{1,3},{4,8},{5,1},{8,12},{9,5},{12,14},{13,9},{14,10},{15,13... | collective-permute-start | bytes 442376 | tf_op jit(solution)/shard_map/ppermute | solution.py:147
  12.5 7.7 %collective-permute-start.7 = (bf16[24,3072]{1,0:T(8,128)(2,1)S(1)}, bf16[24,3072]{1,0:T(8,128)(2,1)S(1)}, u32[]{:S(2)}, u32[]{:S(2)}) collective-permute-start(bf16[24,3072]{1,0:T(8,128)(2,1)S(1)} %collective-permute-done.5.refs_8_), channel_id=1, source_target_pairs={{0,4},{1,3},{4,8},{5,1},{8,12},{9,5},{12,14},{13,9},{14,10},{15,13... | collective-permute-start | bytes 442376 | tf_op jit(solution)/shard_map/ppermute | solution.py:147
  14.0 7.7 %collective-permute-start.12 = (bf16[24,3072]{1,0:T(8,128)(2,1)S(1)}, bf16[24,3072]{1,0:T(8,128)(2,1)S(1)}, u32[]{:S(2)}, u32[]{:S(2)}) collective-permute-start(bf16[24,3072]{1,0:T(8,128)(2,1)S(1)} %collective-permute-done.1.refs_0_), channel_id=1, source_target_pairs={{0,1},{1,0},{2,3},{3,2},{4,5},{5,4},{6,7},{7,6},{8,9},{9,8},{10,11... | collective-permute-start | bytes 442376 | tf_op jit(solution)/shard_map/ppermute | solution.py:144
  14.0 7.7 %collective-permute-start.6 = (bf16[24,3072]{1,0:T(8,128)(2,1)S(1)}, bf16[24,3072]{1,0:T(8,128)(2,1)S(1)}, u32[]{:S(2)}, u32[]{:S(2)}) collective-permute-start(bf16[24,3072]{1,0:T(8,128)(2,1)S(1)} %collective-permute-done.5.refs_8_), channel_id=1, source_target_pairs={{0,1},{1,0},{2,3},{3,2},{4,5},{5,4},{6,7},{7,6},{8,9},{9,8},{10,11... | collective-permute-start | bytes 442376 | tf_op jit(solution)/shard_map/ppermute | solution.py:144
  15.5 7.3 %collective-permute-start.4 = (bf16[24,3072]{1,0:T(8,128)(2,1)S(1)}, bf16[24,3072]{1,0:T(8,128)(2,1)S(1)}, u32[]{:S(2)}, u32[]{:S(2)}) collective-permute-start(bf16[24,3072]{1,0:T(8,128)(2,1)S(1)} %collective-permute-done.2.refs_1_), channel_id=1, source_target_pairs={{0,8},{1,7},{4,12},{5,3},{8,14},{9,1},{12,10},{13,5},{14,6},{15,9}... | collective-permute-start | bytes 442376 | tf_op jit(solution)/shard_map/ppermute | solution.py:150
  18.6 5.3 %collective-permute-start.3 = (bf16[24,3072]{1,0:T(8,128)(2,1)S(1)}, bf16[24,3072]{1,0:T(8,128)(2,1)S(1)}, u32[]{:S(2)}, u32[]{:S(2)}) collective-permute-start(bf16[24,3072]{1,0:T(8,128)(2,1)S(1)} %collective-permute-done.2.refs_1_), channel_id=1, source_target_pairs={{0,4},{1,3},{4,8},{5,1},{8,12},{9,5},{12,14},{13,9},{14,10},{15,13... | collective-permute-start | bytes 442376 | tf_op jit(solution)/shard_map/ppermute | solution.py:147
  20.2 5.3 %collective-permute-start.9 = (bf16[24,3072]{1,0:T(8,128)(2,1)S(1)}, bf16[24,3072]{1,0:T(8,128)(2,1)S(1)}, u32[]{:S(2)}, u32[]{:S(2)}) collective-permute-start(bf16[24,3072]{1,0:T(8,128)(2,1)S(1)} %collective-permute-done.7.refs_9_), channel_id=1, source_target_pairs={{0,4},{1,3},{4,8},{5,1},{8,12},{9,5},{12,14},{13,9},{14,10},{15,13... | collective-permute-start | bytes 442376 | tf_op jit(solution)/shard_map/ppermute | solution.py:147
  21.7 3.8 %collective-permute-start.13 = (bf16[24,3072]{1,0:T(8,128)(2,1)S(1)}, bf16[24,3072]{1,0:T(8,128)(2,1)S(1)}, u32[]{:S(2)}, u32[]{:S(2)}) collective-permute-start(bf16[24,3072]{1,0:T(8,128)(2,1)S(1)} %collective-permute-done.2.refs_1_), channel_id=1, source_target_pairs={{0,1},{1,0},{2,3},{3,2},{4,5},{5,4},{6,7},{7,6},{8,9},{9,8},{10,11... | collective-permute-start | bytes 442376 | tf_op jit(solution)/shard_map/ppermute | solution.py:144
  21.7 3.8 %collective-permute-start.8 = (bf16[24,3072]{1,0:T(8,128)(2,1)S(1)}, bf16[24,3072]{1,0:T(8,128)(2,1)S(1)}, u32[]{:S(2)}, u32[]{:S(2)}) collective-permute-start(bf16[24,3072]{1,0:T(8,128)(2,1)S(1)} %collective-permute-done.7.refs_9_), channel_id=1, source_target_pairs={{0,1},{1,0},{2,3},{3,2},{4,5},{5,4},{6,7},{7,6},{8,9},{9,8},{10,11... | collective-permute-start | bytes 442376 | tf_op jit(solution)/shard_map/ppermute | solution.py:144
  22.8 2.6 %collective-permute-start.11 = (bf16[24,3072]{1,0:T(8,128)(2,1)S(1)}, bf16[24,3072]{1,0:T(8,128)(2,1)S(1)}, u32[]{:S(2)}, u32[]{:S(2)}) collective-permute-start(bf16[24,3072]{1,0:T(8,128)(2,1)S(1)} %collective-permute-done.4.refs_3_), channel_id=1, source_target_pairs={{0,1},{1,0},{2,3},{3,2},{4,5},{5,4},{6,7},{7,6},{8,9},{9,8},{10,11... | collective-permute-start | bytes 442376 | tf_op jit(solution)/shard_map/ppermute | solution.py:144
  23.9 1.6 %collective-permute-start.14 = (bf16[24,3072]{1,0:T(8,128)(2,1)S(1)}, bf16[24,3072]{1,0:T(8,128)(2,1)S(1)}, u32[]{:S(2)}, u32[]{:S(2)}) collective-permute-start(bf16[24,3072]{1,0:T(8,128)(2,1)S(1)} %collective-permute-done.3.refs_2_), channel_id=1, source_target_pairs={{0,1},{1,0},{2,3},{3,2},{4,5},{5,4},{6,7},{7,6},{8,9},{9,8},{10,11... | collective-permute-start | bytes 442376 | tf_op jit(solution)/shard_map/ppermute | solution.py:144
  40.2 1.9 %collective-permute-start.20 = (bf16[72,3072]{1,0:T(8,128)(2,1)S(1)}, bf16[72,3072]{1,0:T(8,128)(2,1)S(1)}, u32[]{:S(2)}, u32[]{:S(2)}) collective-permute-start(bf16[72,3072]{1,0:T(8,128)(2,1)S(1)} %get-tuple-element.12), channel_id=1, source_target_pairs={{0,1},{1,0},{2,3},{3,2},{4,5},{5,4},{6,7},{7,6},{8,9},{9,8},{10,11... | collective-permute-start | bytes 1327112 | tf_op jit(solution)/shard_map/ppermute | solution.py:144
  41.5 2.7 %collective-permute-start.15 = (bf16[96,3072]{1,0:T(8,128)(2,1)S(1)}, bf16[96,3072]{1,0:T(8,128)(2,1)S(1)}, u32[]{:S(2)}, u32[]{:S(2)}) collective-permute-start(bf16[96,3072]{1,0:T(8,128)(2,1)S(1)} %get-tuple-element.10), channel_id=1, source_target_pairs={{0,1},{1,0},{2,3},{3,2},{4,5},{5,4},{6,7},{7,6},{8,9},{9,8},{10,11... | collective-permute-start | bytes 1769480 | tf_op jit(solution)/shard_map/ppermute | solution.py:144
  42.1 7.2 %collective-permute-start.21 = (bf16[24,3072]{1,0:T(8,128)(2,1)S(1)}, bf16[24,3072]{1,0:T(8,128)(2,1)S(1)}, u32[]{:S(2)}, u32[]{:S(2)}) collective-permute-start(bf16[24,3072]{1,0:T(8,128)(2,1)S(1)} %add_convert_fusion.4), channel_id=1, source_target_pairs={{0,4},{1,3},{4,8},{5,1},{8,12},{9,5},{12,14},{13,9},{14,10},{15,13... | collective-permute-start | bytes 442376 | tf_op jit(solution)/shard_map/ppermute | solution.py:147
  44.2 6.0 %collective-permute-start.16 = (bf16[24,3072]{1,0:T(8,128)(2,1)S(1)}, bf16[24,3072]{1,0:T(8,128)(2,1)S(1)}, u32[]{:S(2)}, u32[]{:S(2)}) collective-permute-start(bf16[24,3072]{1,0:T(8,128)(2,1)S(1)} %get-tuple-element.13), channel_id=1, source_target_pairs={{0,4},{1,3},{4,8},{5,1},{8,12},{9,5},{12,14},{13,9},{14,10},{15,13... | collective-permute-start | bytes 442376 | tf_op jit(solution)/shard_map/ppermute | solution.py:147
  46.8 7.7 %collective-permute-start.17 = (bf16[24,3072]{1,0:T(8,128)(2,1)S(1)}, bf16[24,3072]{1,0:T(8,128)(2,1)S(1)}, u32[]{:S(2)}, u32[]{:S(2)}) collective-permute-start(bf16[24,3072]{1,0:T(8,128)(2,1)S(1)} %get-tuple-element.14), channel_id=1, source_target_pairs={{0,8},{1,7},{4,12},{5,3},{8,14},{9,1},{12,10},{13,5},{14,6},{15,9}... | collective-permute-start | bytes 442376 | tf_op jit(solution)/shard_map/ppermute | solution.py:150
  49.3 6.9 %collective-permute-start.22 = (bf16[24,3072]{1,0:T(8,128)(2,1)S(1)}, bf16[24,3072]{1,0:T(8,128)(2,1)S(1)}, u32[]{:S(2)}, u32[]{:S(2)}) collective-permute-start(bf16[24,3072]{1,0:T(8,128)(2,1)S(1)} %add_convert_fusion.3), channel_id=1, source_target_pairs={{0,4},{1,3},{4,8},{5,1},{8,12},{9,5},{12,14},{13,9},{14,10},{15,13... | collective-permute-start | bytes 442376 | tf_op jit(solution)/shard_map/ppermute | solution.py:147
  54.5 5.2 %collective-permute-start.18 = (bf16[24,3072]{1,0:T(8,128)(2,1)S(1)}, bf16[24,3072]{1,0:T(8,128)(2,1)S(1)}, u32[]{:S(2)}, u32[]{:S(2)}) collective-permute-start(bf16[24,3072]{1,0:T(8,128)(2,1)S(1)} %add_convert_fusion.6), channel_id=1, source_target_pairs={{0,4},{1,3},{4,8},{5,1},{8,12},{9,5},{12,14},{13,9},{14,10},{15,13... | collective-permute-start | bytes 442376 | tf_op jit(solution)/shard_map/ppermute | solution.py:147
  56.2 5.2 %collective-permute-start.23 = (bf16[24,3072]{1,0:T(8,128)(2,1)S(1)}, bf16[24,3072]{1,0:T(8,128)(2,1)S(1)}, u32[]{:S(2)}, u32[]{:S(2)}) collective-permute-start(bf16[24,3072]{1,0:T(8,128)(2,1)S(1)} %add_convert_fusion.2), channel_id=1, source_target_pairs={{0,4},{1,3},{4,8},{5,1},{8,12},{9,5},{12,14},{13,9},{14,10},{15,13... | collective-permute-start | bytes 442376 | tf_op jit(solution)/shard_map/ppermute | solution.py:147
  59.8 5.2 %collective-permute-start.19 = (bf16[24,3072]{1,0:T(8,128)(2,1)S(1)}, bf16[24,3072]{1,0:T(8,128)(2,1)S(1)}, u32[]{:S(2)}, u32[]{:S(2)}) collective-permute-start(bf16[24,3072]{1,0:T(8,128)(2,1)S(1)} %add_convert_fusion.5), channel_id=1, source_target_pairs={{0,4},{1,3},{4,8},{5,1},{8,12},{9,5},{12,14},{13,9},{14,10},{15,13... | collective-permute-start | bytes 442376 | tf_op jit(solution)/shard_map/ppermute | solution.py:147
  65.0 1.6 %collective-permute-start.24 = (bf16[48,3072]{1,0:T(8,128)(2,1)S(1)}, bf16[48,3072]{1,0:T(8,128)(2,1)S(1)}, u32[]{:S(2)}, u32[]{:S(2)}) collective-permute-start(bf16[48,3072]{1,0:T(8,128)(2,1)S(1)} %pad_maximum_fusion), channel_id=1, source_target_pairs={{0,1},{1,0},{2,3},{3,2},{4,5},{5,4},{6,7},{7,6},{8,9},{9,8},{10,11... | collective-permute-start | bytes 884744 | tf_op jit(solution)/shard_map/ppermute | solution.py:144
  (9 other events, 97.6 us)

commit v3 on v2

--- a/solution.py
+++ b/solution.py
@@ -54,6 +54,11 @@
         out_ref[place * PAIR : (place + 1) * PAIR, :] = jnp.dot(
             chooser, tokens_ref[:, pl.ds(start, width // 2)], preferred_element_type=F32
         ).astype(BF16)
+
+
+def join_kernel(own_ref, theirs_ref, first_ref, second_ref):
+    first_ref[...] = own_ref[:PAIR, :] + theirs_ref[PAIR:, :]
+    second_ref[...] = own_ref[PAIR:, :] + theirs_ref[:PAIR, :]
 
 
 def hidden_kernel(blocks, *refs):
@@ -120,8 +125,8 @@
         out_ref[:, pl.ds(start, width // 2)] = (share * picked).astype(BF16)
 
 
-def call(kernel, out_shape, *args, scratch=(), flops=0):
-    moved = sum(a.size * a.dtype.itemsize for a in args)
+def call(kernel, out_shape, *args, scratch=(), flops=0, extra=0):
+    moved = extra + sum(a.size * a.dtype.itemsize for a in args)
     return pl.pallas_call(
         kernel,
         out_shape=out_shape,
@@ -153,8 +158,9 @@
     ids = expert_ids.T
     own = call(compact_kernel, struct((2 * PAIR, half), BF16), ids, tokens)
     theirs = swap(own)
-    chip_first = own[:PAIR] + theirs[PAIR:]
-    chip_second = own[PAIR:] + theirs[:PAIR]
+    chip_first, chip_second = call(
+        join_kernel, (struct((PAIR, half), BF16),) * 2, own, theirs, flops=40 * rows * units * width
+    )
 
     behind = [(chip_first, chip_second)]
     ahead = [None]

time: 68.8 us -> 62.1 us (0.903)
  local copies, waits for them, and re-layouts: 8.8 us -> 2.14 us
    unnamed x16 -> x20, local copies, waits for them, and re-layouts: 8.8 us -> 2.14 us
    pallas_call x5 -> x6, Pallas kernels: 10 us -> 10.1 us  [call(): pl.pallas_call(kernel, out_shape=out_shape, scratch_shapes=list(scratch),...]
where the time goes in v3:
time: 62.1 us; the launch traced here: 62 us
  starting transfers between devices  27.2 us (44%)
  waiting for transfers between devices  22 us (35%)
  Pallas kernels  10.1 us (16%)
  local copies, waits for them, and re-layouts  2.14 us (3%)
    ppermute x12, starting transfers between devices, onward(): return lax.ppermute(a, 'tensor', ring_one)  19.4 us
    ppermute x12, waiting for transfers between devices, onward(): return lax.ppermute(a, 'tensor', ring_one)  12.9 us
    pallas_call x6, Pallas kernels, call(): pl.pallas_call(kernel, out_shape=out_shape, scratch_shapes=list(scratch),...  10.1 us
    ppermute x2, starting transfers between devices, two_on(): return lax.ppermute(a, 'tensor', ring_two)  5.54 us
    ppermute x2, waiting for transfers between devices, two_on(): return lax.ppermute(a, 'tensor', ring_two)  4.79 us
    ppermute x11, waiting for transfers between devices, swap(): return lax.ppermute(a, 'tensor', pair_core)  4.26 us
    ppermute x11, starting transfers between devices, swap(): return lax.ppermute(a, 'tensor', pair_core)  2.26 us
    unnamed x20, local copies, waits for them, and re-layouts  2.14 us
  transfers between devices with their start and end apart: 25, of which 13 were waited for; matrix products, arithmetic and copies ran while one was open for 1% of the time, Pallas kernels for 2%

profile of v3, /device:TPU:0, one launch (start us, length us, event | category | flops | bytes accessed | tf_op | source)
XLA Modules:
  0.0 62.0 jit_solution(6307807209012006889)
XLA Ops:
  0.0 1.4 %copy-done = bf16[128,6144]{1,0:T(8,128)(2,1)S(1)} copy-done((bf16[128,6144]{1,0:T(8,128)(2,1)S(1)}, bf16[128,6144]{1,0:T(8,128)(2,1)}, u32[]{:S(2)}) %copy-start) | copy-done | bytes 1572888
  3.1 1.2 %collective-permute-done.theirs_ref = bf16[48,3072]{1,0:T(8,128)(2,1)S(1)} collective-permute-done((bf16[48,3072]{1,0:T(8,128)(2,1)S(1)}, bf16[48,3072]{1,0:T(8,128)(2,1)S(1)}, u32[]{:S(2)}, u32[]{:S(2)}) %collective-permute-start) | collective-permute-done | bytes 294944 | tf_op jit(solution)/shard_map/ppermute | solution.py:149
  4.4 3.0 %collective-permute-start.1 = (bf16[24,3072]{1,0:T(8,128)(2,1)S(1)}, bf16[24,3072]{1,0:T(8,128)(2,1)S(1)}, u32[]{:S(2)}, u32[]{:S(2)}) collective-permute-start(bf16[24,3072]{1,0:T(8,128)(2,1)S(1)} %get-tuple-element.11.refs_7_), channel_id=1, source_target_pairs={{0,4},{1,3},{4,8},{5,1},{8,12},{9,5},{12,14},{13,9},{14,10},{15,13... | collective-permute-start | bytes 442376 | tf_op jit(solution)/shard_map/ppermute | solution.py:152
  7.4 1.6 %collective-permute-start.5 = (bf16[24,3072]{1,0:T(8,128)(2,1)S(1)}, bf16[24,3072]{1,0:T(8,128)(2,1)S(1)}, u32[]{:S(2)}, u32[]{:S(2)}) collective-permute-start(bf16[24,3072]{1,0:T(8,128)(2,1)S(1)} %get-tuple-element.12.refs_15_), channel_id=1, source_target_pairs={{0,4},{1,3},{4,8},{5,1},{8,12},{9,5},{12,14},{13,9},{14,10},{15,13... | collective-permute-start | bytes 442376 | tf_op jit(solution)/shard_map/ppermute | solution.py:152
  8.9 1.5 %collective-permute-done.1.refs_0_ = bf16[24,3072]{1,0:T(8,128)(2,1)S(1)} collective-permute-done((bf16[24,3072]{1,0:T(8,128)(2,1)S(1)}, bf16[24,3072]{1,0:T(8,128)(2,1)S(1)}, u32[]{:S(2)}, u32[]{:S(2)}) %collective-permute-start.1) | collective-permute-done | bytes 147488 | tf_op jit(solution)/shard_map/ppermute | solution.py:152
  10.4 2.1 %collective-permute-start.2 = (bf16[24,3072]{1,0:T(8,128)(2,1)S(1)}, bf16[24,3072]{1,0:T(8,128)(2,1)S(1)}, u32[]{:S(2)}, u32[]{:S(2)}) collective-permute-start(bf16[24,3072]{1,0:T(8,128)(2,1)S(1)} %collective-permute-done.1.refs_0_), channel_id=1, source_target_pairs={{0,4},{1,3},{4,8},{5,1},{8,12},{9,5},{12,14},{13,9},{14,10},{15,13... | collective-permute-start | bytes 442376 | tf_op jit(solution)/shard_map/ppermute | solution.py:152
  12.5 1.6 %collective-permute-start.7 = (bf16[24,3072]{1,0:T(8,128)(2,1)S(1)}, bf16[24,3072]{1,0:T(8,128)(2,1)S(1)}, u32[]{:S(2)}, u32[]{:S(2)}) collective-permute-start(bf16[24,3072]{1,0:T(8,128)(2,1)S(1)} %collective-permute-done.5.refs_8_), channel_id=1, source_target_pairs={{0,4},{1,3},{4,8},{5,1},{8,12},{9,5},{12,14},{13,9},{14,10},{15,13... | collective-permute-start | bytes 442376 | tf_op jit(solution)/shard_map/ppermute | solution.py:152
  15.6 3.1 %collective-permute-start.4 = (bf16[24,3072]{1,0:T(8,128)(2,1)S(1)}, bf16[24,3072]{1,0:T(8,128)(2,1)S(1)}, u32[]{:S(2)}, u32[]{:S(2)}) collective-permute-start(bf16[24,3072]{1,0:T(8,128)(2,1)S(1)} %collective-permute-done.2.refs_1_), channel_id=1, source_target_pairs={{0,8},{1,7},{4,12},{5,3},{8,14},{9,1},{12,10},{13,5},{14,6},{15,9}... | collective-permute-start | bytes 442376 | tf_op jit(solution)/shard_map/ppermute | solution.py:155
  18.7 1.6 %collective-permute-start.3 = (bf16[24,3072]{1,0:T(8,128)(2,1)S(1)}, bf16[24,3072]{1,0:T(8,128)(2,1)S(1)}, u32[]{:S(2)}, u32[]{:S(2)}) collective-permute-start(bf16[24,3072]{1,0:T(8,128)(2,1)S(1)} %collective-permute-done.2.refs_1_), channel_id=1, source_target_pairs={{0,4},{1,3},{4,8},{5,1},{8,12},{9,5},{12,14},{13,9},{14,10},{15,13... | collective-permute-start | bytes 442376 | tf_op jit(solution)/shard_map/ppermute | solution.py:152
  20.2 1.5 %collective-permute-start.9 = (bf16[24,3072]{1,0:T(8,128)(2,1)S(1)}, bf16[24,3072]{1,0:T(8,128)(2,1)S(1)}, u32[]{:S(2)}, u32[]{:S(2)}) collective-permute-start(bf16[24,3072]{1,0:T(8,128)(2,1)S(1)} %collective-permute-done.7.refs_9_), channel_id=1, source_target_pairs={{0,4},{1,3},{4,8},{5,1},{8,12},{9,5},{12,14},{13,9},{14,10},{15,13... | collective-permute-start | bytes 442376 | tf_op jit(solution)/shard_map/ppermute | solution.py:152
  23.9 1.6 %collective-permute-done.9.refs_10_ = bf16[24,3072]{1,0:T(8,128)(2,1)S(1)} collective-permute-done((bf16[24,3072]{1,0:T(8,128)(2,1)S(1)}, bf16[24,3072]{1,0:T(8,128)(2,1)S(1)}, u32[]{:S(2)}, u32[]{:S(2)}) %collective-permute-start.9) | collective-permute-done | bytes 147488 | tf_op jit(solution)/shard_map/ppermute | solution.py:152
  25.5 1.3 %collective-permute-done.10.refs_6_ = bf16[24,3072]{1,0:T(8,128)(2,1)S(1)} collective-permute-done((bf16[24,3072]{1,0:T(8,128)(2,1)S(1)}, bf16[24,3072]{1,0:T(8,128)(2,1)S(1)}, u32[]{:S(2)}, u32[]{:S(2)}) %collective-permute-start.10) | collective-permute-done | bytes 147488 | tf_op jit(solution)/shard_map/ppermute | solution.py:149
  26.9 5.5 %shard_map.66.refs_0_ = bf16[192,672]{1,0:T(8,128)(2,1)S(1)} custom-call(bf16[24,3072]{1,0:T(8,128)(2,1)S(1)} %collective-permute-done.1.refs_0_, bf16[24,3072]{1,0:T(8,128)(2,1)S(1)} %collective-permute-done.2.refs_1_, bf16[24,3072]{1,0:T(8,128)(2,1)S(1)} %collective-permute-done.3.refs_2_, bf16[24,3072]{1,0:T(8,128)(2,1)S(1)} %collective-permute-done.4.refs_3_, ...), custom_call_target="tpu_custom_call" | custom-call | flops 3170893824 | bytes 18874368 | tf_op jit(solution)/shard_map/pallas_call | solution.py:130
  32.5 1.1 %shard_map.67 = (bf16[72,3072]{1,0:T(8,128)(2,1)S(1)}, f32[120,3072]{1,0:T(8,128)S(1)}) custom-call(bf16[192,672]{1,0:T(8,128)(2,1)S(1)} %shard_map.66.refs_0_, bf16[672,6144]{1,0:T(8,128)(2,1)S(1)} %bitcast.3), custom_call_target="tpu_custom_call" | custom-call | flops 792723456 | bytes 8515584 | tf_op jit(solution)/shard_map/pallas_call | solution.py:130
  35.5 2.1 %collective-permute-start.21 = (bf16[24,3072]{1,0:T(8,128)(2,1)S(1)}, bf16[24,3072]{1,0:T(8,128)(2,1)S(1)}, u32[]{:S(2)}, u32[]{:S(2)}) collective-permute-start(bf16[24,3072]{1,0:T(8,128)(2,1)S(1)} %add_convert_fusion.4), channel_id=1, source_target_pairs={{0,4},{1,3},{4,8},{5,1},{8,12},{9,5},{12,14},{13,9},{14,10},{15,13... | collective-permute-start | bytes 442376 | tf_op jit(solution)/shard_map/ppermute | solution.py:152
  37.6 2.5 %collective-permute-start.16 = (bf16[24,3072]{1,0:T(8,128)(2,1)S(1)}, bf16[24,3072]{1,0:T(8,128)(2,1)S(1)}, u32[]{:S(2)}, u32[]{:S(2)}) collective-permute-start(bf16[24,3072]{1,0:T(8,128)(2,1)S(1)} %get-tuple-element.17), channel_id=1, source_target_pairs={{0,4},{1,3},{4,8},{5,1},{8,12},{9,5},{12,14},{13,9},{14,10},{15,13... | collective-permute-start | bytes 442376 | tf_op jit(solution)/shard_map/ppermute | solution.py:152
  40.2 2.4 %collective-permute-start.17 = (bf16[24,3072]{1,0:T(8,128)(2,1)S(1)}, bf16[24,3072]{1,0:T(8,128)(2,1)S(1)}, u32[]{:S(2)}, u32[]{:S(2)}) collective-permute-start(bf16[24,3072]{1,0:T(8,128)(2,1)S(1)} %get-tuple-element.18), channel_id=1, source_target_pairs={{0,8},{1,7},{4,12},{5,3},{8,14},{9,1},{12,10},{13,5},{14,6},{15,9}... | collective-permute-start | bytes 442376 | tf_op jit(solution)/shard_map/ppermute | solution.py:155
  43.7 4.2 %collective-permute-done.17 = bf16[24,3072]{1,0:T(8,128)(2,1)S(1)} collective-permute-done((bf16[24,3072]{1,0:T(8,128)(2,1)S(1)}, bf16[24,3072]{1,0:T(8,128)(2,1)S(1)}, u32[]{:S(2)}, u32[]{:S(2)}) %collective-permute-start.17) | collective-permute-done | bytes 147488 | tf_op jit(solution)/shard_map/ppermute | solution.py:155
  47.9 1.6 %collective-permute-start.18 = (bf16[24,3072]{1,0:T(8,128)(2,1)S(1)}, bf16[24,3072]{1,0:T(8,128)(2,1)S(1)}, u32[]{:S(2)}, u32[]{:S(2)}) collective-permute-start(bf16[24,3072]{1,0:T(8,128)(2,1)S(1)} %add_convert_fusion.6), channel_id=1, source_target_pairs={{0,4},{1,3},{4,8},{5,1},{8,12},{9,5},{12,14},{13,9},{14,10},{15,13... | collective-permute-start | bytes 442376 | tf_op jit(solution)/shard_map/ppermute | solution.py:152
  49.7 3.4 %collective-permute-done.18 = bf16[24,3072]{1,0:T(8,128)(2,1)S(1)} collective-permute-done((bf16[24,3072]{1,0:T(8,128)(2,1)S(1)}, bf16[24,3072]{1,0:T(8,128)(2,1)S(1)}, u32[]{:S(2)}, u32[]{:S(2)}) %collective-permute-start.18) | collective-permute-done | bytes 147488 | tf_op jit(solution)/shard_map/ppermute | solution.py:152
  53.2 1.6 %collective-permute-start.19 = (bf16[24,3072]{1,0:T(8,128)(2,1)S(1)}, bf16[24,3072]{1,0:T(8,128)(2,1)S(1)}, u32[]{:S(2)}, u32[]{:S(2)}) collective-permute-start(bf16[24,3072]{1,0:T(8,128)(2,1)S(1)} %add_convert_fusion.5), channel_id=1, source_target_pairs={{0,4},{1,3},{4,8},{5,1},{8,12},{9,5},{12,14},{13,9},{14,10},{15,13... | collective-permute-start | bytes 442376 | tf_op jit(solution)/shard_map/ppermute | solution.py:152
  54.8 3.5 %collective-permute-done.19.first_ref = bf16[24,3072]{1,0:T(8,128)(2,1)S(1)} collective-permute-done((bf16[24,3072]{1,0:T(8,128)(2,1)S(1)}, bf16[24,3072]{1,0:T(8,128)(2,1)S(1)}, u32[]{:S(2)}, u32[]{:S(2)}) %collective-permute-start.19) | collective-permute-done | bytes 147488 | tf_op jit(solution)/shard_map/ppermute | solution.py:152
  58.5 1.6 %collective-permute-done.24.sibling_ref = bf16[48,3072]{1,0:T(8,128)(2,1)S(1)} collective-permute-done((bf16[48,3072]{1,0:T(8,128)(2,1)S(1)}, bf16[48,3072]{1,0:T(8,128)(2,1)S(1)}, u32[]{:S(2)}, u32[]{:S(2)}) %collective-permute-start.24) | collective-permute-done | bytes 294944 | tf_op jit(solution)/shard_map/ppermute | solution.py:149
  60.1 1.9 %shard_map.69 = bf16[128,6144]{1,0:T(8,128)(2,1)} custom-call(s32[4,128]{1,0:T(4,128)S(1)} %bitcast.9, f32[4,128]{1,0:T(4,128)S(1)} %bitcast.10, bf16[24,3072]{1,0:T(8,128)(2,1)S(1)} %collective-permute-done.19.first_ref, bf16[24,3072]{1,0:T(8,128)(2,1)S(1)} %collective-permute-done.23.second_ref, f32[24,3072]{1,0:T(8,128)S(1)} %get-tuple-element.20.own_first, ...), custom_call_target="tpu_custom_call" | custom-call | bytes 1183744 | tf_op jit(solution)/shard_map/pallas_call | solution.py:130
  (64 shorter events, 8.8 us)
Async XLA Ops:
  2.6 1.7 %collective-permute-start = (bf16[48,3072]{1,0:T(8,128)(2,1)S(1)}, bf16[48,3072]{1,0:T(8,128)(2,1)S(1)}, u32[]{:S(2)}, u32[]{:S(2)}) collective-permute-start(bf16[48,3072]{1,0:T(8,128)(2,1)S(1)} %shard_map.64.own_ref), channel_id=1, source_target_pairs={{0,1},{1,0},{2,3},{3,2},{4,5},{5,4},{6,7},{7,6},{8,9},{9,8},{10,11... | collective-permute-start | bytes 884744 | tf_op jit(solution)/shard_map/ppermute | solution.py:149
  4.4 6.1 %collective-permute-start.1 = (bf16[24,3072]{1,0:T(8,128)(2,1)S(1)}, bf16[24,3072]{1,0:T(8,128)(2,1)S(1)}, u32[]{:S(2)}, u32[]{:S(2)}) collective-permute-start(bf16[24,3072]{1,0:T(8,128)(2,1)S(1)} %get-tuple-element.11.refs_7_), channel_id=1, source_target_pairs={{0,4},{1,3},{4,8},{5,1},{8,12},{9,5},{12,14},{13,9},{14,10},{15,13... | collective-permute-start | bytes 442376 | tf_op jit(solution)/shard_map/ppermute | solution.py:152
  7.4 5.1 %collective-permute-start.5 = (bf16[24,3072]{1,0:T(8,128)(2,1)S(1)}, bf16[24,3072]{1,0:T(8,128)(2,1)S(1)}, u32[]{:S(2)}, u32[]{:S(2)}) collective-permute-start(bf16[24,3072]{1,0:T(8,128)(2,1)S(1)} %get-tuple-element.12.refs_15_), channel_id=1, source_target_pairs={{0,4},{1,3},{4,8},{5,1},{8,12},{9,5},{12,14},{13,9},{14,10},{15,13... | collective-permute-start | bytes 442376 | tf_op jit(solution)/shard_map/ppermute | solution.py:152
  10.4 5.1 %collective-permute-start.2 = (bf16[24,3072]{1,0:T(8,128)(2,1)S(1)}, bf16[24,3072]{1,0:T(8,128)(2,1)S(1)}, u32[]{:S(2)}, u32[]{:S(2)}) collective-permute-start(bf16[24,3072]{1,0:T(8,128)(2,1)S(1)} %collective-permute-done.1.refs_0_), channel_id=1, source_target_pairs={{0,4},{1,3},{4,8},{5,1},{8,12},{9,5},{12,14},{13,9},{14,10},{15,13... | collective-permute-start | bytes 442376 | tf_op jit(solution)/shard_map/ppermute | solution.py:152
  12.5 7.7 %collective-permute-start.7 = (bf16[24,3072]{1,0:T(8,128)(2,1)S(1)}, bf16[24,3072]{1,0:T(8,128)(2,1)S(1)}, u32[]{:S(2)}, u32[]{:S(2)}) collective-permute-start(bf16[24,3072]{1,0:T(8,128)(2,1)S(1)} %collective-permute-done.5.refs_8_), channel_id=1, source_target_pairs={{0,4},{1,3},{4,8},{5,1},{8,12},{9,5},{12,14},{13,9},{14,10},{15,13... | collective-permute-start | bytes 442376 | tf_op jit(solution)/shard_map/ppermute | solution.py:152
  14.1 7.7 %collective-permute-start.12 = (bf16[24,3072]{1,0:T(8,128)(2,1)S(1)}, bf16[24,3072]{1,0:T(8,128)(2,1)S(1)}, u32[]{:S(2)}, u32[]{:S(2)}) collective-permute-start(bf16[24,3072]{1,0:T(8,128)(2,1)S(1)} %collective-permute-done.1.refs_0_), channel_id=1, source_target_pairs={{0,1},{1,0},{2,3},{3,2},{4,5},{5,4},{6,7},{7,6},{8,9},{9,8},{10,11... | collective-permute-start | bytes 442376 | tf_op jit(solution)/shard_map/ppermute | solution.py:149
  14.1 7.7 %collective-permute-start.6 = (bf16[24,3072]{1,0:T(8,128)(2,1)S(1)}, bf16[24,3072]{1,0:T(8,128)(2,1)S(1)}, u32[]{:S(2)}, u32[]{:S(2)}) collective-permute-start(bf16[24,3072]{1,0:T(8,128)(2,1)S(1)} %collective-permute-done.5.refs_8_), channel_id=1, source_target_pairs={{0,1},{1,0},{2,3},{3,2},{4,5},{5,4},{6,7},{7,6},{8,9},{9,8},{10,11... | collective-permute-start | bytes 442376 | tf_op jit(solution)/shard_map/ppermute | solution.py:149
  15.6 7.3 %collective-permute-start.4 = (bf16[24,3072]{1,0:T(8,128)(2,1)S(1)}, bf16[24,3072]{1,0:T(8,128)(2,1)S(1)}, u32[]{:S(2)}, u32[]{:S(2)}) collective-permute-start(bf16[24,3072]{1,0:T(8,128)(2,1)S(1)} %collective-permute-done.2.refs_1_), channel_id=1, source_target_pairs={{0,8},{1,7},{4,12},{5,3},{8,14},{9,1},{12,10},{13,5},{14,6},{15,9}... | collective-permute-start | bytes 442376 | tf_op jit(solution)/shard_map/ppermute | solution.py:155
  18.7 5.3 %collective-permute-start.3 = (bf16[24,3072]{1,0:T(8,128)(2,1)S(1)}, bf16[24,3072]{1,0:T(8,128)(2,1)S(1)}, u32[]{:S(2)}, u32[]{:S(2)}) collective-permute-start(bf16[24,3072]{1,0:T(8,128)(2,1)S(1)} %collective-permute-done.2.refs_1_), channel_id=1, source_target_pairs={{0,4},{1,3},{4,8},{5,1},{8,12},{9,5},{12,14},{13,9},{14,10},{15,13... | collective-permute-start | bytes 442376 | tf_op jit(solution)/shard_map/ppermute | solution.py:152
  20.2 5.3 %collective-permute-start.9 = (bf16[24,3072]{1,0:T(8,128)(2,1)S(1)}, bf16[24,3072]{1,0:T(8,128)(2,1)S(1)}, u32[]{:S(2)}, u32[]{:S(2)}) collective-permute-start(bf16[24,3072]{1,0:T(8,128)(2,1)S(1)} %collective-permute-done.7.refs_9_), channel_id=1, source_target_pairs={{0,4},{1,3},{4,8},{5,1},{8,12},{9,5},{12,14},{13,9},{14,10},{15,13... | collective-permute-start | bytes 442376 | tf_op jit(solution)/shard_map/ppermute | solution.py:152
  21.8 3.8 %collective-permute-start.13 = (bf16[24,3072]{1,0:T(8,128)(2,1)S(1)}, bf16[24,3072]{1,0:T(8,128)(2,1)S(1)}, u32[]{:S(2)}, u32[]{:S(2)}) collective-permute-start(bf16[24,3072]{1,0:T(8,128)(2,1)S(1)} %collective-permute-done.2.refs_1_), channel_id=1, source_target_pairs={{0,1},{1,0},{2,3},{3,2},{4,5},{5,4},{6,7},{7,6},{8,9},{9,8},{10,11... | collective-permute-start | bytes 442376 | tf_op jit(solution)/shard_map/ppermute | solution.py:149
  21.8 3.8 %collective-permute-start.8 = (bf16[24,3072]{1,0:T(8,128)(2,1)S(1)}, bf16[24,3072]{1,0:T(8,128)(2,1)S(1)}, u32[]{:S(2)}, u32[]{:S(2)}) collective-permute-start(bf16[24,3072]{1,0:T(8,128)(2,1)S(1)} %collective-permute-done.7.refs_9_), channel_id=1, source_target_pairs={{0,1},{1,0},{2,3},{3,2},{4,5},{5,4},{6,7},{7,6},{8,9},{9,8},{10,11... | collective-permute-start | bytes 442376 | tf_op jit(solution)/shard_map/ppermute | solution.py:149
  22.9 2.6 %collective-permute-start.11 = (bf16[24,3072]{1,0:T(8,128)(2,1)S(1)}, bf16[24,3072]{1,0:T(8,128)(2,1)S(1)}, u32[]{:S(2)}, u32[]{:S(2)}) collective-permute-start(bf16[24,3072]{1,0:T(8,128)(2,1)S(1)} %collective-permute-done.4.refs_3_), channel_id=1, source_target_pairs={{0,1},{1,0},{2,3},{3,2},{4,5},{5,4},{6,7},{7,6},{8,9},{9,8},{10,11... | collective-permute-start | bytes 442376 | tf_op jit(solution)/shard_map/ppermute | solution.py:149
  23.9 1.6 %collective-permute-start.14 = (bf16[24,3072]{1,0:T(8,128)(2,1)S(1)}, bf16[24,3072]{1,0:T(8,128)(2,1)S(1)}, u32[]{:S(2)}, u32[]{:S(2)}) collective-permute-start(bf16[24,3072]{1,0:T(8,128)(2,1)S(1)} %collective-permute-done.3.refs_2_), channel_id=1, source_target_pairs={{0,1},{1,0},{2,3},{3,2},{4,5},{5,4},{6,7},{7,6},{8,9},{9,8},{10,11... | collective-permute-start | bytes 442376 | tf_op jit(solution)/shard_map/ppermute | solution.py:149
  33.6 1.9 %collective-permute-start.20 = (bf16[72,3072]{1,0:T(8,128)(2,1)S(1)}, bf16[72,3072]{1,0:T(8,128)(2,1)S(1)}, u32[]{:S(2)}, u32[]{:S(2)}) collective-permute-start(bf16[72,3072]{1,0:T(8,128)(2,1)S(1)} %get-tuple-element.16), channel_id=1, source_target_pairs={{0,1},{1,0},{2,3},{3,2},{4,5},{5,4},{6,7},{7,6},{8,9},{9,8},{10,11... | collective-permute-start | bytes 1327112 | tf_op jit(solution)/shard_map/ppermute | solution.py:149
  34.9 2.7 %collective-permute-start.15 = (bf16[96,3072]{1,0:T(8,128)(2,1)S(1)}, bf16[96,3072]{1,0:T(8,128)(2,1)S(1)}, u32[]{:S(2)}, u32[]{:S(2)}) collective-permute-start(bf16[96,3072]{1,0:T(8,128)(2,1)S(1)} %get-tuple-element.14), channel_id=1, source_target_pairs={{0,1},{1,0},{2,3},{3,2},{4,5},{5,4},{6,7},{7,6},{8,9},{9,8},{10,11... | collective-permute-start | bytes 1769480 | tf_op jit(solution)/shard_map/ppermute | solution.py:149
  35.5 7.2 %collective-permute-start.21 = (bf16[24,3072]{1,0:T(8,128)(2,1)S(1)}, bf16[24,3072]{1,0:T(8,128)(2,1)S(1)}, u32[]{:S(2)}, u32[]{:S(2)}) collective-permute-start(bf16[24,3072]{1,0:T(8,128)(2,1)S(1)} %add_convert_fusion.4), channel_id=1, source_target_pairs={{0,4},{1,3},{4,8},{5,1},{8,12},{9,5},{12,14},{13,9},{14,10},{15,13... | collective-permute-start | bytes 442376 | tf_op jit(solution)/shard_map/ppermute | solution.py:152
  37.6 6.0 %collective-permute-start.16 = (bf16[24,3072]{1,0:T(8,128)(2,1)S(1)}, bf16[24,3072]{1,0:T(8,128)(2,1)S(1)}, u32[]{:S(2)}, u32[]{:S(2)}) collective-permute-start(bf16[24,3072]{1,0:T(8,128)(2,1)S(1)} %get-tuple-element.17), channel_id=1, source_target_pairs={{0,4},{1,3},{4,8},{5,1},{8,12},{9,5},{12,14},{13,9},{14,10},{15,13... | collective-permute-start | bytes 442376 | tf_op jit(solution)/shard_map/ppermute | solution.py:152
  40.2 7.7 %collective-permute-start.17 = (bf16[24,3072]{1,0:T(8,128)(2,1)S(1)}, bf16[24,3072]{1,0:T(8,128)(2,1)S(1)}, u32[]{:S(2)}, u32[]{:S(2)}) collective-permute-start(bf16[24,3072]{1,0:T(8,128)(2,1)S(1)} %get-tuple-element.18), channel_id=1, source_target_pairs={{0,8},{1,7},{4,12},{5,3},{8,14},{9,1},{12,10},{13,5},{14,6},{15,9}... | collective-permute-start | bytes 442376 | tf_op jit(solution)/shard_map/ppermute | solution.py:155
  42.7 6.9 %collective-permute-start.22 = (bf16[24,3072]{1,0:T(8,128)(2,1)S(1)}, bf16[24,3072]{1,0:T(8,128)(2,1)S(1)}, u32[]{:S(2)}, u32[]{:S(2)}) collective-permute-start(bf16[24,3072]{1,0:T(8,128)(2,1)S(1)} %add_convert_fusion.3), channel_id=1, source_target_pairs={{0,4},{1,3},{4,8},{5,1},{8,12},{9,5},{12,14},{13,9},{14,10},{15,13... | collective-permute-start | bytes 442376 | tf_op jit(solution)/shard_map/ppermute | solution.py:152
  47.9 5.2 %collective-permute-start.18 = (bf16[24,3072]{1,0:T(8,128)(2,1)S(1)}, bf16[24,3072]{1,0:T(8,128)(2,1)S(1)}, u32[]{:S(2)}, u32[]{:S(2)}) collective-permute-start(bf16[24,3072]{1,0:T(8,128)(2,1)S(1)} %add_convert_fusion.6), channel_id=1, source_target_pairs={{0,4},{1,3},{4,8},{5,1},{8,12},{9,5},{12,14},{13,9},{14,10},{15,13... | collective-permute-start | bytes 442376 | tf_op jit(solution)/shard_map/ppermute | solution.py:152
  49.6 5.2 %collective-permute-start.23 = (bf16[24,3072]{1,0:T(8,128)(2,1)S(1)}, bf16[24,3072]{1,0:T(8,128)(2,1)S(1)}, u32[]{:S(2)}, u32[]{:S(2)}) collective-permute-start(bf16[24,3072]{1,0:T(8,128)(2,1)S(1)} %add_convert_fusion.2), channel_id=1, source_target_pairs={{0,4},{1,3},{4,8},{5,1},{8,12},{9,5},{12,14},{13,9},{14,10},{15,13... | collective-permute-start | bytes 442376 | tf_op jit(solution)/shard_map/ppermute | solution.py:152
  53.2 5.2 %collective-permute-start.19 = (bf16[24,3072]{1,0:T(8,128)(2,1)S(1)}, bf16[24,3072]{1,0:T(8,128)(2,1)S(1)}, u32[]{:S(2)}, u32[]{:S(2)}) collective-permute-start(bf16[24,3072]{1,0:T(8,128)(2,1)S(1)} %add_convert_fusion.5), channel_id=1, source_target_pairs={{0,4},{1,3},{4,8},{5,1},{8,12},{9,5},{12,14},{13,9},{14,10},{15,13... | collective-permute-start | bytes 442376 | tf_op jit(solution)/shard_map/ppermute | solution.py:152
  58.4 1.6 %collective-permute-start.24 = (bf16[48,3072]{1,0:T(8,128)(2,1)S(1)}, bf16[48,3072]{1,0:T(8,128)(2,1)S(1)}, u32[]{:S(2)}, u32[]{:S(2)}) collective-permute-start(bf16[48,3072]{1,0:T(8,128)(2,1)S(1)} %pad_maximum_fusion), channel_id=1, source_target_pairs={{0,1},{1,0},{2,3},{3,2},{4,5},{5,4},{6,7},{7,6},{8,9},{9,8},{10,11... | collective-permute-start | bytes 884744 | tf_op jit(solution)/shard_map/ppermute | solution.py:149
  (11 other events, 182.9 us)

commit v4 on v3

--- a/solution.py
+++ b/solution.py
@@ -162,14 +162,19 @@
         join_kernel, (struct((PAIR, half), BF16),) * 2, own, theirs, flops=40 * rows * units * width
     )
 
-    behind = [(chip_first, chip_second)]
-    ahead = [None]
-    for _ in range(1, reach):
-        first, second = (onward(a) for a in behind[-1])
-        behind.append((first, second))
-        ahead.append((swap(second), swap(first)))
-    far_first = two_on(behind[reach - 2][0])
+    first_behind, second_behind = [chip_first], [chip_second]
+    for distance in range(1, reach):
+        second_behind.append(onward(second_behind[-1]))
+        if distance == 1:
+            first_behind.append(onward(chip_first))
+        elif distance % 2 == 0:
+            first_behind.append(two_on(first_behind[distance - 2]))
+        else:
+            first_behind.append(onward(first_behind[distance - 1]))
+    far_first = two_on(first_behind[reach - 2])
     far_second = swap(far_first)
+    behind = list(zip(first_behind, second_behind))
+    ahead = [None] + [(swap(b), swap(a)) for a, b in behind[1:]]
     order = behind[1:] + [(far_first, far_second)] + ahead[1:] + [behind[0]]
 
     hidden = call(

time: 62.1 us -> 60.1 us (0.968)
  starting transfers between devices: 27.2 us -> 23.8 us
  waiting for transfers between devices: 22 us -> 23.3 us
    ppermute x2 -> x3, waiting for transfers between devices: 4.79 us -> 8.74 us  [two_on(): return lax.ppermute(a, 'tensor', ring_two)]
    ppermute x12 -> x11, starting transfers between devices: 19.4 us -> 16.1 us  [onward(): return lax.ppermute(a, 'tensor', ring_one)]
    ppermute x12 -> x11, waiting for transfers between devices: 12.9 us -> 9.9 us  [onward(): return lax.ppermute(a, 'tensor', ring_one)]
    ppermute x2 -> x3, starting transfers between devices: 5.54 us -> 5.34 us  [two_on(): return lax.ppermute(a, 'tensor', ring_two)]
  transfers between devices with their start and end apart: 25 -> 25, of which waited for: 13 -> 15; matrix products, arithmetic and copies ran while one was open for 1% -> 1% of each run, Pallas kernels for 2% -> 2%
where the time goes in v4:
time: 60.1 us; the launch traced here: 59.9 us
  starting transfers between devices  23.8 us (40%)
  waiting for transfers between devices  23.3 us (39%)
  Pallas kernels  10.1 us (17%)
  local copies, waits for them, and re-layouts  2.14 us (4%)
    ppermute x11, starting transfers between devices, onward(): return lax.ppermute(a, 'tensor', ring_one)  16.1 us
    pallas_call x6, Pallas kernels, call(): pl.pallas_call(kernel, out_shape=out_shape, scratch_shapes=list(scratch),...  10.1 us
    ppermute x11, waiting for transfers between devices, onward(): return lax.ppermute(a, 'tensor', ring_one)  9.9 us
    ppermute x3, waiting for transfers between devices, two_on(): return lax.ppermute(a, 'tensor', ring_two)  8.74 us
    ppermute x3, starting transfers between devices, two_on(): return lax.ppermute(a, 'tensor', ring_two)  5.34 us
    ppermute x11, waiting for transfers between devices, swap(): return lax.ppermute(a, 'tensor', pair_core)  4.7 us
    ppermute x11, starting transfers between devices, swap(): return lax.ppermute(a, 'tensor', pair_core)  2.33 us
    unnamed x20, local copies, waits for them, and re-layouts  2.14 us
  transfers between devices with their start and end apart: 25, of which 15 were waited for; matrix products, arithmetic and copies ran while one was open for 1% of the time, Pallas kernels for 2%

profile of v4, /device:TPU:0, one launch (start us, length us, event | category | flops | bytes accessed | tf_op | source)
XLA Modules:
  0.0 59.9 jit_solution(15818336166639684976)
XLA Ops:
  0.0 1.4 %copy-done = bf16[128,6144]{1,0:T(8,128)(2,1)S(1)} copy-done((bf16[128,6144]{1,0:T(8,128)(2,1)S(1)}, bf16[128,6144]{1,0:T(8,128)(2,1)}, u32[]{:S(2)}) %copy-start) | copy-done | bytes 1572888
  3.1 1.2 %collective-permute-done.theirs_ref = bf16[48,3072]{1,0:T(8,128)(2,1)S(1)} collective-permute-done((bf16[48,3072]{1,0:T(8,128)(2,1)S(1)}, bf16[48,3072]{1,0:T(8,128)(2,1)S(1)}, u32[]{:S(2)}, u32[]{:S(2)}) %collective-permute-start) | collective-permute-done | bytes 294944 | tf_op jit(solution)/shard_map/ppermute | solution.py:149
  4.4 3.0 %collective-permute-start.5 = (bf16[24,3072]{1,0:T(8,128)(2,1)S(1)}, bf16[24,3072]{1,0:T(8,128)(2,1)S(1)}, u32[]{:S(2)}, u32[]{:S(2)}) collective-permute-start(bf16[24,3072]{1,0:T(8,128)(2,1)S(1)} %get-tuple-element.12.refs_15_), channel_id=1, source_target_pairs={{0,4},{1,3},{4,8},{5,1},{8,12},{9,5},{12,14},{13,9},{14,10},{15,13... | collective-permute-start | bytes 442376 | tf_op jit(solution)/shard_map/ppermute | solution.py:152
  7.4 2.6 %collective-permute-start.2 = (bf16[24,3072]{1,0:T(8,128)(2,1)S(1)}, bf16[24,3072]{1,0:T(8,128)(2,1)S(1)}, u32[]{:S(2)}, u32[]{:S(2)}) collective-permute-start(bf16[24,3072]{1,0:T(8,128)(2,1)S(1)} %get-tuple-element.11.refs_7_), channel_id=1, source_target_pairs={{0,8},{1,7},{4,12},{5,3},{8,14},{9,1},{12,10},{13,5},{14,6},{15,9}... | collective-permute-start | bytes 442376 | tf_op jit(solution)/shard_map/ppermute | solution.py:155
  9.9 1.5 %collective-permute-start.1 = (bf16[24,3072]{1,0:T(8,128)(2,1)S(1)}, bf16[24,3072]{1,0:T(8,128)(2,1)S(1)}, u32[]{:S(2)}, u32[]{:S(2)}) collective-permute-start(bf16[24,3072]{1,0:T(8,128)(2,1)S(1)} %get-tuple-element.11.refs_7_), channel_id=1, source_target_pairs={{0,4},{1,3},{4,8},{5,1},{8,12},{9,5},{12,14},{13,9},{14,10},{15,13... | collective-permute-start | bytes 442376 | tf_op jit(solution)/shard_map/ppermute | solution.py:152
  11.5 1.1 %collective-permute-start.7 = (bf16[24,3072]{1,0:T(8,128)(2,1)S(1)}, bf16[24,3072]{1,0:T(8,128)(2,1)S(1)}, u32[]{:S(2)}, u32[]{:S(2)}) collective-permute-start(bf16[24,3072]{1,0:T(8,128)(2,1)S(1)} %collective-permute-done.5.refs_8_), channel_id=1, source_target_pairs={{0,4},{1,3},{4,8},{5,1},{8,12},{9,5},{12,14},{13,9},{14,10},{15,13... | collective-permute-start | bytes 442376 | tf_op jit(solution)/shard_map/ppermute | solution.py:152
  12.6 2.5 %collective-permute-done.2.refs_1_ = bf16[24,3072]{1,0:T(8,128)(2,1)S(1)} collective-permute-done((bf16[24,3072]{1,0:T(8,128)(2,1)S(1)}, bf16[24,3072]{1,0:T(8,128)(2,1)S(1)}, u32[]{:S(2)}, u32[]{:S(2)}) %collective-permute-start.2) | collective-permute-done | bytes 147488 | tf_op jit(solution)/shard_map/ppermute | solution.py:155
  15.1 1.5 %collective-permute-start.4 = (bf16[24,3072]{1,0:T(8,128)(2,1)S(1)}, bf16[24,3072]{1,0:T(8,128)(2,1)S(1)}, u32[]{:S(2)}, u32[]{:S(2)}) collective-permute-start(bf16[24,3072]{1,0:T(8,128)(2,1)S(1)} %collective-permute-done.2.refs_1_), channel_id=1, source_target_pairs={{0,8},{1,7},{4,12},{5,3},{8,14},{9,1},{12,10},{13,5},{14,6},{15,9}... | collective-permute-start | bytes 442376 | tf_op jit(solution)/shard_map/ppermute | solution.py:155
  16.7 2.5 %collective-permute-start.3 = (bf16[24,3072]{1,0:T(8,128)(2,1)S(1)}, bf16[24,3072]{1,0:T(8,128)(2,1)S(1)}, u32[]{:S(2)}, u32[]{:S(2)}) collective-permute-start(bf16[24,3072]{1,0:T(8,128)(2,1)S(1)} %collective-permute-done.2.refs_1_), channel_id=1, source_target_pairs={{0,4},{1,3},{4,8},{5,1},{8,12},{9,5},{12,14},{13,9},{14,10},{15,13... | collective-permute-start | bytes 442376 | tf_op jit(solution)/shard_map/ppermute | solution.py:152
  19.7 2.8 %collective-permute-done.4.refs_3_ = bf16[24,3072]{1,0:T(8,128)(2,1)S(1)} collective-permute-done((bf16[24,3072]{1,0:T(8,128)(2,1)S(1)}, bf16[24,3072]{1,0:T(8,128)(2,1)S(1)}, u32[]{:S(2)}, u32[]{:S(2)}) %collective-permute-start.4) | collective-permute-done | bytes 147488 | tf_op jit(solution)/shard_map/ppermute | solution.py:155
  25.2 1.1 %collective-permute-done.10.refs_6_ = bf16[24,3072]{1,0:T(8,128)(2,1)S(1)} collective-permute-done((bf16[24,3072]{1,0:T(8,128)(2,1)S(1)}, bf16[24,3072]{1,0:T(8,128)(2,1)S(1)}, u32[]{:S(2)}, u32[]{:S(2)}) %collective-permute-start.10) | collective-permute-done | bytes 147488 | tf_op jit(solution)/shard_map/ppermute | solution.py:149
  26.3 5.5 %shard_map.66.refs_0_ = bf16[192,672]{1,0:T(8,128)(2,1)S(1)} custom-call(bf16[24,3072]{1,0:T(8,128)(2,1)S(1)} %collective-permute-done.1.refs_0_, bf16[24,3072]{1,0:T(8,128)(2,1)S(1)} %collective-permute-done.2.refs_1_, bf16[24,3072]{1,0:T(8,128)(2,1)S(1)} %collective-permute-done.3.refs_2_, bf16[24,3072]{1,0:T(8,128)(2,1)S(1)} %collective-permute-done.4.refs_3_, ...), custom_call_target="tpu_custom_call" | custom-call | flops 3170893824 | bytes 18874368 | tf_op jit(solution)/shard_map/pallas_call | solution.py:130
  31.9 1.1 %shard_map.67 = (bf16[72,3072]{1,0:T(8,128)(2,1)S(1)}, f32[120,3072]{1,0:T(8,128)S(1)}) custom-call(bf16[192,672]{1,0:T(8,128)(2,1)S(1)} %shard_map.66.refs_0_, bf16[672,6144]{1,0:T(8,128)(2,1)S(1)} %bitcast.3), custom_call_target="tpu_custom_call" | custom-call | flops 792723456 | bytes 8515584 | tf_op jit(solution)/shard_map/pallas_call | solution.py:130
  33.2 1.1 %shard_map.68 = (bf16[96,3072]{1,0:T(8,128)(2,1)S(1)}, f32[96,3072]{1,0:T(8,128)S(1)}) custom-call(bf16[192,672]{1,0:T(8,128)(2,1)S(1)} %shard_map.66.refs_0_, bf16[672,6144]{1,0:T(8,128)(2,1)S(1)} %bitcast.3), custom_call_target="tpu_custom_call" | custom-call | flops 792723456 | bytes 8515584 | tf_op jit(solution)/shard_map/pallas_call | solution.py:130
  36.4 2.0 %collective-permute-start.16 = (bf16[24,3072]{1,0:T(8,128)(2,1)S(1)}, bf16[24,3072]{1,0:T(8,128)(2,1)S(1)}, u32[]{:S(2)}, u32[]{:S(2)}) collective-permute-start(bf16[24,3072]{1,0:T(8,128)(2,1)S(1)} %get-tuple-element.17), channel_id=1, source_target_pairs={{0,4},{1,3},{4,8},{5,1},{8,12},{9,5},{12,14},{13,9},{14,10},{15,13... | collective-permute-start | bytes 442376 | tf_op jit(solution)/shard_map/ppermute | solution.py:152
  38.4 1.2 %collective-permute-start.17 = (bf16[24,3072]{1,0:T(8,128)(2,1)S(1)}, bf16[24,3072]{1,0:T(8,128)(2,1)S(1)}, u32[]{:S(2)}, u32[]{:S(2)}) collective-permute-start(bf16[24,3072]{1,0:T(8,128)(2,1)S(1)} %get-tuple-element.18), channel_id=1, source_target_pairs={{0,8},{1,7},{4,12},{5,3},{8,14},{9,1},{12,10},{13,5},{14,6},{15,9}... | collective-permute-start | bytes 442376 | tf_op jit(solution)/shard_map/ppermute | solution.py:155
  41.1 1.3 %collective-permute-done.16 = bf16[24,3072]{1,0:T(8,128)(2,1)S(1)} collective-permute-done((bf16[24,3072]{1,0:T(8,128)(2,1)S(1)}, bf16[24,3072]{1,0:T(8,128)(2,1)S(1)}, u32[]{:S(2)}, u32[]{:S(2)}) %collective-permute-start.16) | collective-permute-done | bytes 147488 | tf_op jit(solution)/shard_map/ppermute | solution.py:152
  42.4 3.4 %collective-permute-done.17 = bf16[24,3072]{1,0:T(8,128)(2,1)S(1)} collective-permute-done((bf16[24,3072]{1,0:T(8,128)(2,1)S(1)}, bf16[24,3072]{1,0:T(8,128)(2,1)S(1)}, u32[]{:S(2)}, u32[]{:S(2)}) %collective-permute-start.17) | collective-permute-done | bytes 147488 | tf_op jit(solution)/shard_map/ppermute | solution.py:155
  45.9 1.5 %collective-permute-start.18 = (bf16[24,3072]{1,0:T(8,128)(2,1)S(1)}, bf16[24,3072]{1,0:T(8,128)(2,1)S(1)}, u32[]{:S(2)}, u32[]{:S(2)}) collective-permute-start(bf16[24,3072]{1,0:T(8,128)(2,1)S(1)} %add_convert_fusion.6), channel_id=1, source_target_pairs={{0,4},{1,3},{4,8},{5,1},{8,12},{9,5},{12,14},{13,9},{14,10},{15,13... | collective-permute-start | bytes 442376 | tf_op jit(solution)/shard_map/ppermute | solution.py:152
  48.3 2.8 %collective-permute-done.18 = bf16[24,3072]{1,0:T(8,128)(2,1)S(1)} collective-permute-done((bf16[24,3072]{1,0:T(8,128)(2,1)S(1)}, bf16[24,3072]{1,0:T(8,128)(2,1)S(1)}, u32[]{:S(2)}, u32[]{:S(2)}) %collective-permute-start.18) | collective-permute-done | bytes 147488 | tf_op jit(solution)/shard_map/ppermute | solution.py:152
  51.1 1.5 %collective-permute-start.19 = (bf16[24,3072]{1,0:T(8,128)(2,1)S(1)}, bf16[24,3072]{1,0:T(8,128)(2,1)S(1)}, u32[]{:S(2)}, u32[]{:S(2)}) collective-permute-start(bf16[24,3072]{1,0:T(8,128)(2,1)S(1)} %add_convert_fusion.5), channel_id=1, source_target_pairs={{0,4},{1,3},{4,8},{5,1},{8,12},{9,5},{12,14},{13,9},{14,10},{15,13... | collective-permute-start | bytes 442376 | tf_op jit(solution)/shard_map/ppermute | solution.py:152
  52.7 3.6 %collective-permute-done.19.first_ref = bf16[24,3072]{1,0:T(8,128)(2,1)S(1)} collective-permute-done((bf16[24,3072]{1,0:T(8,128)(2,1)S(1)}, bf16[24,3072]{1,0:T(8,128)(2,1)S(1)}, u32[]{:S(2)}, u32[]{:S(2)}) %collective-permute-start.19) | collective-permute-done | bytes 147488 | tf_op jit(solution)/shard_map/ppermute | solution.py:152
  56.5 1.6 %collective-permute-done.24.sibling_ref = bf16[48,3072]{1,0:T(8,128)(2,1)S(1)} collective-permute-done((bf16[48,3072]{1,0:T(8,128)(2,1)S(1)}, bf16[48,3072]{1,0:T(8,128)(2,1)S(1)}, u32[]{:S(2)}, u32[]{:S(2)}) %collective-permute-start.24) | collective-permute-done | bytes 294944 | tf_op jit(solution)/shard_map/ppermute | solution.py:149
  58.0 1.9 %shard_map.69 = bf16[128,6144]{1,0:T(8,128)(2,1)} custom-call(s32[4,128]{1,0:T(4,128)S(1)} %bitcast.9, f32[4,128]{1,0:T(4,128)S(1)} %bitcast.10, bf16[24,3072]{1,0:T(8,128)(2,1)S(1)} %collective-permute-done.19.first_ref, bf16[24,3072]{1,0:T(8,128)(2,1)S(1)} %collective-permute-done.23.second_ref, f32[24,3072]{1,0:T(8,128)S(1)} %get-tuple-element.20.own_first, ...), custom_call_target="tpu_custom_call" | custom-call | bytes 1183744 | tf_op jit(solution)/shard_map/pallas_call | solution.py:130
  (64 shorter events, 10.0 us)
Async XLA Ops:
  2.6 1.7 %collective-permute-start = (bf16[48,3072]{1,0:T(8,128)(2,1)S(1)}, bf16[48,3072]{1,0:T(8,128)(2,1)S(1)}, u32[]{:S(2)}, u32[]{:S(2)}) collective-permute-start(bf16[48,3072]{1,0:T(8,128)(2,1)S(1)} %shard_map.64.own_ref), channel_id=1, source_target_pairs={{0,1},{1,0},{2,3},{3,2},{4,5},{5,4},{6,7},{7,6},{8,9},{9,8},{10,11... | collective-permute-start | bytes 884744 | tf_op jit(solution)/shard_map/ppermute | solution.py:149
  4.4 7.1 %collective-permute-start.5 = (bf16[24,3072]{1,0:T(8,128)(2,1)S(1)}, bf16[24,3072]{1,0:T(8,128)(2,1)S(1)}, u32[]{:S(2)}, u32[]{:S(2)}) collective-permute-start(bf16[24,3072]{1,0:T(8,128)(2,1)S(1)} %get-tuple-element.12.refs_15_), channel_id=1, source_target_pairs={{0,4},{1,3},{4,8},{5,1},{8,12},{9,5},{12,14},{13,9},{14,10},{15,13... | collective-permute-start | bytes 442376 | tf_op jit(solution)/shard_map/ppermute | solution.py:152
  7.4 7.8 %collective-permute-start.2 = (bf16[24,3072]{1,0:T(8,128)(2,1)S(1)}, bf16[24,3072]{1,0:T(8,128)(2,1)S(1)}, u32[]{:S(2)}, u32[]{:S(2)}) collective-permute-start(bf16[24,3072]{1,0:T(8,128)(2,1)S(1)} %get-tuple-element.11.refs_7_), channel_id=1, source_target_pairs={{0,8},{1,7},{4,12},{5,3},{8,14},{9,1},{12,10},{13,5},{14,6},{15,9}... | collective-permute-start | bytes 442376 | tf_op jit(solution)/shard_map/ppermute | solution.py:155
  9.9 9.2 %collective-permute-start.1 = (bf16[24,3072]{1,0:T(8,128)(2,1)S(1)}, bf16[24,3072]{1,0:T(8,128)(2,1)S(1)}, u32[]{:S(2)}, u32[]{:S(2)}) collective-permute-start(bf16[24,3072]{1,0:T(8,128)(2,1)S(1)} %get-tuple-element.11.refs_7_), channel_id=1, source_target_pairs={{0,4},{1,3},{4,8},{5,1},{8,12},{9,5},{12,14},{13,9},{14,10},{15,13... | collective-permute-start | bytes 442376 | tf_op jit(solution)/shard_map/ppermute | solution.py:152
  11.5 8.2 %collective-permute-start.7 = (bf16[24,3072]{1,0:T(8,128)(2,1)S(1)}, bf16[24,3072]{1,0:T(8,128)(2,1)S(1)}, u32[]{:S(2)}, u32[]{:S(2)}) collective-permute-start(bf16[24,3072]{1,0:T(8,128)(2,1)S(1)} %collective-permute-done.5.refs_8_), channel_id=1, source_target_pairs={{0,4},{1,3},{4,8},{5,1},{8,12},{9,5},{12,14},{13,9},{14,10},{15,13... | collective-permute-start | bytes 442376 | tf_op jit(solution)/shard_map/ppermute | solution.py:152
  15.1 7.4 %collective-permute-start.4 = (bf16[24,3072]{1,0:T(8,128)(2,1)S(1)}, bf16[24,3072]{1,0:T(8,128)(2,1)S(1)}, u32[]{:S(2)}, u32[]{:S(2)}) collective-permute-start(bf16[24,3072]{1,0:T(8,128)(2,1)S(1)} %collective-permute-done.2.refs_1_), channel_id=1, source_target_pairs={{0,8},{1,7},{4,12},{5,3},{8,14},{9,1},{12,10},{13,5},{14,6},{15,9}... | collective-permute-start | bytes 442376 | tf_op jit(solution)/shard_map/ppermute | solution.py:155
  16.7 6.7 %collective-permute-start.3 = (bf16[24,3072]{1,0:T(8,128)(2,1)S(1)}, bf16[24,3072]{1,0:T(8,128)(2,1)S(1)}, u32[]{:S(2)}, u32[]{:S(2)}) collective-permute-start(bf16[24,3072]{1,0:T(8,128)(2,1)S(1)} %collective-permute-done.2.refs_1_), channel_id=1, source_target_pairs={{0,4},{1,3},{4,8},{5,1},{8,12},{9,5},{12,14},{13,9},{14,10},{15,13... | collective-permute-start | bytes 442376 | tf_op jit(solution)/shard_map/ppermute | solution.py:152
  19.2 4.2 %collective-permute-start.13 = (bf16[24,3072]{1,0:T(8,128)(2,1)S(1)}, bf16[24,3072]{1,0:T(8,128)(2,1)S(1)}, u32[]{:S(2)}, u32[]{:S(2)}) collective-permute-start(bf16[24,3072]{1,0:T(8,128)(2,1)S(1)} %collective-permute-done.2.refs_1_), channel_id=1, source_target_pairs={{0,1},{1,0},{2,3},{3,2},{4,5},{5,4},{6,7},{7,6},{8,9},{9,8},{10,11... | collective-permute-start | bytes 442376 | tf_op jit(solution)/shard_map/ppermute | solution.py:149
  19.2 4.7 %collective-permute-start.12 = (bf16[24,3072]{1,0:T(8,128)(2,1)S(1)}, bf16[24,3072]{1,0:T(8,128)(2,1)S(1)}, u32[]{:S(2)}, u32[]{:S(2)}) collective-permute-start(bf16[24,3072]{1,0:T(8,128)(2,1)S(1)} %collective-permute-done.1.refs_0_), channel_id=1, source_target_pairs={{0,1},{1,0},{2,3},{3,2},{4,5},{5,4},{6,7},{7,6},{8,9},{9,8},{10,11... | collective-permute-start | bytes 442376 | tf_op jit(solution)/shard_map/ppermute | solution.py:149
  19.7 5.2 %collective-permute-start.9 = (bf16[24,3072]{1,0:T(8,128)(2,1)S(1)}, bf16[24,3072]{1,0:T(8,128)(2,1)S(1)}, u32[]{:S(2)}, u32[]{:S(2)}) collective-permute-start(bf16[24,3072]{1,0:T(8,128)(2,1)S(1)} %collective-permute-done.7.refs_9_), channel_id=1, source_target_pairs={{0,4},{1,3},{4,8},{5,1},{8,12},{9,5},{12,14},{13,9},{14,10},{15,13... | collective-permute-start | bytes 442376 | tf_op jit(solution)/shard_map/ppermute | solution.py:152
  22.5 2.4 %collective-permute-start.6 = (bf16[24,3072]{1,0:T(8,128)(2,1)S(1)}, bf16[24,3072]{1,0:T(8,128)(2,1)S(1)}, u32[]{:S(2)}, u32[]{:S(2)}) collective-permute-start(bf16[24,3072]{1,0:T(8,128)(2,1)S(1)} %collective-permute-done.5.refs_8_), channel_id=1, source_target_pairs={{0,1},{1,0},{2,3},{3,2},{4,5},{5,4},{6,7},{7,6},{8,9},{9,8},{10,11... | collective-permute-start | bytes 442376 | tf_op jit(solution)/shard_map/ppermute | solution.py:149
  23.3 1.9 %collective-permute-start.8 = (bf16[24,3072]{1,0:T(8,128)(2,1)S(1)}, bf16[24,3072]{1,0:T(8,128)(2,1)S(1)}, u32[]{:S(2)}, u32[]{:S(2)}) collective-permute-start(bf16[24,3072]{1,0:T(8,128)(2,1)S(1)} %collective-permute-done.7.refs_9_), channel_id=1, source_target_pairs={{0,1},{1,0},{2,3},{3,2},{4,5},{5,4},{6,7},{7,6},{8,9},{9,8},{10,11... | collective-permute-start | bytes 442376 | tf_op jit(solution)/shard_map/ppermute | solution.py:149
  23.3 1.6 %collective-permute-start.11 = (bf16[24,3072]{1,0:T(8,128)(2,1)S(1)}, bf16[24,3072]{1,0:T(8,128)(2,1)S(1)}, u32[]{:S(2)}, u32[]{:S(2)}) collective-permute-start(bf16[24,3072]{1,0:T(8,128)(2,1)S(1)} %collective-permute-done.4.refs_3_), channel_id=1, source_target_pairs={{0,1},{1,0},{2,3},{3,2},{4,5},{5,4},{6,7},{7,6},{8,9},{9,8},{10,11... | collective-permute-start | bytes 442376 | tf_op jit(solution)/shard_map/ppermute | solution.py:149
  23.8 1.4 %collective-permute-start.14 = (bf16[24,3072]{1,0:T(8,128)(2,1)S(1)}, bf16[24,3072]{1,0:T(8,128)(2,1)S(1)}, u32[]{:S(2)}, u32[]{:S(2)}) collective-permute-start(bf16[24,3072]{1,0:T(8,128)(2,1)S(1)} %collective-permute-done.3.refs_2_), channel_id=1, source_target_pairs={{0,1},{1,0},{2,3},{3,2},{4,5},{5,4},{6,7},{7,6},{8,9},{9,8},{10,11... | collective-permute-start | bytes 442376 | tf_op jit(solution)/shard_map/ppermute | solution.py:149
  33.0 1.9 %collective-permute-start.20 = (bf16[72,3072]{1,0:T(8,128)(2,1)S(1)}, bf16[72,3072]{1,0:T(8,128)(2,1)S(1)}, u32[]{:S(2)}, u32[]{:S(2)}) collective-permute-start(bf16[72,3072]{1,0:T(8,128)(2,1)S(1)} %get-tuple-element.16), channel_id=1, source_target_pairs={{0,1},{1,0},{2,3},{3,2},{4,5},{5,4},{6,7},{7,6},{8,9},{9,8},{10,11... | collective-permute-start | bytes 1327112 | tf_op jit(solution)/shard_map/ppermute | solution.py:149
  34.2 2.1 %collective-permute-start.15 = (bf16[96,3072]{1,0:T(8,128)(2,1)S(1)}, bf16[96,3072]{1,0:T(8,128)(2,1)S(1)}, u32[]{:S(2)}, u32[]{:S(2)}) collective-permute-start(bf16[96,3072]{1,0:T(8,128)(2,1)S(1)} %get-tuple-element.14), channel_id=1, source_target_pairs={{0,1},{1,0},{2,3},{3,2},{4,5},{5,4},{6,7},{7,6},{8,9},{9,8},{10,11... | collective-permute-start | bytes 1769480 | tf_op jit(solution)/shard_map/ppermute | solution.py:149
  34.8 5.2 %collective-permute-start.21 = (bf16[24,3072]{1,0:T(8,128)(2,1)S(1)}, bf16[24,3072]{1,0:T(8,128)(2,1)S(1)}, u32[]{:S(2)}, u32[]{:S(2)}) collective-permute-start(bf16[24,3072]{1,0:T(8,128)(2,1)S(1)} %add_convert_fusion.4), channel_id=1, source_target_pairs={{0,4},{1,3},{4,8},{5,1},{8,12},{9,5},{12,14},{13,9},{14,10},{15,13... | collective-permute-start | bytes 442376 | tf_op jit(solution)/shard_map/ppermute | solution.py:152
  36.4 6.0 %collective-permute-start.16 = (bf16[24,3072]{1,0:T(8,128)(2,1)S(1)}, bf16[24,3072]{1,0:T(8,128)(2,1)S(1)}, u32[]{:S(2)}, u32[]{:S(2)}) collective-permute-start(bf16[24,3072]{1,0:T(8,128)(2,1)S(1)} %get-tuple-element.17), channel_id=1, source_target_pairs={{0,4},{1,3},{4,8},{5,1},{8,12},{9,5},{12,14},{13,9},{14,10},{15,13... | collective-permute-start | bytes 442376 | tf_op jit(solution)/shard_map/ppermute | solution.py:152
  38.4 7.4 %collective-permute-start.17 = (bf16[24,3072]{1,0:T(8,128)(2,1)S(1)}, bf16[24,3072]{1,0:T(8,128)(2,1)S(1)}, u32[]{:S(2)}, u32[]{:S(2)}) collective-permute-start(bf16[24,3072]{1,0:T(8,128)(2,1)S(1)} %get-tuple-element.18), channel_id=1, source_target_pairs={{0,8},{1,7},{4,12},{5,3},{8,14},{9,1},{12,10},{13,5},{14,6},{15,9}... | collective-permute-start | bytes 442376 | tf_op jit(solution)/shard_map/ppermute | solution.py:155
  40.1 7.3 %collective-permute-start.22 = (bf16[24,3072]{1,0:T(8,128)(2,1)S(1)}, bf16[24,3072]{1,0:T(8,128)(2,1)S(1)}, u32[]{:S(2)}, u32[]{:S(2)}) collective-permute-start(bf16[24,3072]{1,0:T(8,128)(2,1)S(1)} %add_convert_fusion.3), channel_id=1, source_target_pairs={{0,4},{1,3},{4,8},{5,1},{8,12},{9,5},{12,14},{13,9},{14,10},{15,13... | collective-permute-start | bytes 442376 | tf_op jit(solution)/shard_map/ppermute | solution.py:152
  45.9 5.2 %collective-permute-start.18 = (bf16[24,3072]{1,0:T(8,128)(2,1)S(1)}, bf16[24,3072]{1,0:T(8,128)(2,1)S(1)}, u32[]{:S(2)}, u32[]{:S(2)}) collective-permute-start(bf16[24,3072]{1,0:T(8,128)(2,1)S(1)} %add_convert_fusion.6), channel_id=1, source_target_pairs={{0,4},{1,3},{4,8},{5,1},{8,12},{9,5},{12,14},{13,9},{14,10},{15,13... | collective-permute-start | bytes 442376 | tf_op jit(solution)/shard_map/ppermute | solution.py:152
  47.5 5.2 %collective-permute-start.23 = (bf16[24,3072]{1,0:T(8,128)(2,1)S(1)}, bf16[24,3072]{1,0:T(8,128)(2,1)S(1)}, u32[]{:S(2)}, u32[]{:S(2)}) collective-permute-start(bf16[24,3072]{1,0:T(8,128)(2,1)S(1)} %add_convert_fusion.2), channel_id=1, source_target_pairs={{0,4},{1,3},{4,8},{5,1},{8,12},{9,5},{12,14},{13,9},{14,10},{15,13... | collective-permute-start | bytes 442376 | tf_op jit(solution)/shard_map/ppermute | solution.py:152
  51.1 5.2 %collective-permute-start.19 = (bf16[24,3072]{1,0:T(8,128)(2,1)S(1)}, bf16[24,3072]{1,0:T(8,128)(2,1)S(1)}, u32[]{:S(2)}, u32[]{:S(2)}) collective-permute-start(bf16[24,3072]{1,0:T(8,128)(2,1)S(1)} %add_convert_fusion.5), channel_id=1, source_target_pairs={{0,4},{1,3},{4,8},{5,1},{8,12},{9,5},{12,14},{13,9},{14,10},{15,13... | collective-permute-start | bytes 442376 | tf_op jit(solution)/shard_map/ppermute | solution.py:152
  56.4 1.6 %collective-permute-start.24 = (bf16[48,3072]{1,0:T(8,128)(2,1)S(1)}, bf16[48,3072]{1,0:T(8,128)(2,1)S(1)}, u32[]{:S(2)}, u32[]{:S(2)}) collective-permute-start(bf16[48,3072]{1,0:T(8,128)(2,1)S(1)} %pad_maximum_fusion), channel_id=1, source_target_pairs={{0,1},{1,0},{2,3},{3,2},{4,5},{5,4},{6,7},{7,6},{8,9},{9,8},{10,11... | collective-permute-start | bytes 884744 | tf_op jit(solution)/shard_map/ppermute | solution.py:149
  (11 other events, 179.5 us)

commit v5 on v0

v5 whole, which is shorter than its diff:
```python
import jax
import jax.numpy as jnp
from jax import lax
from jax.experimental import pallas as pl
from jax.experimental.pallas import tpu as pltpu
from jax.sharding import PartitionSpec as P

CAP = 12
PAIR = 2 * CAP
F32 = jnp.float32
BF16 = jnp.bfloat16
MIB = 2**20


def permutations(size):
    chips = size // 2
    order = list(range(0, chips, 2)) + list(range(chips - 1, 0, -2))

    def pairs(target):
        made = []
        for place, chip in enumerate(order):
            for core in range(2):
                step, to = target(core)
                made.append((2 * chip + core, 2 * order[(place + step) % chips] + to))
        return made

    way = (1, -1)
    return {
        "swap": pairs(lambda core: (0, 1 - core)),
        "one": pairs(lambda core: (way[core], core)),
        "two": pairs(lambda core: (2 * way[core], core)),
        "board": pairs(lambda core: (way[1 - core], 1 - core)),
        "leave": pairs(lambda core: (way[core], 1 - core)),
    }


def choose(ids):
    tokens = ids.shape[1]
    routed = jnp.max(jnp.where(ids == 0, 1.0, 0.0), axis=0, keepdims=True)
    earlier = lax.broadcasted_iota(jnp.int32, (tokens, tokens), 0) < lax.broadcasted_iota(
        jnp.int32, (tokens, tokens), 1
    )
    before = jnp.dot(
        jnp.broadcast_to(routed, (8, tokens)).astype(BF16),
        jnp.where(earlier, 1.0, 0.0).astype(BF16),
        preferred_element_type=F32,
    )[:1]

    def rows(first):
        slot = lax.broadcasted_iota(jnp.int32, (PAIR, tokens), 0) - first
        return jnp.where((slot.astype(F32) == before) & (routed > 0.0), 1.0, 0.0).astype(BF16)

    return rows(0), rows(CAP)


def compact_kernel(ids_ref, tokens_ref, out_ref):
    half = out_ref.shape[1]
    upper, lower = choose(ids_ref[...])
    out_ref[...] = (
        jnp.dot(upper, tokens_ref[:, :half], preferred_element_type=F32)
        + jnp.dot(lower, tokens_ref[:, half:], preferred_element_type=F32)
    ).astype(BF16)


def hidden_kernel(count, *refs):
    blocks, (gate_ref, up_ref, out_ref, first, second) = refs[:count], refs[count:]
    units, width = gate_ref.shape
    half = width // 2
    for j, block in enumerate(blocks):
        first[j * CAP : (j + 1) * CAP, :] = block[:CAP, :]
        second[j * CAP : (j + 1) * CAP, :] = block[CAP:, :]
    contract = (((1,), (1,)), ((), ()))

    def product(ref, here):
        return lax.dot_general(
            first[...], ref[here, :half], contract, preferred_element_type=F32
        ) + lax.dot_general(second[...], ref[here, half:], contract, preferred_element_type=F32)

    tile = 224 if units % 224 == 0 else units
    for start in range(0, units, tile):
        here = slice(start, start + tile)
        gate = product(gate_ref, here)
        up = product(up_ref, here)
        out_ref[:, here] = (gate / (1.0 + jnp.exp(-gate)) * up).astype(BF16)


def down_kernel(places, hidden_ref, down_ref, *out_refs):
    half = down_ref.shape[1] // 2
    tile = half // 3
    for step in range(3):
        here = slice(step * tile, (step + 1) * tile)
        low, high = (
            jnp.dot(
                hidden_ref[...],
                down_ref[:, start + step * tile : start + (step + 1) * tile],
                preferred_element_type=F32,
            )
            for start in (0, half)
        )
        for out_ref, indices in zip(out_refs, places):
            for k, j in enumerate(indices):
                rows = slice(j * CAP, (j + 1) * CAP)
                out_ref[k * PAIR : (k + 1) * PAIR, here] = jnp.concatenate(
                    [low[rows], high[rows]]
                ).astype(out_ref.dtype)


def mix_kernel(ids_ref, gates_ref, *refs):
    (*parts, out_ref, values, written) = refs
    half = values.shape[1] // 2
    tile = half // 3
    ids = ids_ref[...]
    tokens = ids.shape[1]
    share = jnp.sum(jnp.where(ids == 0, gates_ref[...], 0.0), axis=0, keepdims=True)
    share = jnp.broadcast_to(share, (tokens, tokens)).T[:, :1]
    choosers = choose(ids)
    copies = []
    for step in range(3):
        here = slice(step * tile, (step + 1) * tile)
        rows = sum(part[:, here].astype(F32) for part in parts).astype(BF16)
        for side, chooser in enumerate(choosers):
            picked = lax.dot_general(
                chooser, rows, (((0,), (0,)), ((), ())), preferred_element_type=F32
            )
            start = side * half + step * tile
            there = slice(start, start + tile)
            values[:, there] = (share * picked).astype(BF16)
            copies.append(
                pltpu.make_async_copy(
                    values.at[:, there], out_ref.at[:, there], written.at[2 * step + side]
                )
            )
            copies[-1].start()
    for copy in copies:
        copy.wait()


def call(kernel, out_shape, *args, scratch=(), flops=0, **specs):
    moved = sum(a.size * a.dtype.itemsize for a in args)
    return pl.pallas_call(
        kernel,
        out_shape=out_shape,
        scratch_shapes=list(scratch),
        compiler_params=pltpu.CompilerParams(vmem_limit_bytes=16 * MIB),
        cost_estimate=pl.CostEstimate(flops=flops, bytes_accessed=moved, transcendentals=0),
        **specs,
    )(*args)


def body(size, tokens, expert_ids, gates, gate_weight, up_weight, down_weight):
    count, width = tokens.shape
    half = width // 2
    units = gate_weight.shape[0]
    chips = size // 2
    reach = chips // 2
    rows = size * CAP
    steps = permutations(size)

    def move(kind, a):
        return lax.ppermute(a.astype(BF16), "tensor", steps[kind])

    struct = jax.ShapeDtypeStruct
    ids = expert_ids.T
    work = 2 * rows * units * width
    own = call(compact_kernel, struct((PAIR, half), BF16), ids, tokens, flops=20 * work)

    like, cross = [own], [None]
    for distance in range(1, reach):
        cross.append(move("board", own) if distance == 1 else move("one", cross[-1]))
        if distance % 2 == 0:
            like.append(move("two", like[distance - 2]))
        else:
            like.append(move("one", like[distance - 1]))
    like.append(move("two", like[reach - 2]))
    cross[0] = move("swap", own)
    cross.append(move("swap", like[reach]))
    ahead_like = [None] + [move("swap", a) for a in cross[1:reach]]
    ahead_cross = [None] + [move("swap", a) for a in like[1:reach]]

    names, blocks = {}, []
    for distance in range(reach, -1, -1):
        for kind, found in (("like", like), ("cross", cross)):
            names["behind", kind, distance] = len(blocks)
            blocks.append(found[distance])
    for distance in range(1, reach):
        for kind, found in (("like", ahead_like), ("cross", ahead_cross)):
            names["ahead", kind, distance] = len(blocks)
            blocks.append(found[distance])

    hidden = call(
        lambda *refs: hidden_kernel(len(blocks), *refs),
        struct((rows, units), BF16),
        *blocks,
        gate_weight,
        up_weight,
        scratch=[pltpu.VMEM((rows, half), BF16)] * 2,
        flops=2 * work,
    )

    away = range(reach - 1, 0, -1)
    kept = [("like", reach)] + [(kind, d) for d in away for kind in ("like", "cross")] + [("like", 0)]
    other = {"like": "cross", "cross": "like"}

    def index(kind, distance, side):
        side = "behind" if distance in (0, reach) else side
        return names[side, kind, distance]

    urgent = 3
    places = [
        [index(kind, d, "ahead") for kind, d in kept],
        [index(other[kind], d, "behind") for kind, d in kept[:urgent]],
        [index(other[kind], d, "behind") for kind, d in kept[urgent:]],
    ]
    keep, *sent = call(
        lambda *refs: down_kernel(places, *refs),
        [
            struct((len(indices) * PAIR, half), kind)
            for indices, kind in zip(places, (F32, BF16, BF16))
        ],
        hidden,
        down_weight,
        flops=work,
    )
    sent = [move("swap", a) for a in sent]

    def part(a, k):
        return a[k * PAIR : (k + 1) * PAIR]

    def chip_sum(kind, distance):
        k = kept.index((kind, distance))
        theirs = part(sent[0], k) if k < urgent else part(sent[1], k - urgent)
        return part(keep, k) + theirs.astype(F32)

    far, last_like, last_cross = lax.optimization_barrier(
        tuple(
            chip_sum(*name).astype(BF16)
            for name in (("like", reach), ("like", reach - 1), ("cross", reach - 1))
        )
    )
    like_sums = {d: chip_sum("like", d) for d in range(1, reach - 1)} | {reach - 1: last_like}
    like_sums[reach - 2] += move("two", far).astype(F32)
    cross_sum = last_cross
    arrived = []
    for distance in away:
        if distance > 1:
            cross_sum = move("one", cross_sum).astype(F32) + chip_sum("cross", distance - 1)
        else:
            arrived.append(move("leave", cross_sum))
        length = 2 - distance % 2
        came = move("two" if length == 2 else "one", like_sums[distance])
        if distance == length:
            arrived.append(came)
        else:
            like_sums[distance - length] += came.astype(F32)
    return call(
        mix_kernel,
        struct(tokens.shape, BF16),
        ids,
        gates.T,
        *arrived,
        part(keep, len(kept) - 1),
        part(sent[1], len(kept) - 1 - urgent),
        out_specs=pl.BlockSpec(memory_space=pl.ANY),
        scratch=[pltpu.VMEM(tokens.shape, BF16), pltpu.SemaphoreType.DMA((6,))],
    )


def solution(mesh):
    size = mesh.shape["tensor"]
    tokens = P(("groups", "tensor"), None)
    weights = P("tensor", None)
    return jax.shard_map(
        lambda *args: body(size, *args),
        mesh=mesh,
        in_specs=(tokens, tokens, tokens, weights, weights, weights),
        out_specs=tokens,
        check_vma=False,
    )
```

time: 307 us -> 56.7 us (0.18)
  waiting for transfers between devices: 220 us -> 19.2 us
  local copies, waits for them, and re-layouts: 28.8 us -> 2.7 us
  matrix products: 24.3 us -> 0 us
  starting transfers between devices: 7.64 us -> 24.8 us
  between operations: 13.5 us -> 0.13 us
  blocking collectives: 12.1 us -> 0 us
  Pallas kernels: 0 us -> 9.35 us
    all_gather x2 -> x0, waiting for transfers between devices: 220 us -> none  [the longest x1 141 us: body(): block_rows = lax.all_gather(slot_rows, 'tensor', axis=0, tiled=True)]
    ppermute x0 -> x24, starting transfers between devices: none -> 24.8 us  [move(): return lax.ppermute(a.astype(BF16), 'tensor', steps[kind])]
    dot_general x5 -> x0, matrix products: 24.3 us -> none  [the longest x1 6.92 us: body(): lax.dot_general(block_rows, gate_weight, contract, preferred_element_type...]
    ppermute x0 -> x24, waiting for transfers between devices: none -> 19.2 us  [move(): return lax.ppermute(a.astype(BF16), 'tensor', steps[kind])]
    all_to_all x1 -> x0, blocking collectives: 12.1 us -> none  [body(): lax.all_to_all(partial_value.astype(jnp.bfloat16), 'tensor', split_axis=0...]
    unnamed x12 -> x18, local copies, waits for them, and re-layouts: 14 us -> 2.69 us
    pallas_call x0 -> x4, Pallas kernels: none -> 9.35 us  [call(): pl.pallas_call(kernel, out_shape=out_shape, scratch_shapes=list(scratch),...]
    all_to_all x1 -> x0, starting transfers between devices: 7.56 us -> none  [body(): lax.all_to_all(down_weight, 'tensor', split_axis=1, concat_axis=0, tiled=...]
  transfers between devices with their start and end apart: 3 -> 24, of which waited for: 2 -> 15; matrix products, arithmetic and copies ran while one was open for 12% -> 0% of each run, Pallas kernels for 0% -> 0%
where the time goes in v5:
time: 56.7 us; the launch traced here: 56.5 us
  starting transfers between devices  24.8 us (44%)
  waiting for transfers between devices  19.2 us (34%)
  Pallas kernels  9.35 us (16%)
  local copies, waits for them, and re-layouts  2.7 us (5%)
    ppermute x24, starting transfers between devices, move(): return lax.ppermute(a.astype(BF16), 'tensor', steps[kind])  24.8 us
    ppermute x24, waiting for transfers between devices, move(): return lax.ppermute(a.astype(BF16), 'tensor', steps[kind])  19.2 us
    pallas_call x4, Pallas kernels, call(): pl.pallas_call(kernel, out_shape=out_shape, scratch_shapes=list(scratch),...  9.35 us
    unnamed x18, local copies, waits for them, and re-layouts  2.69 us
  transfers between devices with their start and end apart: 24, of which 15 were waited for; matrix products, arithmetic and copies ran while one was open for 0% of the time, Pallas kernels for 0%

profile of v5, /device:TPU:0, one launch (start us, length us, event | category | flops | bytes accessed | tf_op | source)
XLA Modules:
  0.0 56.5 jit_solution(5101051996583456920)
XLA Ops:
  0.8 1.8 %copy-done.4 = bf16[128,6144]{1,0:T(8,128)(2,1)S(1)} copy-done((bf16[128,6144]{1,0:T(8,128)(2,1)S(1)}, bf16[128,6144]{1,0:T(8,128)(2,1)}, u32[]{:S(2)}) %copy-start.4) | copy-done | bytes 1572888
  3.1 2.5 %collective-permute-start.4 = (bf16[24,3072]{1,0:T(8,128)(2,1)S(1)}, bf16[24,3072]{1,0:T(8,128)(2,1)S(1)}, u32[]{:S(2)}, u32[]{:S(2)}) collective-permute-start(bf16[24,3072]{1,0:T(8,128)(2,1)S(1)} %shard_map.64.refs_8_), channel_id=1, source_target_pairs={{0,3},{1,4},{4,1},{5,8},{8,5},{9,12},{12,9},{13,14},{14,13},{15,10... | collective-permute-start | bytes 442376 | tf_op jit(solution)/shard_map/ppermute | solution.py:160
  5.6 1.7 %collective-permute-start = (bf16[24,3072]{1,0:T(8,128)(2,1)S(1)}, bf16[24,3072]{1,0:T(8,128)(2,1)S(1)}, u32[]{:S(2)}, u32[]{:S(2)}) collective-permute-start(bf16[24,3072]{1,0:T(8,128)(2,1)S(1)} %shard_map.64.refs_8_), channel_id=1, source_target_pairs={{0,8},{1,7},{4,12},{5,3},{8,14},{9,1},{12,10},{13,5},{14,6},{15,9}... | collective-permute-start | bytes 442376 | tf_op jit(solution)/shard_map/ppermute | solution.py:160
  7.3 1.6 %collective-permute-start.7 = (bf16[24,3072]{1,0:T(8,128)(2,1)S(1)}, bf16[24,3072]{1,0:T(8,128)(2,1)S(1)}, u32[]{:S(2)}, u32[]{:S(2)}) collective-permute-start(bf16[24,3072]{1,0:T(8,128)(2,1)S(1)} %shard_map.64.refs_8_), channel_id=1, source_target_pairs={{0,4},{1,3},{4,8},{5,1},{8,12},{9,5},{12,14},{13,9},{14,10},{15,13... | collective-permute-start | bytes 442376 | tf_op jit(solution)/shard_map/ppermute | solution.py:160
  8.9 1.9 %collective-permute-start.5 = (bf16[24,3072]{1,0:T(8,128)(2,1)S(1)}, bf16[24,3072]{1,0:T(8,128)(2,1)S(1)}, u32[]{:S(2)}, u32[]{:S(2)}) collective-permute-start(bf16[24,3072]{1,0:T(8,128)(2,1)S(1)} %collective-permute-done.4.refs_7_), channel_id=1, source_target_pairs={{0,4},{1,3},{4,8},{5,1},{8,12},{9,5},{12,14},{13,9},{14,10},{15,13... | collective-permute-start | bytes 442376 | tf_op jit(solution)/shard_map/ppermute | solution.py:160
  10.8 2.5 %collective-permute-done.refs_4_ = bf16[24,3072]{1,0:T(8,128)(2,1)S(1)} collective-permute-done((bf16[24,3072]{1,0:T(8,128)(2,1)S(1)}, bf16[24,3072]{1,0:T(8,128)(2,1)S(1)}, u32[]{:S(2)}, u32[]{:S(2)}) %collective-permute-start) | collective-permute-done | bytes 147488 | tf_op jit(solution)/shard_map/ppermute | solution.py:160
  13.3 2.0 %collective-permute-start.3 = (bf16[24,3072]{1,0:T(8,128)(2,1)S(1)}, bf16[24,3072]{1,0:T(8,128)(2,1)S(1)}, u32[]{:S(2)}, u32[]{:S(2)}) collective-permute-start(bf16[24,3072]{1,0:T(8,128)(2,1)S(1)} %collective-permute-done.refs_4_), channel_id=1, source_target_pairs={{0,4},{1,3},{4,8},{5,1},{8,12},{9,5},{12,14},{13,9},{14,10},{15,13... | collective-permute-start | bytes 442376 | tf_op jit(solution)/shard_map/ppermute | solution.py:160
  15.3 1.2 %collective-permute-start.1 = (bf16[24,3072]{1,0:T(8,128)(2,1)S(1)}, bf16[24,3072]{1,0:T(8,128)(2,1)S(1)}, u32[]{:S(2)}, u32[]{:S(2)}) collective-permute-start(bf16[24,3072]{1,0:T(8,128)(2,1)S(1)} %collective-permute-done.refs_4_), channel_id=1, source_target_pairs={{0,8},{1,7},{4,12},{5,3},{8,14},{9,1},{12,10},{13,5},{14,6},{15,9}... | collective-permute-start | bytes 442376 | tf_op jit(solution)/shard_map/ppermute | solution.py:160
  17.0 1.5 %collective-permute-start.6 = (bf16[24,3072]{1,0:T(8,128)(2,1)S(1)}, bf16[24,3072]{1,0:T(8,128)(2,1)S(1)}, u32[]{:S(2)}, u32[]{:S(2)}) collective-permute-start(bf16[24,3072]{1,0:T(8,128)(2,1)S(1)} %collective-permute-done.5.refs_5_), channel_id=1, source_target_pairs={{0,4},{1,3},{4,8},{5,1},{8,12},{9,5},{12,14},{13,9},{14,10},{15,13... | collective-permute-start | bytes 442376 | tf_op jit(solution)/shard_map/ppermute | solution.py:160
  19.1 3.8 %collective-permute-done.1.refs_0_ = bf16[24,3072]{1,0:T(8,128)(2,1)S(1)} collective-permute-done((bf16[24,3072]{1,0:T(8,128)(2,1)S(1)}, bf16[24,3072]{1,0:T(8,128)(2,1)S(1)}, u32[]{:S(2)}, u32[]{:S(2)}) %collective-permute-start.1) | collective-permute-done | bytes 147488 | tf_op jit(solution)/shard_map/ppermute | solution.py:160
  25.1 5.3 %shard_map.65.refs_0_ = bf16[192,672]{1,0:T(8,128)(2,1)S(1)} custom-call(bf16[24,3072]{1,0:T(8,128)(2,1)S(1)} %collective-permute-done.1.refs_0_, bf16[24,3072]{1,0:T(8,128)(2,1)S(1)} %collective-permute-done.2.refs_1_, bf16[24,3072]{1,0:T(8,128)(2,1)S(1)} %collective-permute-done.3.refs_2_, bf16[24,3072]{1,0:T(8,128)(2,1)S(1)} %collective-permute-done.6.refs_3_, ...), custom_call_target="tpu_custom_call" | custom-call | flops 3170893824 | bytes 18874368 | tf_op jit(solution)/shard_map/pallas_call | solution.py:140
  30.4 2.0 %shard_map.66 = (f32[192,3072]{1,0:T(8,128)S(1)}, bf16[72,3072]{1,0:T(8,128)(2,1)S(1)}, bf16[120,3072]{1,0:T(8,128)(2,1)S(1)}) custom-call(bf16[192,672]{1,0:T(8,128)(2,1)S(1)} %shard_map.65.refs_0_, bf16[672,6144]{1,0:T(8,128)(2,1)S(1)} %copy-done), custom_call_target="tpu_custom_call" | custom-call | flops 1585446912 | bytes 8515584 | tf_op jit(solution)/shard_map/pallas_call | solution.py:140
  33.0 1.3 %collective-permute-done.16 = bf16[72,3072]{1,0:T(8,128)(2,1)S(1)} collective-permute-done((bf16[72,3072]{1,0:T(8,128)(2,1)S(1)}, bf16[72,3072]{1,0:T(8,128)(2,1)S(1)}, u32[]{:S(2)}, u32[]{:S(2)}) %collective-permute-start.16) | collective-permute-done | bytes 442400 | tf_op jit(solution)/shard_map/ppermute | solution.py:160
  34.4 1.2 %collective-permute-start.20 = (bf16[24,3072]{1,0:T(8,128)(2,1)S(1)}, bf16[24,3072]{1,0:T(8,128)(2,1)S(1)}, u32[]{:S(2)}, u32[]{:S(2)}) collective-permute-start(bf16[24,3072]{1,0:T(8,128)(2,1)S(1)} %get-tuple-element.16), channel_id=1, source_target_pairs={{0,4},{1,3},{4,8},{5,1},{8,12},{9,5},{12,14},{13,9},{14,10},{15,13... | collective-permute-start | bytes 442376 | tf_op jit(solution)/shard_map/ppermute | solution.py:160
  35.5 2.4 %collective-permute-start.17 = (bf16[24,3072]{1,0:T(8,128)(2,1)S(1)}, bf16[24,3072]{1,0:T(8,128)(2,1)S(1)}, u32[]{:S(2)}, u32[]{:S(2)}) collective-permute-start(bf16[24,3072]{1,0:T(8,128)(2,1)S(1)} %get-tuple-element.14), channel_id=1, source_target_pairs={{0,8},{1,7},{4,12},{5,3},{8,14},{9,1},{12,10},{13,5},{14,6},{15,9}... | collective-permute-start | bytes 442376 | tf_op jit(solution)/shard_map/ppermute | solution.py:160
  38.5 1.1 %collective-permute-done.20 = bf16[24,3072]{1,0:T(8,128)(2,1)S(1)} collective-permute-done((bf16[24,3072]{1,0:T(8,128)(2,1)S(1)}, bf16[24,3072]{1,0:T(8,128)(2,1)S(1)}, u32[]{:S(2)}, u32[]{:S(2)}) %collective-permute-start.20) | collective-permute-done | bytes 147488 | tf_op jit(solution)/shard_map/ppermute | solution.py:160
  39.6 2.2 %collective-permute-start.21 = (bf16[24,3072]{1,0:T(8,128)(2,1)S(1)}, bf16[24,3072]{1,0:T(8,128)(2,1)S(1)}, u32[]{:S(2)}, u32[]{:S(2)}) collective-permute-start(bf16[24,3072]{1,0:T(8,128)(2,1)S(1)} %add_convert_fusion.2), channel_id=1, source_target_pairs={{0,4},{1,3},{4,8},{5,1},{8,12},{9,5},{12,14},{13,9},{14,10},{15,13... | collective-permute-start | bytes 442376 | tf_op jit(solution)/shard_map/ppermute | solution.py:160
  41.8 1.8 %collective-permute-done.17 = bf16[24,3072]{1,0:T(8,128)(2,1)S(1)} collective-permute-done((bf16[24,3072]{1,0:T(8,128)(2,1)S(1)}, bf16[24,3072]{1,0:T(8,128)(2,1)S(1)}, u32[]{:S(2)}, u32[]{:S(2)}) %collective-permute-start.17) | collective-permute-done | bytes 147488 | tf_op jit(solution)/shard_map/ppermute | solution.py:160
  43.9 1.6 %collective-permute-done.21 = bf16[24,3072]{1,0:T(8,128)(2,1)S(1)} collective-permute-done((bf16[24,3072]{1,0:T(8,128)(2,1)S(1)}, bf16[24,3072]{1,0:T(8,128)(2,1)S(1)}, u32[]{:S(2)}, u32[]{:S(2)}) %collective-permute-start.21) | collective-permute-done | bytes 147488 | tf_op jit(solution)/shard_map/ppermute | solution.py:160
  45.6 2.6 %collective-permute-start.19 = (bf16[24,3072]{1,0:T(8,128)(2,1)S(1)}, bf16[24,3072]{1,0:T(8,128)(2,1)S(1)}, u32[]{:S(2)}, u32[]{:S(2)}) collective-permute-start(bf16[24,3072]{1,0:T(8,128)(2,1)S(1)} %get-tuple-element.19), channel_id=1, source_target_pairs={{0,8},{1,7},{4,12},{5,3},{8,14},{9,1},{12,10},{13,5},{14,6},{15,9}... | collective-permute-start | bytes 442376 | tf_op jit(solution)/shard_map/ppermute | solution.py:160
  48.2 1.4 %collective-permute-start.23 = (bf16[24,3072]{1,0:T(8,128)(2,1)S(1)}, bf16[24,3072]{1,0:T(8,128)(2,1)S(1)}, u32[]{:S(2)}, u32[]{:S(2)}) collective-permute-start(bf16[24,3072]{1,0:T(8,128)(2,1)S(1)} %get-tuple-element.17), channel_id=1, source_target_pairs={{0,4},{1,3},{4,8},{5,1},{8,12},{9,5},{12,14},{13,9},{14,10},{15,13... | collective-permute-start | bytes 442376 | tf_op jit(solution)/shard_map/ppermute | solution.py:160
  49.7 3.0 %collective-permute-done.19.refs_0_ = bf16[24,3072]{1,0:T(8,128)(2,1)S(1)} collective-permute-done((bf16[24,3072]{1,0:T(8,128)(2,1)S(1)}, bf16[24,3072]{1,0:T(8,128)(2,1)S(1)}, u32[]{:S(2)}, u32[]{:S(2)}) %collective-permute-start.19) | collective-permute-done | bytes 147488 | tf_op jit(solution)/shard_map/ppermute | solution.py:160
  52.7 1.2 %collective-permute-done.22.refs_1_ = bf16[24,3072]{1,0:T(8,128)(2,1)S(1)} collective-permute-done((bf16[24,3072]{1,0:T(8,128)(2,1)S(1)}, bf16[24,3072]{1,0:T(8,128)(2,1)S(1)}, u32[]{:S(2)}, u32[]{:S(2)}) %collective-permute-start.22) | collective-permute-done | bytes 147488 | tf_op jit(solution)/shard_map/ppermute | solution.py:160
  54.9 1.6 %shard_map.67 = bf16[128,6144]{1,0:T(8,128)(2,1)} custom-call(s32[4,128]{1,0:T(4,128)S(1)} %bitcast.7, f32[4,128]{1,0:T(4,128)S(1)} %bitcast.8, bf16[24,3072]{1,0:T(8,128)(2,1)S(1)} %collective-permute-done.19.refs_0_, bf16[24,3072]{1,0:T(8,128)(2,1)S(1)} %collective-permute-done.22.refs_1_, bf16[24,3072]{1,0:T(8,128)(2,1)S(1)} %collective-permute-done.23.refs_2_, ...), custom_call_target="tpu_custom_call" | custom-call | bytes 888832 | tf_op jit(solution)/shard_map/pallas_call | solution.py:140
  (52 shorter events, 7.1 us)
Async XLA Ops:
  3.1 5.7 %collective-permute-start.4 = (bf16[24,3072]{1,0:T(8,128)(2,1)S(1)}, bf16[24,3072]{1,0:T(8,128)(2,1)S(1)}, u32[]{:S(2)}, u32[]{:S(2)}) collective-permute-start(bf16[24,3072]{1,0:T(8,128)(2,1)S(1)} %shard_map.64.refs_8_), channel_id=1, source_target_pairs={{0,3},{1,4},{4,1},{5,8},{8,5},{9,12},{12,9},{13,14},{14,13},{15,10... | collective-permute-start | bytes 442376 | tf_op jit(solution)/shard_map/ppermute | solution.py:160
  5.6 7.7 %collective-permute-start = (bf16[24,3072]{1,0:T(8,128)(2,1)S(1)}, bf16[24,3072]{1,0:T(8,128)(2,1)S(1)}, u32[]{:S(2)}, u32[]{:S(2)}) collective-permute-start(bf16[24,3072]{1,0:T(8,128)(2,1)S(1)} %shard_map.64.refs_8_), channel_id=1, source_target_pairs={{0,8},{1,7},{4,12},{5,3},{8,14},{9,1},{12,10},{13,5},{14,6},{15,9}... | collective-permute-start | bytes 442376 | tf_op jit(solution)/shard_map/ppermute | solution.py:160
  7.3 9.2 %collective-permute-start.7 = (bf16[24,3072]{1,0:T(8,128)(2,1)S(1)}, bf16[24,3072]{1,0:T(8,128)(2,1)S(1)}, u32[]{:S(2)}, u32[]{:S(2)}) collective-permute-start(bf16[24,3072]{1,0:T(8,128)(2,1)S(1)} %shard_map.64.refs_8_), channel_id=1, source_target_pairs={{0,4},{1,3},{4,8},{5,1},{8,12},{9,5},{12,14},{13,9},{14,10},{15,13... | collective-permute-start | bytes 442376 | tf_op jit(solution)/shard_map/ppermute | solution.py:160
  8.9 7.6 %collective-permute-start.8 = (bf16[24,3072]{1,0:T(8,128)(2,1)S(1)}, bf16[24,3072]{1,0:T(8,128)(2,1)S(1)}, u32[]{:S(2)}, u32[]{:S(2)}) collective-permute-start(bf16[24,3072]{1,0:T(8,128)(2,1)S(1)} %shard_map.64.refs_8_), channel_id=1, source_target_pairs={{0,1},{1,0},{4,5},{5,4},{8,9},{9,8},{12,13},{13,12},{14,15},{15,14... | collective-permute-start | bytes 442376 | tf_op jit(solution)/shard_map/ppermute | solution.py:160
  8.9 8.1 %collective-permute-start.5 = (bf16[24,3072]{1,0:T(8,128)(2,1)S(1)}, bf16[24,3072]{1,0:T(8,128)(2,1)S(1)}, u32[]{:S(2)}, u32[]{:S(2)}) collective-permute-start(bf16[24,3072]{1,0:T(8,128)(2,1)S(1)} %collective-permute-done.4.refs_7_), channel_id=1, source_target_pairs={{0,4},{1,3},{4,8},{5,1},{8,12},{9,5},{12,14},{13,9},{14,10},{15,13... | collective-permute-start | bytes 442376 | tf_op jit(solution)/shard_map/ppermute | solution.py:160
  13.3 5.8 %collective-permute-start.3 = (bf16[24,3072]{1,0:T(8,128)(2,1)S(1)}, bf16[24,3072]{1,0:T(8,128)(2,1)S(1)}, u32[]{:S(2)}, u32[]{:S(2)}) collective-permute-start(bf16[24,3072]{1,0:T(8,128)(2,1)S(1)} %collective-permute-done.refs_4_), channel_id=1, source_target_pairs={{0,4},{1,3},{4,8},{5,1},{8,12},{9,5},{12,14},{13,9},{14,10},{15,13... | collective-permute-start | bytes 442376 | tf_op jit(solution)/shard_map/ppermute | solution.py:160
  15.3 7.6 %collective-permute-start.1 = (bf16[24,3072]{1,0:T(8,128)(2,1)S(1)}, bf16[24,3072]{1,0:T(8,128)(2,1)S(1)}, u32[]{:S(2)}, u32[]{:S(2)}) collective-permute-start(bf16[24,3072]{1,0:T(8,128)(2,1)S(1)} %collective-permute-done.refs_4_), channel_id=1, source_target_pairs={{0,8},{1,7},{4,12},{5,3},{8,14},{9,1},{12,10},{13,5},{14,6},{15,9}... | collective-permute-start | bytes 442376 | tf_op jit(solution)/shard_map/ppermute | solution.py:160
  16.5 6.5 %collective-permute-start.12 = (bf16[24,3072]{1,0:T(8,128)(2,1)S(1)}, bf16[24,3072]{1,0:T(8,128)(2,1)S(1)}, u32[]{:S(2)}, u32[]{:S(2)}) collective-permute-start(bf16[24,3072]{1,0:T(8,128)(2,1)S(1)} %collective-permute-done.refs_4_), channel_id=1, source_target_pairs={{0,1},{1,0},{4,5},{5,4},{8,9},{9,8},{12,13},{13,12},{14,15},{15,14... | collective-permute-start | bytes 442376 | tf_op jit(solution)/shard_map/ppermute | solution.py:160
  16.5 7.0 %collective-permute-start.9 = (bf16[24,3072]{1,0:T(8,128)(2,1)S(1)}, bf16[24,3072]{1,0:T(8,128)(2,1)S(1)}, u32[]{:S(2)}, u32[]{:S(2)}) collective-permute-start(bf16[24,3072]{1,0:T(8,128)(2,1)S(1)} %collective-permute-done.4.refs_7_), channel_id=1, source_target_pairs={{0,1},{1,0},{4,5},{5,4},{8,9},{9,8},{12,13},{13,12},{14,15},{15,14... | collective-permute-start | bytes 442376 | tf_op jit(solution)/shard_map/ppermute | solution.py:160
  17.0 6.5 %collective-permute-start.6 = (bf16[24,3072]{1,0:T(8,128)(2,1)S(1)}, bf16[24,3072]{1,0:T(8,128)(2,1)S(1)}, u32[]{:S(2)}, u32[]{:S(2)}) collective-permute-start(bf16[24,3072]{1,0:T(8,128)(2,1)S(1)} %collective-permute-done.5.refs_5_), channel_id=1, source_target_pairs={{0,4},{1,3},{4,8},{5,1},{8,12},{9,5},{12,14},{13,9},{14,10},{15,13... | collective-permute-start | bytes 442376 | tf_op jit(solution)/shard_map/ppermute | solution.py:160
  19.1 4.9 %collective-permute-start.10 = (bf16[24,3072]{1,0:T(8,128)(2,1)S(1)}, bf16[24,3072]{1,0:T(8,128)(2,1)S(1)}, u32[]{:S(2)}, u32[]{:S(2)}) collective-permute-start(bf16[24,3072]{1,0:T(8,128)(2,1)S(1)} %collective-permute-done.7.refs_6_), channel_id=1, source_target_pairs={{0,1},{1,0},{4,5},{5,4},{8,9},{9,8},{12,13},{13,12},{14,15},{15,14... | collective-permute-start | bytes 442376 | tf_op jit(solution)/shard_map/ppermute | solution.py:160
  22.9 1.4 %collective-permute-start.11 = (bf16[24,3072]{1,0:T(8,128)(2,1)S(1)}, bf16[24,3072]{1,0:T(8,128)(2,1)S(1)}, u32[]{:S(2)}, u32[]{:S(2)}) collective-permute-start(bf16[24,3072]{1,0:T(8,128)(2,1)S(1)} %collective-permute-done.5.refs_5_), channel_id=1, source_target_pairs={{0,1},{1,0},{4,5},{5,4},{8,9},{9,8},{12,13},{13,12},{14,15},{15,14... | collective-permute-start | bytes 442376 | tf_op jit(solution)/shard_map/ppermute | solution.py:160
  22.9 1.6 %collective-permute-start.14 = (bf16[24,3072]{1,0:T(8,128)(2,1)S(1)}, bf16[24,3072]{1,0:T(8,128)(2,1)S(1)}, u32[]{:S(2)}, u32[]{:S(2)}) collective-permute-start(bf16[24,3072]{1,0:T(8,128)(2,1)S(1)} %collective-permute-done.3.refs_2_), channel_id=1, source_target_pairs={{0,1},{1,0},{4,5},{5,4},{8,9},{9,8},{12,13},{13,12},{14,15},{15,14... | collective-permute-start | bytes 442376 | tf_op jit(solution)/shard_map/ppermute | solution.py:160
  23.5 1.4 %collective-permute-start.2 = (bf16[24,3072]{1,0:T(8,128)(2,1)S(1)}, bf16[24,3072]{1,0:T(8,128)(2,1)S(1)}, u32[]{:S(2)}, u32[]{:S(2)}) collective-permute-start(bf16[24,3072]{1,0:T(8,128)(2,1)S(1)} %collective-permute-done.1.refs_0_), channel_id=1, source_target_pairs={{0,1},{1,0},{4,5},{5,4},{8,9},{9,8},{12,13},{13,12},{14,15},{15,14... | collective-permute-start | bytes 442376 | tf_op jit(solution)/shard_map/ppermute | solution.py:160
  23.5 1.5 %collective-permute-start.13 = (bf16[24,3072]{1,0:T(8,128)(2,1)S(1)}, bf16[24,3072]{1,0:T(8,128)(2,1)S(1)}, u32[]{:S(2)}, u32[]{:S(2)}) collective-permute-start(bf16[24,3072]{1,0:T(8,128)(2,1)S(1)} %collective-permute-done.6.refs_3_), channel_id=1, source_target_pairs={{0,1},{1,0},{4,5},{5,4},{8,9},{9,8},{12,13},{13,12},{14,15},{15,14... | collective-permute-start | bytes 442376 | tf_op jit(solution)/shard_map/ppermute | solution.py:160
  32.4 1.9 %collective-permute-start.16 = (bf16[72,3072]{1,0:T(8,128)(2,1)S(1)}, bf16[72,3072]{1,0:T(8,128)(2,1)S(1)}, u32[]{:S(2)}, u32[]{:S(2)}) collective-permute-start(bf16[72,3072]{1,0:T(8,128)(2,1)S(1)} %get-tuple-element.13), channel_id=1, source_target_pairs={{0,1},{1,0},{4,5},{5,4},{8,9},{9,8},{12,13},{13,12},{14,15},{15,14... | collective-permute-start | bytes 1327112 | tf_op jit(solution)/shard_map/ppermute | solution.py:160
  32.8 6.8 %collective-permute-start.15 = (bf16[120,3072]{1,0:T(8,128)(2,1)S(1)}, bf16[120,3072]{1,0:T(8,128)(2,1)S(1)}, u32[]{:S(2)}, u32[]{:S(2)}) collective-permute-start(bf16[120,3072]{1,0:T(8,128)(2,1)S(1)} %get-tuple-element.12), channel_id=1, source_target_pairs={{0,1},{1,0},{4,5},{5,4},{8,9},{9,8},{12,13},{13,12},{14,15},{15,14... | collective-permute-start | bytes 2211848 | tf_op jit(solution)/shard_map/ppermute | solution.py:160
  34.4 5.2 %collective-permute-start.20 = (bf16[24,3072]{1,0:T(8,128)(2,1)S(1)}, bf16[24,3072]{1,0:T(8,128)(2,1)S(1)}, u32[]{:S(2)}, u32[]{:S(2)}) collective-permute-start(bf16[24,3072]{1,0:T(8,128)(2,1)S(1)} %get-tuple-element.16), channel_id=1, source_target_pairs={{0,4},{1,3},{4,8},{5,1},{8,12},{9,5},{12,14},{13,9},{14,10},{15,13... | collective-permute-start | bytes 442376 | tf_op jit(solution)/shard_map/ppermute | solution.py:160
  35.5 8.1 %collective-permute-start.17 = (bf16[24,3072]{1,0:T(8,128)(2,1)S(1)}, bf16[24,3072]{1,0:T(8,128)(2,1)S(1)}, u32[]{:S(2)}, u32[]{:S(2)}) collective-permute-start(bf16[24,3072]{1,0:T(8,128)(2,1)S(1)} %get-tuple-element.14), channel_id=1, source_target_pairs={{0,8},{1,7},{4,12},{5,3},{8,14},{9,1},{12,10},{13,5},{14,6},{15,9}... | collective-permute-start | bytes 442376 | tf_op jit(solution)/shard_map/ppermute | solution.py:160
  38.0 5.9 %collective-permute-start.18 = (bf16[24,3072]{1,0:T(8,128)(2,1)S(1)}, bf16[24,3072]{1,0:T(8,128)(2,1)S(1)}, u32[]{:S(2)}, u32[]{:S(2)}) collective-permute-start(bf16[24,3072]{1,0:T(8,128)(2,1)S(1)} %get-tuple-element.15), channel_id=1, source_target_pairs={{0,4},{1,3},{4,8},{5,1},{8,12},{9,5},{12,14},{13,9},{14,10},{15,13... | collective-permute-start | bytes 442376 | tf_op jit(solution)/shard_map/ppermute | solution.py:160
  39.6 5.8 %collective-permute-start.21 = (bf16[24,3072]{1,0:T(8,128)(2,1)S(1)}, bf16[24,3072]{1,0:T(8,128)(2,1)S(1)}, u32[]{:S(2)}, u32[]{:S(2)}) collective-permute-start(bf16[24,3072]{1,0:T(8,128)(2,1)S(1)} %add_convert_fusion.2), channel_id=1, source_target_pairs={{0,4},{1,3},{4,8},{5,1},{8,12},{9,5},{12,14},{13,9},{14,10},{15,13... | collective-permute-start | bytes 442376 | tf_op jit(solution)/shard_map/ppermute | solution.py:160
  45.6 7.1 %collective-permute-start.19 = (bf16[24,3072]{1,0:T(8,128)(2,1)S(1)}, bf16[24,3072]{1,0:T(8,128)(2,1)S(1)}, u32[]{:S(2)}, u32[]{:S(2)}) collective-permute-start(bf16[24,3072]{1,0:T(8,128)(2,1)S(1)} %get-tuple-element.19), channel_id=1, source_target_pairs={{0,8},{1,7},{4,12},{5,3},{8,14},{9,1},{12,10},{13,5},{14,6},{15,9}... | collective-permute-start | bytes 442376 | tf_op jit(solution)/shard_map/ppermute | solution.py:160
  48.2 5.7 %collective-permute-start.22 = (bf16[24,3072]{1,0:T(8,128)(2,1)S(1)}, bf16[24,3072]{1,0:T(8,128)(2,1)S(1)}, u32[]{:S(2)}, u32[]{:S(2)}) collective-permute-start(bf16[24,3072]{1,0:T(8,128)(2,1)S(1)} %get-tuple-element.18), channel_id=1, source_target_pairs={{0,5},{1,2},{4,9},{5,0},{8,13},{9,4},{12,15},{13,8},{14,11},{15,12... | collective-permute-start | bytes 442376 | tf_op jit(solution)/shard_map/ppermute | solution.py:160
  48.2 6.6 %collective-permute-start.23 = (bf16[24,3072]{1,0:T(8,128)(2,1)S(1)}, bf16[24,3072]{1,0:T(8,128)(2,1)S(1)}, u32[]{:S(2)}, u32[]{:S(2)}) collective-permute-start(bf16[24,3072]{1,0:T(8,128)(2,1)S(1)} %get-tuple-element.17), channel_id=1, source_target_pairs={{0,4},{1,3},{4,8},{5,1},{8,12},{9,5},{12,14},{13,9},{14,10},{15,13... | collective-permute-start | bytes 442376 | tf_op jit(solution)/shard_map/ppermute | solution.py:160
  (9 other events, 143.8 us)

commit v6 on v5

--- a/solution.py
+++ b/solution.py
@@ -62,13 +62,17 @@
     ).astype(BF16)
 
 
-def hidden_kernel(count, *refs):
-    blocks, (gate_ref, up_ref, out_ref, first, second) = refs[:count], refs[count:]
+def copy_kernel(in_ref, out_ref):
+    out_ref[...] = in_ref[...]
+
+
+def hidden_kernel(blocks, *refs):
+    arrays, (gate_ref, up_ref, out_ref, first, second) = refs[:-5], refs[-5:]
     units, width = gate_ref.shape
     half = width // 2
-    for j, block in enumerate(blocks):
-        first[j * CAP : (j + 1) * CAP, :] = block[:CAP, :]
-        second[j * CAP : (j + 1) * CAP, :] = block[CAP:, :]
+    for j, (i, row) in enumerate(blocks):
+        first[j * CAP : (j + 1) * CAP, :] = arrays[i][row : row + CAP, :]
+        second[j * CAP : (j + 1) * CAP, :] = arrays[i][row + CAP : row + PAIR, :]
     contract = (((1,), (1,)), ((), ()))
 
     def product(ref, here):
@@ -105,8 +109,14 @@
                 ).astype(out_ref.dtype)
 
 
-def mix_kernel(ids_ref, gates_ref, *refs):
-    (*parts, out_ref, values, written) = refs
+def sum_kernel(blocks, *refs):
+    out_ref = refs[-1]
+    total = sum(refs[i][row : row + PAIR, :].astype(F32) for i, row in blocks)
+    out_ref[...] = total.astype(out_ref.dtype)
+
+
+def mix_kernel(blocks, ids_ref, gates_ref, *refs):
+    (*arrays, out_ref, values, written) = refs
     half = values.shape[1] // 2
     tile = half // 3
     ids = ids_ref[...]
@@ -117,7 +127,7 @@
     copies = []
     for step in range(3):
         here = slice(step * tile, (step + 1) * tile)
-        rows = sum(part[:, here].astype(F32) for part in parts).astype(BF16)
+        rows = sum(arrays[i][row : row + PAIR, here].astype(F32) for i, row in blocks).astype(BF16)
         for side, chooser in enumerate(choosers):
             picked = lax.dot_general(
                 chooser, rows, (((0,), (0,)), ((), ())), preferred_element_type=F32
@@ -147,6 +157,16 @@
     )(*args)
 
 
+def distinct(blocks):
+    arrays, where = [], []
+    for a, row in blocks:
+        i = next((i for i, known in enumerate(arrays) if known is a), len(arrays))
+        if i == len(arrays):
+            arrays.append(a)
+        where.append((i, row))
+    return arrays, where
+
+
 def body(size, tokens, expert_ids, gates, gate_weight, up_weight, down_weight):
     count, width = tokens.shape
     half = width // 2
@@ -162,35 +182,43 @@
     struct = jax.ShapeDtypeStruct
     ids = expert_ids.T
     work = 2 * rows * units * width
-    own = call(compact_kernel, struct((PAIR, half), BF16), ids, tokens, flops=20 * work)
-
-    like, cross = [own], [None]
-    for distance in range(1, reach):
-        cross.append(move("board", own) if distance == 1 else move("one", cross[-1]))
-        if distance % 2 == 0:
-            like.append(move("two", like[distance - 2]))
-        else:
-            like.append(move("one", like[distance - 1]))
-    like.append(move("two", like[reach - 2]))
-    cross[0] = move("swap", own)
-    cross.append(move("swap", like[reach]))
-    ahead_like = [None] + [move("swap", a) for a in cross[1:reach]]
-    ahead_cross = [None] + [move("swap", a) for a in like[1:reach]]
+    own = call(compact_kernel, struct((PAIR, half), BF16), ids, tokens)
+    own = call(copy_kernel, struct(own.shape, BF16), own, flops=20 * work)
+
+    def block(a, k=0):
+        return a, k * PAIR
+
+    def add(blocks):
+        arrays, where = distinct(blocks)
+        return call(lambda *refs: sum_kernel(where, *refs), struct((PAIR, half), BF16), *arrays)
+
+    behind = {("like", 0): own, ("cross", 0): move("swap", own)}
+    for distance in range(1, reach + 1):
+        if distance < reach:
+            source = behind["cross", distance - 1] if distance > 1 else own
+            behind["cross", distance] = move("one" if distance > 1 else "board", source)
+        length = 2 - distance % 2
+        behind["like", distance] = move("two" if length == 2 else "one", behind["like", distance - length])
+    behind["cross", reach] = move("swap", behind["like", reach])
+    other = {"like": "cross", "cross": "like"}
+    ahead = {
+        (other[kind], distance): move("swap", a)
+        for (kind, distance), a in behind.items()
+        if 0 < distance < reach
+    }
+    behind, ahead = ({name: block(a) for name, a in found.items()} for found in (behind, ahead))
 
     names, blocks = {}, []
-    for distance in range(reach, -1, -1):
-        for kind, found in (("like", like), ("cross", cross)):
-            names["behind", kind, distance] = len(blocks)
-            blocks.append(found[distance])
-    for distance in range(1, reach):
-        for kind, found in (("like", ahead_like), ("cross", ahead_cross)):
-            names["ahead", kind, distance] = len(blocks)
-            blocks.append(found[distance])
-
+    for side, found in (("behind", behind), ("ahead", ahead)):
+        for kind, distance in found:
+            names[side, kind, distance] = len(blocks)
+            blocks.append(found[kind, distance])
+
+    arrays, where = distinct(blocks)
     hidden = call(
-        lambda *refs: hidden_kernel(len(blocks), *refs),
+        lambda *refs: hidden_kernel(where, *refs),
         struct((rows, units), BF16),
-        *blocks,
+        *arrays,
         gate_weight,
         up_weight,
         scratch=[pltpu.VMEM((rows, half), BF16)] * 2,
@@ -199,8 +227,6 @@
 
     away = range(reach - 1, 0, -1)
     kept = [("like", reach)] + [(kind, d) for d in away for kind in ("like", "cross")] + [("like", 0)]
-    other = {"like": "cross", "cross": "like"}
-
     def index(kind, distance, side):
         side = "behind" if distance in (0, reach) else side
         return names[side, kind, distance]
@@ -221,45 +247,50 @@
         down_weight,
         flops=work,
     )
-    sent = [move("swap", a) for a in sent]
-
-    def part(a, k):
-        return a[k * PAIR : (k + 1) * PAIR]
-
-    def chip_sum(kind, distance):
+    urgently = move("swap", sent[0])
+    rest, urgently = lax.optimization_barrier((sent[1], urgently))
+    sent = [urgently, move("swap", rest)]
+
+    def terms(kind, distance):
         k = kept.index((kind, distance))
-        theirs = part(sent[0], k) if k < urgent else part(sent[1], k - urgent)
-        return part(keep, k) + theirs.astype(F32)
-
-    far, last_like, last_cross = lax.optimization_barrier(
-        tuple(
-            chip_sum(*name).astype(BF16)
-            for name in (("like", reach), ("like", reach - 1), ("cross", reach - 1))
-        )
-    )
-    like_sums = {d: chip_sum("like", d) for d in range(1, reach - 1)} | {reach - 1: last_like}
-    like_sums[reach - 2] += move("two", far).astype(F32)
-    cross_sum = last_cross
-    arrived = []
-    for distance in away:
-        if distance > 1:
-            cross_sum = move("one", cross_sum).astype(F32) + chip_sum("cross", distance - 1)
+        return [block(keep, k), block(sent[0], k) if k < urgent else block(sent[1], k - urgent)]
+
+    came, arrived = {}, []
+
+    def total(kind, distance):
+        return add(terms(kind, distance) + came.get((kind, distance), []))
+
+    def deliver(kind, a, name, distance):
+        held = came.setdefault((name, distance), []) if distance else arrived
+        held.append(block(move(kind, a)))
+
+    first = [("cross", reach - 1), ("like", reach), ("like", reach - 1)]
+    ready = dict(zip(first, lax.optimization_barrier(tuple(total(*name) for name in first))))
+    deliver("one", ready["cross", reach - 1], "cross", reach - 2)
+    deliver("two", ready["like", reach], "like", reach - 2)
+    deliver("one", ready["like", reach - 1], "like", reach - 2)
+    for distance in range(reach - 2, 0, -1):
+        cross = total("cross", distance)
+        if distance == 1:
+            deliver("leave", cross, "like", 0)
+        elif distance == 2:
+            cross, near = lax.optimization_barrier((cross, total("like", 1)))
+            deliver("one", cross, "cross", 1)
+            deliver("one", near, "like", 0)
+            deliver("two", total("like", 2), "like", 0)
+        elif distance % 2:
+            deliver("one", cross, "cross", distance - 1)
+            deliver("one", total("like", distance), "like", distance - 1)
         else:
-            arrived.append(move("leave", cross_sum))
-        length = 2 - distance % 2
-        came = move("two" if length == 2 else "one", like_sums[distance])
-        if distance == length:
-            arrived.append(came)
-        else:
-            like_sums[distance - length] += came.astype(F32)
+            deliver("one", cross, "cross", distance - 1)
+            deliver("two", total("like", distance), "like", distance - 2)
+    arrays, mixed = distinct(arrived + terms("like", 0))
     return call(
-        mix_kernel,
+        lambda *refs: mix_kernel(mixed, *refs),
         struct(tokens.shape, BF16),
         ids,
         gates.T,
-        *arrived,
-        part(keep, len(kept) - 1),
-        part(sent[1], len(kept) - 1 - urgent),
+        *arrays,
         out_specs=pl.BlockSpec(memory_space=pl.ANY),
         scratch=[pltpu.VMEM(tokens.shape, BF16), pltpu.SemaphoreType.DMA((6,))],
     )

time: 56.7 us -> 53.6 us (0.945)
  starting transfers between devices: 24.8 us -> 23.5 us
  waiting for transfers between devices: 19.2 us -> 17.9 us
  local copies, waits for them, and re-layouts: 2.7 us -> 2.13 us
    ppermute x24, starting transfers between devices: 24.8 us -> 23.5 us  [move(): return lax.ppermute(a.astype(BF16), 'tensor', steps[kind])]
    ppermute x24, waiting for transfers between devices: 19.2 us -> 17.9 us  [move(): return lax.ppermute(a.astype(BF16), 'tensor', steps[kind])]
    unnamed x18 -> x20, local copies, waits for them, and re-layouts: 2.69 us -> 2.13 us
    pallas_call x4 -> x12, Pallas kernels: 9.35 us -> 9.68 us  [call(): pl.pallas_call(kernel, out_shape=out_shape, scratch_shapes=list(scratch),...]
  transfers between devices with their start and end apart: 24 -> 24, of which waited for: 15 -> 12; matrix products, arithmetic and copies ran while one was open for 0% -> 0% of each run, Pallas kernels for 0% -> 1%
where the time goes in v6:
time: 53.6 us; the launch traced here: 53.5 us
  starting transfers between devices  23.5 us (44%)
  waiting for transfers between devices  17.9 us (33%)
  Pallas kernels  9.68 us (18%)
  local copies, waits for them, and re-layouts  2.13 us (4%)
    ppermute x24, starting transfers between devices, move(): return lax.ppermute(a.astype(BF16), 'tensor', steps[kind])  23.5 us
    ppermute x24, waiting for transfers between devices, move(): return lax.ppermute(a.astype(BF16), 'tensor', steps[kind])  17.9 us
    pallas_call x12, Pallas kernels, call(): pl.pallas_call(kernel, out_shape=out_shape, scratch_shapes=list(scratch),...  9.68 us
    unnamed x20, local copies, waits for them, and re-layouts  2.13 us
  transfers between devices with their start and end apart: 24, of which 12 were waited for; matrix products, arithmetic and copies ran while one was open for 0% of the time, Pallas kernels for 1%

profile of v6, /device:TPU:0, one launch (start us, length us, event | category | flops | bytes accessed | tf_op | source)
XLA Modules:
  0.0 53.5 jit_solution(17074625627119472894)
XLA Ops:
  0.0 1.4 %copy-done = bf16[128,6144]{1,0:T(8,128)(2,1)S(1)} copy-done((bf16[128,6144]{1,0:T(8,128)(2,1)S(1)}, bf16[128,6144]{1,0:T(8,128)(2,1)}, u32[]{:S(2)}) %copy-start) | copy-done | bytes 1572888
  2.6 2.5 %collective-permute-start.1 = (bf16[24,3072]{1,0:T(8,128)(2,1)S(1)}, bf16[24,3072]{1,0:T(8,128)(2,1)S(1)}, u32[]{:S(2)}, u32[]{:S(2)}) collective-permute-start(bf16[24,3072]{1,0:T(8,128)(2,1)S(1)} %shard_map.65.refs_0_), channel_id=1, source_target_pairs={{0,3},{1,4},{4,1},{5,8},{8,5},{9,12},{12,9},{13,14},{14,13},{15,10... | collective-permute-start | bytes 442376 | tf_op jit(solution)/shard_map/ppermute | solution.py:180
  5.1 1.7 %collective-permute-start.4 = (bf16[24,3072]{1,0:T(8,128)(2,1)S(1)}, bf16[24,3072]{1,0:T(8,128)(2,1)S(1)}, u32[]{:S(2)}, u32[]{:S(2)}) collective-permute-start(bf16[24,3072]{1,0:T(8,128)(2,1)S(1)} %shard_map.65.refs_0_), channel_id=1, source_target_pairs={{0,8},{1,7},{4,12},{5,3},{8,14},{9,1},{12,10},{13,5},{14,6},{15,9}... | collective-permute-start | bytes 442376 | tf_op jit(solution)/shard_map/ppermute | solution.py:180
  6.8 1.6 %collective-permute-start.2 = (bf16[24,3072]{1,0:T(8,128)(2,1)S(1)}, bf16[24,3072]{1,0:T(8,128)(2,1)S(1)}, u32[]{:S(2)}, u32[]{:S(2)}) collective-permute-start(bf16[24,3072]{1,0:T(8,128)(2,1)S(1)} %shard_map.65.refs_0_), channel_id=1, source_target_pairs={{0,4},{1,3},{4,8},{5,1},{8,12},{9,5},{12,14},{13,9},{14,10},{15,13... | collective-permute-start | bytes 442376 | tf_op jit(solution)/shard_map/ppermute | solution.py:180
  8.4 1.9 %collective-permute-start.3 = (bf16[24,3072]{1,0:T(8,128)(2,1)S(1)}, bf16[24,3072]{1,0:T(8,128)(2,1)S(1)}, u32[]{:S(2)}, u32[]{:S(2)}) collective-permute-start(bf16[24,3072]{1,0:T(8,128)(2,1)S(1)} %collective-permute-done.1.refs_2_), channel_id=1, source_target_pairs={{0,4},{1,3},{4,8},{5,1},{8,12},{9,5},{12,14},{13,9},{14,10},{15,13... | collective-permute-start | bytes 442376 | tf_op jit(solution)/shard_map/ppermute | solution.py:180
  10.3 2.5 %collective-permute-done.4.refs_5_ = bf16[24,3072]{1,0:T(8,128)(2,1)S(1)} collective-permute-done((bf16[24,3072]{1,0:T(8,128)(2,1)S(1)}, bf16[24,3072]{1,0:T(8,128)(2,1)S(1)}, u32[]{:S(2)}, u32[]{:S(2)}) %collective-permute-start.4) | collective-permute-done | bytes 147488 | tf_op jit(solution)/shard_map/ppermute | solution.py:180
  12.9 2.4 %collective-permute-start.7 = (bf16[24,3072]{1,0:T(8,128)(2,1)S(1)}, bf16[24,3072]{1,0:T(8,128)(2,1)S(1)}, u32[]{:S(2)}, u32[]{:S(2)}) collective-permute-start(bf16[24,3072]{1,0:T(8,128)(2,1)S(1)} %collective-permute-done.4.refs_5_), channel_id=1, source_target_pairs={{0,8},{1,7},{4,12},{5,3},{8,14},{9,1},{12,10},{13,5},{14,6},{15,9}... | collective-permute-start | bytes 442376 | tf_op jit(solution)/shard_map/ppermute | solution.py:180
  15.3 1.5 %collective-permute-start.6 = (bf16[24,3072]{1,0:T(8,128)(2,1)S(1)}, bf16[24,3072]{1,0:T(8,128)(2,1)S(1)}, u32[]{:S(2)}, u32[]{:S(2)}) collective-permute-start(bf16[24,3072]{1,0:T(8,128)(2,1)S(1)} %collective-permute-done.4.refs_5_), channel_id=1, source_target_pairs={{0,4},{1,3},{4,8},{5,1},{8,12},{9,5},{12,14},{13,9},{14,10},{15,13... | collective-permute-start | bytes 442376 | tf_op jit(solution)/shard_map/ppermute | solution.py:180
  16.9 0.7 %collective-permute-start.5 = (bf16[24,3072]{1,0:T(8,128)(2,1)S(1)}, bf16[24,3072]{1,0:T(8,128)(2,1)S(1)}, u32[]{:S(2)}, u32[]{:S(2)}) collective-permute-start(bf16[24,3072]{1,0:T(8,128)(2,1)S(1)} %collective-permute-done.3.refs_4_), channel_id=1, source_target_pairs={{0,4},{1,3},{4,8},{5,1},{8,12},{9,5},{12,14},{13,9},{14,10},{15,13... | collective-permute-start | bytes 442376 | tf_op jit(solution)/shard_map/ppermute | solution.py:180
  17.6 3.0 %collective-permute-done.7.refs_8_ = bf16[24,3072]{1,0:T(8,128)(2,1)S(1)} collective-permute-done((bf16[24,3072]{1,0:T(8,128)(2,1)S(1)}, bf16[24,3072]{1,0:T(8,128)(2,1)S(1)}, u32[]{:S(2)}, u32[]{:S(2)}) %collective-permute-start.7) | collective-permute-done | bytes 147488 | tf_op jit(solution)/shard_map/ppermute | solution.py:180
  20.6 0.7 %collective-permute-done.6.refs_7_ = bf16[24,3072]{1,0:T(8,128)(2,1)S(1)} collective-permute-done((bf16[24,3072]{1,0:T(8,128)(2,1)S(1)}, bf16[24,3072]{1,0:T(8,128)(2,1)S(1)}, u32[]{:S(2)}, u32[]{:S(2)}) %collective-permute-start.6) | collective-permute-done | bytes 147488 | tf_op jit(solution)/shard_map/ppermute | solution.py:180
  21.8 1.1 %collective-permute-done.5.refs_6_ = bf16[24,3072]{1,0:T(8,128)(2,1)S(1)} collective-permute-done((bf16[24,3072]{1,0:T(8,128)(2,1)S(1)}, bf16[24,3072]{1,0:T(8,128)(2,1)S(1)}, u32[]{:S(2)}, u32[]{:S(2)}) %collective-permute-start.5) | collective-permute-done | bytes 147488 | tf_op jit(solution)/shard_map/ppermute | solution.py:180
  22.9 1.3 %collective-permute-done.13.refs_14_ = bf16[24,3072]{1,0:T(8,128)(2,1)S(1)} collective-permute-done((bf16[24,3072]{1,0:T(8,128)(2,1)S(1)}, bf16[24,3072]{1,0:T(8,128)(2,1)S(1)}, u32[]{:S(2)}, u32[]{:S(2)}) %collective-permute-start.13) | collective-permute-done | bytes 147488 | tf_op jit(solution)/shard_map/ppermute | solution.py:180
  24.3 5.3 %shard_map.66.refs_0_ = bf16[192,672]{1,0:T(8,128)(2,1)S(1)} custom-call(bf16[24,3072]{1,0:T(8,128)(2,1)S(1)} %shard_map.65.refs_0_, bf16[24,3072]{1,0:T(8,128)(2,1)S(1)} %collective-permute-done.refs_1_, bf16[24,3072]{1,0:T(8,128)(2,1)S(1)} %collective-permute-done.1.refs_2_, bf16[24,3072]{1,0:T(8,128)(2,1)S(1)} %collective-permute-done.2.refs_3_, ...), custom_call_target="tpu_custom_call" | custom-call | flops 3170893824 | bytes 18874368 | tf_op jit(solution)/shard_map/pallas_call | solution.py:150
  29.6 2.0 %shard_map.67 = (f32[192,3072]{1,0:T(8,128)S(1)}, bf16[72,3072]{1,0:T(8,128)(2,1)S(1)}, bf16[120,3072]{1,0:T(8,128)(2,1)S(1)}) custom-call(bf16[192,672]{1,0:T(8,128)(2,1)S(1)} %shard_map.66.refs_0_, bf16[672,6144]{1,0:T(8,128)(2,1)S(1)} %bitcast.7), custom_call_target="tpu_custom_call" | custom-call | flops 1585446912 | bytes 8515584 | tf_op jit(solution)/shard_map/pallas_call | solution.py:150
  31.9 1.7 %collective-permute-done.15.refs_1_ = bf16[72,3072]{1,0:T(8,128)(2,1)S(1)} collective-permute-done((bf16[72,3072]{1,0:T(8,128)(2,1)S(1)}, bf16[72,3072]{1,0:T(8,128)(2,1)S(1)}, u32[]{:S(2)}, u32[]{:S(2)}) %collective-permute-start.15) | collective-permute-done | bytes 442400 | tf_op jit(solution)/shard_map/ppermute | solution.py:180
  33.8 1.9 %collective-permute-start.17 = (bf16[24,3072]{1,0:T(8,128)(2,1)S(1)}, bf16[24,3072]{1,0:T(8,128)(2,1)S(1)}, u32[]{:S(2)}, u32[]{:S(2)}) collective-permute-start(bf16[24,3072]{1,0:T(8,128)(2,1)S(1)} %shard_map.68), channel_id=1, source_target_pairs={{0,4},{1,3},{4,8},{5,1},{8,12},{9,5},{12,14},{13,9},{14,10},{15,13... | collective-permute-start | bytes 442376 | tf_op jit(solution)/shard_map/ppermute | solution.py:180
  35.7 2.1 %collective-permute-start.19 = (bf16[24,3072]{1,0:T(8,128)(2,1)S(1)}, bf16[24,3072]{1,0:T(8,128)(2,1)S(1)}, u32[]{:S(2)}, u32[]{:S(2)}) collective-permute-start(bf16[24,3072]{1,0:T(8,128)(2,1)S(1)} %shard_map.69), channel_id=1, source_target_pairs={{0,8},{1,7},{4,12},{5,3},{8,14},{9,1},{12,10},{13,5},{14,6},{15,9}... | collective-permute-start | bytes 442376 | tf_op jit(solution)/shard_map/ppermute | solution.py:180
  37.9 1.9 %collective-permute-done.17.refs_2_ = bf16[24,3072]{1,0:T(8,128)(2,1)S(1)} collective-permute-done((bf16[24,3072]{1,0:T(8,128)(2,1)S(1)}, bf16[24,3072]{1,0:T(8,128)(2,1)S(1)}, u32[]{:S(2)}, u32[]{:S(2)}) %collective-permute-start.17) | collective-permute-done | bytes 147488 | tf_op jit(solution)/shard_map/ppermute | solution.py:180
  39.9 2.5 %collective-permute-start.22 = (bf16[24,3072]{1,0:T(8,128)(2,1)S(1)}, bf16[24,3072]{1,0:T(8,128)(2,1)S(1)}, u32[]{:S(2)}, u32[]{:S(2)}) collective-permute-start(bf16[24,3072]{1,0:T(8,128)(2,1)S(1)} %shard_map.71), channel_id=1, source_target_pairs={{0,4},{1,3},{4,8},{5,1},{8,12},{9,5},{12,14},{13,9},{14,10},{15,13... | collective-permute-start | bytes 442376 | tf_op jit(solution)/shard_map/ppermute | solution.py:180
  43.9 3.1 %collective-permute-start.21 = (bf16[24,3072]{1,0:T(8,128)(2,1)S(1)}, bf16[24,3072]{1,0:T(8,128)(2,1)S(1)}, u32[]{:S(2)}, u32[]{:S(2)}) collective-permute-start(bf16[24,3072]{1,0:T(8,128)(2,1)S(1)} %shard_map.73), channel_id=1, source_target_pairs={{0,8},{1,7},{4,12},{5,3},{8,14},{9,1},{12,10},{13,5},{14,6},{15,9}... | collective-permute-start | bytes 442376 | tf_op jit(solution)/shard_map/ppermute | solution.py:180
  47.6 3.4 %collective-permute-done.21.refs_3_ = bf16[24,3072]{1,0:T(8,128)(2,1)S(1)} collective-permute-done((bf16[24,3072]{1,0:T(8,128)(2,1)S(1)}, bf16[24,3072]{1,0:T(8,128)(2,1)S(1)}, u32[]{:S(2)}, u32[]{:S(2)}) %collective-permute-start.21) | collective-permute-done | bytes 147488 | tf_op jit(solution)/shard_map/ppermute | solution.py:180
  51.1 0.8 %collective-permute-done.23.refs_4_ = bf16[24,3072]{1,0:T(8,128)(2,1)S(1)} collective-permute-done((bf16[24,3072]{1,0:T(8,128)(2,1)S(1)}, bf16[24,3072]{1,0:T(8,128)(2,1)S(1)}, u32[]{:S(2)}, u32[]{:S(2)}) %collective-permute-start.23) | collective-permute-done | bytes 147488 | tf_op jit(solution)/shard_map/ppermute | solution.py:180
  51.9 1.6 %shard_map.75 = bf16[128,6144]{1,0:T(8,128)(2,1)} custom-call(s32[4,128]{1,0:T(4,128)S(1)} %bitcast.9, f32[4,128]{1,0:T(4,128)S(1)} %bitcast.10, bf16[24,3072]{1,0:T(8,128)(2,1)S(1)} %collective-permute-done.18.refs_2_, bf16[24,3072]{1,0:T(8,128)(2,1)S(1)} %collective-permute-done.21.refs_3_, bf16[24,3072]{1,0:T(8,128)(2,1)S(1)} %collective-permute-done.23.refs_4_, ...), custom_call_target="tpu_custom_call" | custom-call | bytes 3543040 | tf_op jit(solution)/shard_map/pallas_call | solution.py:150
  (59 shorter events, 4.6 us)
Async XLA Ops:
  2.6 5.7 %collective-permute-start.1 = (bf16[24,3072]{1,0:T(8,128)(2,1)S(1)}, bf16[24,3072]{1,0:T(8,128)(2,1)S(1)}, u32[]{:S(2)}, u32[]{:S(2)}) collective-permute-start(bf16[24,3072]{1,0:T(8,128)(2,1)S(1)} %shard_map.65.refs_0_), channel_id=1, source_target_pairs={{0,3},{1,4},{4,1},{5,8},{8,5},{9,12},{12,9},{13,14},{14,13},{15,10... | collective-permute-start | bytes 442376 | tf_op jit(solution)/shard_map/ppermute | solution.py:180
  5.1 7.7 %collective-permute-start.4 = (bf16[24,3072]{1,0:T(8,128)(2,1)S(1)}, bf16[24,3072]{1,0:T(8,128)(2,1)S(1)}, u32[]{:S(2)}, u32[]{:S(2)}) collective-permute-start(bf16[24,3072]{1,0:T(8,128)(2,1)S(1)} %shard_map.65.refs_0_), channel_id=1, source_target_pairs={{0,8},{1,7},{4,12},{5,3},{8,14},{9,1},{12,10},{13,5},{14,6},{15,9}... | collective-permute-start | bytes 442376 | tf_op jit(solution)/shard_map/ppermute | solution.py:180
  6.8 8.5 %collective-permute-start.2 = (bf16[24,3072]{1,0:T(8,128)(2,1)S(1)}, bf16[24,3072]{1,0:T(8,128)(2,1)S(1)}, u32[]{:S(2)}, u32[]{:S(2)}) collective-permute-start(bf16[24,3072]{1,0:T(8,128)(2,1)S(1)} %shard_map.65.refs_0_), channel_id=1, source_target_pairs={{0,4},{1,3},{4,8},{5,1},{8,12},{9,5},{12,14},{13,9},{14,10},{15,13... | collective-permute-start | bytes 442376 | tf_op jit(solution)/shard_map/ppermute | solution.py:180
  8.4 8.5 %collective-permute-start = (bf16[24,3072]{1,0:T(8,128)(2,1)S(1)}, bf16[24,3072]{1,0:T(8,128)(2,1)S(1)}, u32[]{:S(2)}, u32[]{:S(2)}) collective-permute-start(bf16[24,3072]{1,0:T(8,128)(2,1)S(1)} %shard_map.65.refs_0_), channel_id=1, source_target_pairs={{0,1},{1,0},{4,5},{5,4},{8,9},{9,8},{12,13},{13,12},{14,15},{15,14... | collective-permute-start | bytes 442376 | tf_op jit(solution)/shard_map/ppermute | solution.py:180
  8.4 8.5 %collective-permute-start.3 = (bf16[24,3072]{1,0:T(8,128)(2,1)S(1)}, bf16[24,3072]{1,0:T(8,128)(2,1)S(1)}, u32[]{:S(2)}, u32[]{:S(2)}) collective-permute-start(bf16[24,3072]{1,0:T(8,128)(2,1)S(1)} %collective-permute-done.1.refs_2_), channel_id=1, source_target_pairs={{0,4},{1,3},{4,8},{5,1},{8,12},{9,5},{12,14},{13,9},{14,10},{15,13... | collective-permute-start | bytes 442376 | tf_op jit(solution)/shard_map/ppermute | solution.py:180
  12.8 4.9 %collective-permute-start.12 = (bf16[24,3072]{1,0:T(8,128)(2,1)S(1)}, bf16[24,3072]{1,0:T(8,128)(2,1)S(1)}, u32[]{:S(2)}, u32[]{:S(2)}) collective-permute-start(bf16[24,3072]{1,0:T(8,128)(2,1)S(1)} %collective-permute-done.4.refs_5_), channel_id=1, source_target_pairs={{0,1},{1,0},{4,5},{5,4},{8,9},{9,8},{12,13},{13,12},{14,15},{15,14... | collective-permute-start | bytes 442376 | tf_op jit(solution)/shard_map/ppermute | solution.py:180
  12.9 7.7 %collective-permute-start.7 = (bf16[24,3072]{1,0:T(8,128)(2,1)S(1)}, bf16[24,3072]{1,0:T(8,128)(2,1)S(1)}, u32[]{:S(2)}, u32[]{:S(2)}) collective-permute-start(bf16[24,3072]{1,0:T(8,128)(2,1)S(1)} %collective-permute-done.4.refs_5_), channel_id=1, source_target_pairs={{0,8},{1,7},{4,12},{5,3},{8,14},{9,1},{12,10},{13,5},{14,6},{15,9}... | collective-permute-start | bytes 442376 | tf_op jit(solution)/shard_map/ppermute | solution.py:180
  15.3 6.1 %collective-permute-start.6 = (bf16[24,3072]{1,0:T(8,128)(2,1)S(1)}, bf16[24,3072]{1,0:T(8,128)(2,1)S(1)}, u32[]{:S(2)}, u32[]{:S(2)}) collective-permute-start(bf16[24,3072]{1,0:T(8,128)(2,1)S(1)} %collective-permute-done.4.refs_5_), channel_id=1, source_target_pairs={{0,4},{1,3},{4,8},{5,1},{8,12},{9,5},{12,14},{13,9},{14,10},{15,13... | collective-permute-start | bytes 442376 | tf_op jit(solution)/shard_map/ppermute | solution.py:180
  16.8 4.5 %collective-permute-start.10 = (bf16[24,3072]{1,0:T(8,128)(2,1)S(1)}, bf16[24,3072]{1,0:T(8,128)(2,1)S(1)}, u32[]{:S(2)}, u32[]{:S(2)}) collective-permute-start(bf16[24,3072]{1,0:T(8,128)(2,1)S(1)} %collective-permute-done.2.refs_3_), channel_id=1, source_target_pairs={{0,1},{1,0},{4,5},{5,4},{8,9},{9,8},{12,13},{13,12},{14,15},{15,14... | collective-permute-start | bytes 442376 | tf_op jit(solution)/shard_map/ppermute | solution.py:180
  16.9 6.0 %collective-permute-start.5 = (bf16[24,3072]{1,0:T(8,128)(2,1)S(1)}, bf16[24,3072]{1,0:T(8,128)(2,1)S(1)}, u32[]{:S(2)}, u32[]{:S(2)}) collective-permute-start(bf16[24,3072]{1,0:T(8,128)(2,1)S(1)} %collective-permute-done.3.refs_4_), channel_id=1, source_target_pairs={{0,4},{1,3},{4,8},{5,1},{8,12},{9,5},{12,14},{13,9},{14,10},{15,13... | collective-permute-start | bytes 442376 | tf_op jit(solution)/shard_map/ppermute | solution.py:180
  17.6 5.3 %collective-permute-start.9 = (bf16[24,3072]{1,0:T(8,128)(2,1)S(1)}, bf16[24,3072]{1,0:T(8,128)(2,1)S(1)}, u32[]{:S(2)}, u32[]{:S(2)}) collective-permute-start(bf16[24,3072]{1,0:T(8,128)(2,1)S(1)} %collective-permute-done.1.refs_2_), channel_id=1, source_target_pairs={{0,1},{1,0},{4,5},{5,4},{8,9},{9,8},{12,13},{13,12},{14,15},{15,14... | collective-permute-start | bytes 442376 | tf_op jit(solution)/shard_map/ppermute | solution.py:180
  20.6 2.3 %collective-permute-start.11 = (bf16[24,3072]{1,0:T(8,128)(2,1)S(1)}, bf16[24,3072]{1,0:T(8,128)(2,1)S(1)}, u32[]{:S(2)}, u32[]{:S(2)}) collective-permute-start(bf16[24,3072]{1,0:T(8,128)(2,1)S(1)} %collective-permute-done.3.refs_4_), channel_id=1, source_target_pairs={{0,1},{1,0},{4,5},{5,4},{8,9},{9,8},{12,13},{13,12},{14,15},{15,14... | collective-permute-start | bytes 442376 | tf_op jit(solution)/shard_map/ppermute | solution.py:180
  21.3 1.6 %collective-permute-start.8 = (bf16[24,3072]{1,0:T(8,128)(2,1)S(1)}, bf16[24,3072]{1,0:T(8,128)(2,1)S(1)}, u32[]{:S(2)}, u32[]{:S(2)}) collective-permute-start(bf16[24,3072]{1,0:T(8,128)(2,1)S(1)} %collective-permute-done.7.refs_8_), channel_id=1, source_target_pairs={{0,1},{1,0},{4,5},{5,4},{8,9},{9,8},{12,13},{13,12},{14,15},{15,14... | collective-permute-start | bytes 442376 | tf_op jit(solution)/shard_map/ppermute | solution.py:180
  21.3 1.6 %collective-permute-start.14 = (bf16[24,3072]{1,0:T(8,128)(2,1)S(1)}, bf16[24,3072]{1,0:T(8,128)(2,1)S(1)}, u32[]{:S(2)}, u32[]{:S(2)}) collective-permute-start(bf16[24,3072]{1,0:T(8,128)(2,1)S(1)} %collective-permute-done.6.refs_7_), channel_id=1, source_target_pairs={{0,1},{1,0},{4,5},{5,4},{8,9},{9,8},{12,13},{13,12},{14,15},{15,14... | collective-permute-start | bytes 442376 | tf_op jit(solution)/shard_map/ppermute | solution.py:180
  22.9 1.4 %collective-permute-start.13 = (bf16[24,3072]{1,0:T(8,128)(2,1)S(1)}, bf16[24,3072]{1,0:T(8,128)(2,1)S(1)}, u32[]{:S(2)}, u32[]{:S(2)}) collective-permute-start(bf16[24,3072]{1,0:T(8,128)(2,1)S(1)} %collective-permute-done.5.refs_6_), channel_id=1, source_target_pairs={{0,1},{1,0},{4,5},{5,4},{8,9},{9,8},{12,13},{13,12},{14,15},{15,14... | collective-permute-start | bytes 442376 | tf_op jit(solution)/shard_map/ppermute | solution.py:180
  31.7 1.9 %collective-permute-start.15 = (bf16[72,3072]{1,0:T(8,128)(2,1)S(1)}, bf16[72,3072]{1,0:T(8,128)(2,1)S(1)}, u32[]{:S(2)}, u32[]{:S(2)}) collective-permute-start(bf16[72,3072]{1,0:T(8,128)(2,1)S(1)} %get-tuple-element.17), channel_id=1, source_target_pairs={{0,1},{1,0},{4,5},{5,4},{8,9},{9,8},{12,13},{13,12},{14,15},{15,14... | collective-permute-start | bytes 1327112 | tf_op jit(solution)/shard_map/ppermute | solution.py:180
  33.5 4.4 %collective-permute-start.16 = (bf16[120,3072]{1,0:T(8,128)(2,1)S(1)}, bf16[120,3072]{1,0:T(8,128)(2,1)S(1)}, u32[]{:S(2)}, u32[]{:S(2)}) collective-permute-start(bf16[120,3072]{1,0:T(8,128)(2,1)S(1)} %get-tuple-element.18), channel_id=1, source_target_pairs={{0,1},{1,0},{4,5},{5,4},{8,9},{9,8},{12,13},{13,12},{14,15},{15,14... | collective-permute-start | bytes 2211848 | tf_op jit(solution)/shard_map/ppermute | solution.py:180
  33.8 6.0 %collective-permute-start.17 = (bf16[24,3072]{1,0:T(8,128)(2,1)S(1)}, bf16[24,3072]{1,0:T(8,128)(2,1)S(1)}, u32[]{:S(2)}, u32[]{:S(2)}) collective-permute-start(bf16[24,3072]{1,0:T(8,128)(2,1)S(1)} %shard_map.68), channel_id=1, source_target_pairs={{0,4},{1,3},{4,8},{5,1},{8,12},{9,5},{12,14},{13,9},{14,10},{15,13... | collective-permute-start | bytes 442376 | tf_op jit(solution)/shard_map/ppermute | solution.py:180
  35.7 7.7 %collective-permute-start.19 = (bf16[24,3072]{1,0:T(8,128)(2,1)S(1)}, bf16[24,3072]{1,0:T(8,128)(2,1)S(1)}, u32[]{:S(2)}, u32[]{:S(2)}) collective-permute-start(bf16[24,3072]{1,0:T(8,128)(2,1)S(1)} %shard_map.69), channel_id=1, source_target_pairs={{0,8},{1,7},{4,12},{5,3},{8,14},{9,1},{12,10},{13,5},{14,6},{15,9}... | collective-permute-start | bytes 442376 | tf_op jit(solution)/shard_map/ppermute | solution.py:180
  37.8 6.0 %collective-permute-start.20 = (bf16[24,3072]{1,0:T(8,128)(2,1)S(1)}, bf16[24,3072]{1,0:T(8,128)(2,1)S(1)}, u32[]{:S(2)}, u32[]{:S(2)}) collective-permute-start(bf16[24,3072]{1,0:T(8,128)(2,1)S(1)} %shard_map.70), channel_id=1, source_target_pairs={{0,4},{1,3},{4,8},{5,1},{8,12},{9,5},{12,14},{13,9},{14,10},{15,13... | collective-permute-start | bytes 442376 | tf_op jit(solution)/shard_map/ppermute | solution.py:180
  39.9 7.2 %collective-permute-start.22 = (bf16[24,3072]{1,0:T(8,128)(2,1)S(1)}, bf16[24,3072]{1,0:T(8,128)(2,1)S(1)}, u32[]{:S(2)}, u32[]{:S(2)}) collective-permute-start(bf16[24,3072]{1,0:T(8,128)(2,1)S(1)} %shard_map.71), channel_id=1, source_target_pairs={{0,4},{1,3},{4,8},{5,1},{8,12},{9,5},{12,14},{13,9},{14,10},{15,13... | collective-permute-start | bytes 442376 | tf_op jit(solution)/shard_map/ppermute | solution.py:180
  42.4 5.2 %collective-permute-start.18 = (bf16[24,3072]{1,0:T(8,128)(2,1)S(1)}, bf16[24,3072]{1,0:T(8,128)(2,1)S(1)}, u32[]{:S(2)}, u32[]{:S(2)}) collective-permute-start(bf16[24,3072]{1,0:T(8,128)(2,1)S(1)} %shard_map.72), channel_id=1, source_target_pairs={{0,4},{1,3},{4,8},{5,1},{8,12},{9,5},{12,14},{13,9},{14,10},{15,13... | collective-permute-start | bytes 442376 | tf_op jit(solution)/shard_map/ppermute | solution.py:180
  43.9 7.1 %collective-permute-start.21 = (bf16[24,3072]{1,0:T(8,128)(2,1)S(1)}, bf16[24,3072]{1,0:T(8,128)(2,1)S(1)}, u32[]{:S(2)}, u32[]{:S(2)}) collective-permute-start(bf16[24,3072]{1,0:T(8,128)(2,1)S(1)} %shard_map.73), channel_id=1, source_target_pairs={{0,8},{1,7},{4,12},{5,3},{8,14},{9,1},{12,10},{13,5},{14,6},{15,9}... | collective-permute-start | bytes 442376 | tf_op jit(solution)/shard_map/ppermute | solution.py:180
  47.1 4.8 %collective-permute-start.23 = (bf16[24,3072]{1,0:T(8,128)(2,1)S(1)}, bf16[24,3072]{1,0:T(8,128)(2,1)S(1)}, u32[]{:S(2)}, u32[]{:S(2)}) collective-permute-start(bf16[24,3072]{1,0:T(8,128)(2,1)S(1)} %shard_map.74), channel_id=1, source_target_pairs={{0,5},{1,2},{4,9},{5,0},{8,13},{9,4},{12,15},{13,8},{14,11},{15,12... | collective-permute-start | bytes 442376 | tf_op jit(solution)/shard_map/ppermute | solution.py:180
  (10 other events, 180.8 us)

commit v7 on v6

--- a/solution.py
+++ b/solution.py
@@ -53,13 +53,34 @@
     return rows(0), rows(CAP)
 
 
-def compact_kernel(ids_ref, tokens_ref, out_ref):
+def compact_kernel(ids_ref, tokens_ref, out_ref, upper_ref, lower_ref, ids_here, tokens_here, arrived):
     half = out_ref.shape[1]
-    upper, lower = choose(ids_ref[...])
-    out_ref[...] = (
-        jnp.dot(upper, tokens_ref[:, :half], preferred_element_type=F32)
-        + jnp.dot(lower, tokens_ref[:, half:], preferred_element_type=F32)
-    ).astype(BF16)
+    tile = half // 3
+    copies = [pltpu.make_async_copy(ids_ref, ids_here, arrived.at[6])]
+    for step in range(3):
+        for side in range(2):
+            start = side * half + step * tile
+            there = slice(start, start + tile)
+            copies.append(
+                pltpu.make_async_copy(
+                    tokens_ref.at[:, there], tokens_here.at[:, there], arrived.at[2 * step + side]
+                )
+            )
+    for copy in copies:
+        copy.start()
+    copies[0].wait()
+    choosers = choose(ids_here[...])
+    upper_ref[...], lower_ref[...] = choosers
+    for step in range(3):
+        here = slice(step * tile, (step + 1) * tile)
+        total = 0.0
+        for side, chooser in enumerate(choosers):
+            copies[1 + 2 * step + side].wait()
+            start = side * half + step * tile
+            total = total + jnp.dot(
+                chooser, tokens_here[:, start : start + tile], preferred_element_type=F32
+            )
+        out_ref[:, here] = total.astype(BF16)
 
 
 def copy_kernel(in_ref, out_ref):
@@ -115,7 +136,7 @@
     out_ref[...] = total.astype(out_ref.dtype)
 
 
-def mix_kernel(blocks, ids_ref, gates_ref, *refs):
+def mix_kernel(blocks, ids_ref, gates_ref, upper_ref, lower_ref, *refs):
     (*arrays, out_ref, values, written) = refs
     half = values.shape[1] // 2
     tile = half // 3
@@ -123,7 +144,7 @@
     tokens = ids.shape[1]
     share = jnp.sum(jnp.where(ids == 0, gates_ref[...], 0.0), axis=0, keepdims=True)
     share = jnp.broadcast_to(share, (tokens, tokens)).T[:, :1]
-    choosers = choose(ids)
+    choosers = (upper_ref[...], lower_ref[...])
     copies = []
     for step in range(3):
         here = slice(step * tile, (step + 1) * tile)
@@ -182,8 +203,19 @@
     struct = jax.ShapeDtypeStruct
     ids = expert_ids.T
     work = 2 * rows * units * width
-    own = call(compact_kernel, struct((PAIR, half), BF16), ids, tokens)
-    own = call(copy_kernel, struct(own.shape, BF16), own, flops=20 * work)
+    own, *choosers = call(
+        compact_kernel,
+        [struct((PAIR, half), BF16)] + [struct((PAIR, count), BF16)] * 2,
+        pltpu.with_memory_space_constraint(ids, pltpu.MemorySpace.HBM),
+        pltpu.with_memory_space_constraint(tokens, pltpu.MemorySpace.HBM),
+        in_specs=[pl.BlockSpec(memory_space=pl.ANY)] * 2,
+        scratch=[
+            pltpu.VMEM(ids.shape, ids.dtype),
+            pltpu.VMEM(tokens.shape, BF16),
+            pltpu.SemaphoreType.DMA((7,)),
+        ],
+    )
+    own = call(copy_kernel, struct(own.shape, BF16), own, flops=8 * work)
 
     def block(a, k=0):
         return a, k * PAIR
@@ -290,6 +322,7 @@
         struct(tokens.shape, BF16),
         ids,
         gates.T,
+        *choosers,
         *arrays,
         out_specs=pl.BlockSpec(memory_space=pl.ANY),
         scratch=[pltpu.VMEM(tokens.shape, BF16), pltpu.SemaphoreType.DMA((6,))],

time: 53.6 us -> 52.9 us (0.987)
  local copies, waits for them, and re-layouts: 2.13 us -> 0.05 us
  Pallas kernels: 9.68 us -> 11 us
    unnamed x20 -> x16, local copies, waits for them, and re-layouts: 2.13 us -> 0.05 us
    pallas_call x12, Pallas kernels: 9.68 us -> 11 us  [call(): pl.pallas_call(kernel, out_shape=out_shape, scratch_shapes=list(scratch),...]
where the time goes in v7:
time: 52.9 us; the launch traced here: 52.7 us
  starting transfers between devices  23.6 us (45%)
  waiting for transfers between devices  17.9 us (34%)
  Pallas kernels  11 us (21%)
    ppermute x24, starting transfers between devices, move(): return lax.ppermute(a.astype(BF16), 'tensor', steps[kind])  23.6 us
    ppermute x24, waiting for transfers between devices, move(): return lax.ppermute(a.astype(BF16), 'tensor', steps[kind])  17.9 us
    pallas_call x12, Pallas kernels, call(): pl.pallas_call(kernel, out_shape=out_shape, scratch_shapes=list(scratch),...  11 us
  transfers between devices with their start and end apart: 24, of which 12 were waited for; matrix products, arithmetic and copies ran while one was open for 0% of the time, Pallas kernels for 1%

profile of v7, /device:TPU:0, one launch (start us, length us, event | category | flops | bytes accessed | tf_op | source)
XLA Modules:
  0.0 52.7 jit_solution(14108909476684491708)
XLA Ops:
  0.0 1.9 %shard_map.64 = (bf16[24,3072]{1,0:T(8,128)(2,1)S(1)}, bf16[24,128]{1,0:T(8,128)(2,1)S(1)}, bf16[24,128]{1,0:T(8,128)(2,1)S(1)}) custom-call(s32[4,128]{1,0:T(4,128)} %bitcast.8, bf16[128,6144]{1,0:T(8,128)(2,1)} %tokens_ref.1), custom_call_target="tpu_custom_call" | custom-call | bytes 1574912 | tf_op jit(solution)/shard_map/pallas_call | solution.py:171
  2.0 2.5 %collective-permute-start.1 = (bf16[24,3072]{1,0:T(8,128)(2,1)S(1)}, bf16[24,3072]{1,0:T(8,128)(2,1)S(1)}, u32[]{:S(2)}, u32[]{:S(2)}) collective-permute-start(bf16[24,3072]{1,0:T(8,128)(2,1)S(1)} %shard_map.65.refs_0_), channel_id=1, source_target_pairs={{0,3},{1,4},{4,1},{5,8},{8,5},{9,12},{12,9},{13,14},{14,13},{15,10... | collective-permute-start | bytes 442376 | tf_op jit(solution)/shard_map/ppermute | solution.py:201
  4.5 1.7 %collective-permute-start.4 = (bf16[24,3072]{1,0:T(8,128)(2,1)S(1)}, bf16[24,3072]{1,0:T(8,128)(2,1)S(1)}, u32[]{:S(2)}, u32[]{:S(2)}) collective-permute-start(bf16[24,3072]{1,0:T(8,128)(2,1)S(1)} %shard_map.65.refs_0_), channel_id=1, source_target_pairs={{0,8},{1,7},{4,12},{5,3},{8,14},{9,1},{12,10},{13,5},{14,6},{15,9}... | collective-permute-start | bytes 442376 | tf_op jit(solution)/shard_map/ppermute | solution.py:201
  6.2 1.6 %collective-permute-start.2 = (bf16[24,3072]{1,0:T(8,128)(2,1)S(1)}, bf16[24,3072]{1,0:T(8,128)(2,1)S(1)}, u32[]{:S(2)}, u32[]{:S(2)}) collective-permute-start(bf16[24,3072]{1,0:T(8,128)(2,1)S(1)} %shard_map.65.refs_0_), channel_id=1, source_target_pairs={{0,4},{1,3},{4,8},{5,1},{8,12},{9,5},{12,14},{13,9},{14,10},{15,13... | collective-permute-start | bytes 442376 | tf_op jit(solution)/shard_map/ppermute | solution.py:201
  7.8 1.9 %collective-permute-start.3 = (bf16[24,3072]{1,0:T(8,128)(2,1)S(1)}, bf16[24,3072]{1,0:T(8,128)(2,1)S(1)}, u32[]{:S(2)}, u32[]{:S(2)}) collective-permute-start(bf16[24,3072]{1,0:T(8,128)(2,1)S(1)} %collective-permute-done.1.refs_2_), channel_id=1, source_target_pairs={{0,4},{1,3},{4,8},{5,1},{8,12},{9,5},{12,14},{13,9},{14,10},{15,13... | collective-permute-start | bytes 442376 | tf_op jit(solution)/shard_map/ppermute | solution.py:201
  9.7 2.5 %collective-permute-done.4.refs_5_ = bf16[24,3072]{1,0:T(8,128)(2,1)S(1)} collective-permute-done((bf16[24,3072]{1,0:T(8,128)(2,1)S(1)}, bf16[24,3072]{1,0:T(8,128)(2,1)S(1)}, u32[]{:S(2)}, u32[]{:S(2)}) %collective-permute-start.4) | collective-permute-done | bytes 147488 | tf_op jit(solution)/shard_map/ppermute | solution.py:201
  12.3 2.4 %collective-permute-start.7 = (bf16[24,3072]{1,0:T(8,128)(2,1)S(1)}, bf16[24,3072]{1,0:T(8,128)(2,1)S(1)}, u32[]{:S(2)}, u32[]{:S(2)}) collective-permute-start(bf16[24,3072]{1,0:T(8,128)(2,1)S(1)} %collective-permute-done.4.refs_5_), channel_id=1, source_target_pairs={{0,8},{1,7},{4,12},{5,3},{8,14},{9,1},{12,10},{13,5},{14,6},{15,9}... | collective-permute-start | bytes 442376 | tf_op jit(solution)/shard_map/ppermute | solution.py:201
  14.7 1.6 %collective-permute-start.6 = (bf16[24,3072]{1,0:T(8,128)(2,1)S(1)}, bf16[24,3072]{1,0:T(8,128)(2,1)S(1)}, u32[]{:S(2)}, u32[]{:S(2)}) collective-permute-start(bf16[24,3072]{1,0:T(8,128)(2,1)S(1)} %collective-permute-done.4.refs_5_), channel_id=1, source_target_pairs={{0,4},{1,3},{4,8},{5,1},{8,12},{9,5},{12,14},{13,9},{14,10},{15,13... | collective-permute-start | bytes 442376 | tf_op jit(solution)/shard_map/ppermute | solution.py:201
  16.3 0.7 %collective-permute-start.5 = (bf16[24,3072]{1,0:T(8,128)(2,1)S(1)}, bf16[24,3072]{1,0:T(8,128)(2,1)S(1)}, u32[]{:S(2)}, u32[]{:S(2)}) collective-permute-start(bf16[24,3072]{1,0:T(8,128)(2,1)S(1)} %collective-permute-done.3.refs_4_), channel_id=1, source_target_pairs={{0,4},{1,3},{4,8},{5,1},{8,12},{9,5},{12,14},{13,9},{14,10},{15,13... | collective-permute-start | bytes 442376 | tf_op jit(solution)/shard_map/ppermute | solution.py:201
  17.0 3.0 %collective-permute-done.7.refs_8_ = bf16[24,3072]{1,0:T(8,128)(2,1)S(1)} collective-permute-done((bf16[24,3072]{1,0:T(8,128)(2,1)S(1)}, bf16[24,3072]{1,0:T(8,128)(2,1)S(1)}, u32[]{:S(2)}, u32[]{:S(2)}) %collective-permute-start.7) | collective-permute-done | bytes 147488 | tf_op jit(solution)/shard_map/ppermute | solution.py:201
  20.0 0.7 %collective-permute-done.6.refs_7_ = bf16[24,3072]{1,0:T(8,128)(2,1)S(1)} collective-permute-done((bf16[24,3072]{1,0:T(8,128)(2,1)S(1)}, bf16[24,3072]{1,0:T(8,128)(2,1)S(1)}, u32[]{:S(2)}, u32[]{:S(2)}) %collective-permute-start.6) | collective-permute-done | bytes 147488 | tf_op jit(solution)/shard_map/ppermute | solution.py:201
  21.2 1.1 %collective-permute-done.5.refs_6_ = bf16[24,3072]{1,0:T(8,128)(2,1)S(1)} collective-permute-done((bf16[24,3072]{1,0:T(8,128)(2,1)S(1)}, bf16[24,3072]{1,0:T(8,128)(2,1)S(1)}, u32[]{:S(2)}, u32[]{:S(2)}) %collective-permute-start.5) | collective-permute-done | bytes 147488 | tf_op jit(solution)/shard_map/ppermute | solution.py:201
  22.3 1.3 %collective-permute-done.13.refs_14_ = bf16[24,3072]{1,0:T(8,128)(2,1)S(1)} collective-permute-done((bf16[24,3072]{1,0:T(8,128)(2,1)S(1)}, bf16[24,3072]{1,0:T(8,128)(2,1)S(1)}, u32[]{:S(2)}, u32[]{:S(2)}) %collective-permute-start.13) | collective-permute-done | bytes 147488 | tf_op jit(solution)/shard_map/ppermute | solution.py:201
  23.7 5.3 %shard_map.66.refs_0_ = bf16[192,672]{1,0:T(8,128)(2,1)S(1)} custom-call(bf16[24,3072]{1,0:T(8,128)(2,1)S(1)} %shard_map.65.refs_0_, bf16[24,3072]{1,0:T(8,128)(2,1)S(1)} %collective-permute-done.refs_1_, bf16[24,3072]{1,0:T(8,128)(2,1)S(1)} %collective-permute-done.1.refs_2_, bf16[24,3072]{1,0:T(8,128)(2,1)S(1)} %collective-permute-done.2.refs_3_, ...), custom_call_target="tpu_custom_call" | custom-call | flops 3170893824 | bytes 18874368 | tf_op jit(solution)/shard_map/pallas_call | solution.py:171
  29.0 2.0 %shard_map.67 = (f32[192,3072]{1,0:T(8,128)S(1)}, bf16[72,3072]{1,0:T(8,128)(2,1)S(1)}, bf16[120,3072]{1,0:T(8,128)(2,1)S(1)}) custom-call(bf16[192,672]{1,0:T(8,128)(2,1)S(1)} %shard_map.66.refs_0_, bf16[672,6144]{1,0:T(8,128)(2,1)S(1)} %bitcast.7), custom_call_target="tpu_custom_call" | custom-call | flops 1585446912 | bytes 8515584 | tf_op jit(solution)/shard_map/pallas_call | solution.py:171
  31.2 1.7 %collective-permute-done.15.refs_1_ = bf16[72,3072]{1,0:T(8,128)(2,1)S(1)} collective-permute-done((bf16[72,3072]{1,0:T(8,128)(2,1)S(1)}, bf16[72,3072]{1,0:T(8,128)(2,1)S(1)}, u32[]{:S(2)}, u32[]{:S(2)}) %collective-permute-start.15) | collective-permute-done | bytes 442400 | tf_op jit(solution)/shard_map/ppermute | solution.py:201
  33.2 2.0 %collective-permute-start.17 = (bf16[24,3072]{1,0:T(8,128)(2,1)S(1)}, bf16[24,3072]{1,0:T(8,128)(2,1)S(1)}, u32[]{:S(2)}, u32[]{:S(2)}) collective-permute-start(bf16[24,3072]{1,0:T(8,128)(2,1)S(1)} %shard_map.68), channel_id=1, source_target_pairs={{0,4},{1,3},{4,8},{5,1},{8,12},{9,5},{12,14},{13,9},{14,10},{15,13... | collective-permute-start | bytes 442376 | tf_op jit(solution)/shard_map/ppermute | solution.py:201
  35.1 2.1 %collective-permute-start.19 = (bf16[24,3072]{1,0:T(8,128)(2,1)S(1)}, bf16[24,3072]{1,0:T(8,128)(2,1)S(1)}, u32[]{:S(2)}, u32[]{:S(2)}) collective-permute-start(bf16[24,3072]{1,0:T(8,128)(2,1)S(1)} %shard_map.69), channel_id=1, source_target_pairs={{0,8},{1,7},{4,12},{5,3},{8,14},{9,1},{12,10},{13,5},{14,6},{15,9}... | collective-permute-start | bytes 442376 | tf_op jit(solution)/shard_map/ppermute | solution.py:201
  37.3 1.9 %collective-permute-done.17.refs_2_ = bf16[24,3072]{1,0:T(8,128)(2,1)S(1)} collective-permute-done((bf16[24,3072]{1,0:T(8,128)(2,1)S(1)}, bf16[24,3072]{1,0:T(8,128)(2,1)S(1)}, u32[]{:S(2)}, u32[]{:S(2)}) %collective-permute-start.17) | collective-permute-done | bytes 147488 | tf_op jit(solution)/shard_map/ppermute | solution.py:201
  39.3 2.5 %collective-permute-start.22 = (bf16[24,3072]{1,0:T(8,128)(2,1)S(1)}, bf16[24,3072]{1,0:T(8,128)(2,1)S(1)}, u32[]{:S(2)}, u32[]{:S(2)}) collective-permute-start(bf16[24,3072]{1,0:T(8,128)(2,1)S(1)} %shard_map.71), channel_id=1, source_target_pairs={{0,4},{1,3},{4,8},{5,1},{8,12},{9,5},{12,14},{13,9},{14,10},{15,13... | collective-permute-start | bytes 442376 | tf_op jit(solution)/shard_map/ppermute | solution.py:201
  43.3 3.1 %collective-permute-start.21 = (bf16[24,3072]{1,0:T(8,128)(2,1)S(1)}, bf16[24,3072]{1,0:T(8,128)(2,1)S(1)}, u32[]{:S(2)}, u32[]{:S(2)}) collective-permute-start(bf16[24,3072]{1,0:T(8,128)(2,1)S(1)} %shard_map.73), channel_id=1, source_target_pairs={{0,8},{1,7},{4,12},{5,3},{8,14},{9,1},{12,10},{13,5},{14,6},{15,9}... | collective-permute-start | bytes 442376 | tf_op jit(solution)/shard_map/ppermute | solution.py:201
  47.0 3.5 %collective-permute-done.21.refs_5_ = bf16[24,3072]{1,0:T(8,128)(2,1)S(1)} collective-permute-done((bf16[24,3072]{1,0:T(8,128)(2,1)S(1)}, bf16[24,3072]{1,0:T(8,128)(2,1)S(1)}, u32[]{:S(2)}, u32[]{:S(2)}) %collective-permute-start.21) | collective-permute-done | bytes 147488 | tf_op jit(solution)/shard_map/ppermute | solution.py:201
  50.5 0.8 %collective-permute-done.23.refs_6_ = bf16[24,3072]{1,0:T(8,128)(2,1)S(1)} collective-permute-done((bf16[24,3072]{1,0:T(8,128)(2,1)S(1)}, bf16[24,3072]{1,0:T(8,128)(2,1)S(1)}, u32[]{:S(2)}, u32[]{:S(2)}) %collective-permute-start.23) | collective-permute-done | bytes 147488 | tf_op jit(solution)/shard_map/ppermute | solution.py:201
  51.3 1.5 %shard_map.75 = bf16[128,6144]{1,0:T(8,128)(2,1)} custom-call(s32[4,128]{1,0:T(4,128)S(1)} %bitcast.9, f32[4,128]{1,0:T(4,128)S(1)} %bitcast.10, bf16[24,128]{1,0:T(8,128)(2,1)S(1)} %get-tuple-element.18.refs_2_, bf16[24,128]{1,0:T(8,128)(2,1)S(1)} %get-tuple-element.19.refs_3_, bf16[24,3072]{1,0:T(8,128)(2,1)S(1)} %collective-permute-done.18.refs_4_, ...), custom_call_target="tpu_custom_call" | custom-call | bytes 3555328 | tf_op jit(solution)/shard_map/pallas_call | solution.py:171
  (55 shorter events, 3.4 us)
Async XLA Ops:
  2.0 5.8 %collective-permute-start.1 = (bf16[24,3072]{1,0:T(8,128)(2,1)S(1)}, bf16[24,3072]{1,0:T(8,128)(2,1)S(1)}, u32[]{:S(2)}, u32[]{:S(2)}) collective-permute-start(bf16[24,3072]{1,0:T(8,128)(2,1)S(1)} %shard_map.65.refs_0_), channel_id=1, source_target_pairs={{0,3},{1,4},{4,1},{5,8},{8,5},{9,12},{12,9},{13,14},{14,13},{15,10... | collective-permute-start | bytes 442376 | tf_op jit(solution)/shard_map/ppermute | solution.py:201
  4.5 7.7 %collective-permute-start.4 = (bf16[24,3072]{1,0:T(8,128)(2,1)S(1)}, bf16[24,3072]{1,0:T(8,128)(2,1)S(1)}, u32[]{:S(2)}, u32[]{:S(2)}) collective-permute-start(bf16[24,3072]{1,0:T(8,128)(2,1)S(1)} %shard_map.65.refs_0_), channel_id=1, source_target_pairs={{0,8},{1,7},{4,12},{5,3},{8,14},{9,1},{12,10},{13,5},{14,6},{15,9}... | collective-permute-start | bytes 442376 | tf_op jit(solution)/shard_map/ppermute | solution.py:201
  6.2 8.5 %collective-permute-start.2 = (bf16[24,3072]{1,0:T(8,128)(2,1)S(1)}, bf16[24,3072]{1,0:T(8,128)(2,1)S(1)}, u32[]{:S(2)}, u32[]{:S(2)}) collective-permute-start(bf16[24,3072]{1,0:T(8,128)(2,1)S(1)} %shard_map.65.refs_0_), channel_id=1, source_target_pairs={{0,4},{1,3},{4,8},{5,1},{8,12},{9,5},{12,14},{13,9},{14,10},{15,13... | collective-permute-start | bytes 442376 | tf_op jit(solution)/shard_map/ppermute | solution.py:201
  7.8 8.5 %collective-permute-start = (bf16[24,3072]{1,0:T(8,128)(2,1)S(1)}, bf16[24,3072]{1,0:T(8,128)(2,1)S(1)}, u32[]{:S(2)}, u32[]{:S(2)}) collective-permute-start(bf16[24,3072]{1,0:T(8,128)(2,1)S(1)} %shard_map.65.refs_0_), channel_id=1, source_target_pairs={{0,1},{1,0},{4,5},{5,4},{8,9},{9,8},{12,13},{13,12},{14,15},{15,14... | collective-permute-start | bytes 442376 | tf_op jit(solution)/shard_map/ppermute | solution.py:201
  7.8 8.5 %collective-permute-start.3 = (bf16[24,3072]{1,0:T(8,128)(2,1)S(1)}, bf16[24,3072]{1,0:T(8,128)(2,1)S(1)}, u32[]{:S(2)}, u32[]{:S(2)}) collective-permute-start(bf16[24,3072]{1,0:T(8,128)(2,1)S(1)} %collective-permute-done.1.refs_2_), channel_id=1, source_target_pairs={{0,4},{1,3},{4,8},{5,1},{8,12},{9,5},{12,14},{13,9},{14,10},{15,13... | collective-permute-start | bytes 442376 | tf_op jit(solution)/shard_map/ppermute | solution.py:201
  12.1 4.9 %collective-permute-start.12 = (bf16[24,3072]{1,0:T(8,128)(2,1)S(1)}, bf16[24,3072]{1,0:T(8,128)(2,1)S(1)}, u32[]{:S(2)}, u32[]{:S(2)}) collective-permute-start(bf16[24,3072]{1,0:T(8,128)(2,1)S(1)} %collective-permute-done.4.refs_5_), channel_id=1, source_target_pairs={{0,1},{1,0},{4,5},{5,4},{8,9},{9,8},{12,13},{13,12},{14,15},{15,14... | collective-permute-start | bytes 442376 | tf_op jit(solution)/shard_map/ppermute | solution.py:201
  12.3 7.7 %collective-permute-start.7 = (bf16[24,3072]{1,0:T(8,128)(2,1)S(1)}, bf16[24,3072]{1,0:T(8,128)(2,1)S(1)}, u32[]{:S(2)}, u32[]{:S(2)}) collective-permute-start(bf16[24,3072]{1,0:T(8,128)(2,1)S(1)} %collective-permute-done.4.refs_5_), channel_id=1, source_target_pairs={{0,8},{1,7},{4,12},{5,3},{8,14},{9,1},{12,10},{13,5},{14,6},{15,9}... | collective-permute-start | bytes 442376 | tf_op jit(solution)/shard_map/ppermute | solution.py:201
  14.7 6.0 %collective-permute-start.6 = (bf16[24,3072]{1,0:T(8,128)(2,1)S(1)}, bf16[24,3072]{1,0:T(8,128)(2,1)S(1)}, u32[]{:S(2)}, u32[]{:S(2)}) collective-permute-start(bf16[24,3072]{1,0:T(8,128)(2,1)S(1)} %collective-permute-done.4.refs_5_), channel_id=1, source_target_pairs={{0,4},{1,3},{4,8},{5,1},{8,12},{9,5},{12,14},{13,9},{14,10},{15,13... | collective-permute-start | bytes 442376 | tf_op jit(solution)/shard_map/ppermute | solution.py:201
  16.2 4.5 %collective-permute-start.10 = (bf16[24,3072]{1,0:T(8,128)(2,1)S(1)}, bf16[24,3072]{1,0:T(8,128)(2,1)S(1)}, u32[]{:S(2)}, u32[]{:S(2)}) collective-permute-start(bf16[24,3072]{1,0:T(8,128)(2,1)S(1)} %collective-permute-done.2.refs_3_), channel_id=1, source_target_pairs={{0,1},{1,0},{4,5},{5,4},{8,9},{9,8},{12,13},{13,12},{14,15},{15,14... | collective-permute-start | bytes 442376 | tf_op jit(solution)/shard_map/ppermute | solution.py:201
  16.3 6.0 %collective-permute-start.5 = (bf16[24,3072]{1,0:T(8,128)(2,1)S(1)}, bf16[24,3072]{1,0:T(8,128)(2,1)S(1)}, u32[]{:S(2)}, u32[]{:S(2)}) collective-permute-start(bf16[24,3072]{1,0:T(8,128)(2,1)S(1)} %collective-permute-done.3.refs_4_), channel_id=1, source_target_pairs={{0,4},{1,3},{4,8},{5,1},{8,12},{9,5},{12,14},{13,9},{14,10},{15,13... | collective-permute-start | bytes 442376 | tf_op jit(solution)/shard_map/ppermute | solution.py:201
  17.0 5.3 %collective-permute-start.9 = (bf16[24,3072]{1,0:T(8,128)(2,1)S(1)}, bf16[24,3072]{1,0:T(8,128)(2,1)S(1)}, u32[]{:S(2)}, u32[]{:S(2)}) collective-permute-start(bf16[24,3072]{1,0:T(8,128)(2,1)S(1)} %collective-permute-done.1.refs_2_), channel_id=1, source_target_pairs={{0,1},{1,0},{4,5},{5,4},{8,9},{9,8},{12,13},{13,12},{14,15},{15,14... | collective-permute-start | bytes 442376 | tf_op jit(solution)/shard_map/ppermute | solution.py:201
  20.0 2.3 %collective-permute-start.11 = (bf16[24,3072]{1,0:T(8,128)(2,1)S(1)}, bf16[24,3072]{1,0:T(8,128)(2,1)S(1)}, u32[]{:S(2)}, u32[]{:S(2)}) collective-permute-start(bf16[24,3072]{1,0:T(8,128)(2,1)S(1)} %collective-permute-done.3.refs_4_), channel_id=1, source_target_pairs={{0,1},{1,0},{4,5},{5,4},{8,9},{9,8},{12,13},{13,12},{14,15},{15,14... | collective-permute-start | bytes 442376 | tf_op jit(solution)/shard_map/ppermute | solution.py:201
  20.7 1.6 %collective-permute-start.8 = (bf16[24,3072]{1,0:T(8,128)(2,1)S(1)}, bf16[24,3072]{1,0:T(8,128)(2,1)S(1)}, u32[]{:S(2)}, u32[]{:S(2)}) collective-permute-start(bf16[24,3072]{1,0:T(8,128)(2,1)S(1)} %collective-permute-done.7.refs_8_), channel_id=1, source_target_pairs={{0,1},{1,0},{4,5},{5,4},{8,9},{9,8},{12,13},{13,12},{14,15},{15,14... | collective-permute-start | bytes 442376 | tf_op jit(solution)/shard_map/ppermute | solution.py:201
  20.7 1.6 %collective-permute-start.14 = (bf16[24,3072]{1,0:T(8,128)(2,1)S(1)}, bf16[24,3072]{1,0:T(8,128)(2,1)S(1)}, u32[]{:S(2)}, u32[]{:S(2)}) collective-permute-start(bf16[24,3072]{1,0:T(8,128)(2,1)S(1)} %collective-permute-done.6.refs_7_), channel_id=1, source_target_pairs={{0,1},{1,0},{4,5},{5,4},{8,9},{9,8},{12,13},{13,12},{14,15},{15,14... | collective-permute-start | bytes 442376 | tf_op jit(solution)/shard_map/ppermute | solution.py:201
  22.3 1.4 %collective-permute-start.13 = (bf16[24,3072]{1,0:T(8,128)(2,1)S(1)}, bf16[24,3072]{1,0:T(8,128)(2,1)S(1)}, u32[]{:S(2)}, u32[]{:S(2)}) collective-permute-start(bf16[24,3072]{1,0:T(8,128)(2,1)S(1)} %collective-permute-done.5.refs_6_), channel_id=1, source_target_pairs={{0,1},{1,0},{4,5},{5,4},{8,9},{9,8},{12,13},{13,12},{14,15},{15,14... | collective-permute-start | bytes 442376 | tf_op jit(solution)/shard_map/ppermute | solution.py:201
  31.0 1.9 %collective-permute-start.15 = (bf16[72,3072]{1,0:T(8,128)(2,1)S(1)}, bf16[72,3072]{1,0:T(8,128)(2,1)S(1)}, u32[]{:S(2)}, u32[]{:S(2)}) collective-permute-start(bf16[72,3072]{1,0:T(8,128)(2,1)S(1)} %get-tuple-element.23), channel_id=1, source_target_pairs={{0,1},{1,0},{4,5},{5,4},{8,9},{9,8},{12,13},{13,12},{14,15},{15,14... | collective-permute-start | bytes 1327112 | tf_op jit(solution)/shard_map/ppermute | solution.py:201
  32.9 4.4 %collective-permute-start.16 = (bf16[120,3072]{1,0:T(8,128)(2,1)S(1)}, bf16[120,3072]{1,0:T(8,128)(2,1)S(1)}, u32[]{:S(2)}, u32[]{:S(2)}) collective-permute-start(bf16[120,3072]{1,0:T(8,128)(2,1)S(1)} %get-tuple-element.24), channel_id=1, source_target_pairs={{0,1},{1,0},{4,5},{5,4},{8,9},{9,8},{12,13},{13,12},{14,15},{15,14... | collective-permute-start | bytes 2211848 | tf_op jit(solution)/shard_map/ppermute | solution.py:201
  33.2 6.1 %collective-permute-start.17 = (bf16[24,3072]{1,0:T(8,128)(2,1)S(1)}, bf16[24,3072]{1,0:T(8,128)(2,1)S(1)}, u32[]{:S(2)}, u32[]{:S(2)}) collective-permute-start(bf16[24,3072]{1,0:T(8,128)(2,1)S(1)} %shard_map.68), channel_id=1, source_target_pairs={{0,4},{1,3},{4,8},{5,1},{8,12},{9,5},{12,14},{13,9},{14,10},{15,13... | collective-permute-start | bytes 442376 | tf_op jit(solution)/shard_map/ppermute | solution.py:201
  35.1 7.7 %collective-permute-start.19 = (bf16[24,3072]{1,0:T(8,128)(2,1)S(1)}, bf16[24,3072]{1,0:T(8,128)(2,1)S(1)}, u32[]{:S(2)}, u32[]{:S(2)}) collective-permute-start(bf16[24,3072]{1,0:T(8,128)(2,1)S(1)} %shard_map.69), channel_id=1, source_target_pairs={{0,8},{1,7},{4,12},{5,3},{8,14},{9,1},{12,10},{13,5},{14,6},{15,9}... | collective-permute-start | bytes 442376 | tf_op jit(solution)/shard_map/ppermute | solution.py:201
  37.2 6.0 %collective-permute-start.20 = (bf16[24,3072]{1,0:T(8,128)(2,1)S(1)}, bf16[24,3072]{1,0:T(8,128)(2,1)S(1)}, u32[]{:S(2)}, u32[]{:S(2)}) collective-permute-start(bf16[24,3072]{1,0:T(8,128)(2,1)S(1)} %shard_map.70), channel_id=1, source_target_pairs={{0,4},{1,3},{4,8},{5,1},{8,12},{9,5},{12,14},{13,9},{14,10},{15,13... | collective-permute-start | bytes 442376 | tf_op jit(solution)/shard_map/ppermute | solution.py:201
  39.3 7.2 %collective-permute-start.22 = (bf16[24,3072]{1,0:T(8,128)(2,1)S(1)}, bf16[24,3072]{1,0:T(8,128)(2,1)S(1)}, u32[]{:S(2)}, u32[]{:S(2)}) collective-permute-start(bf16[24,3072]{1,0:T(8,128)(2,1)S(1)} %shard_map.71), channel_id=1, source_target_pairs={{0,4},{1,3},{4,8},{5,1},{8,12},{9,5},{12,14},{13,9},{14,10},{15,13... | collective-permute-start | bytes 442376 | tf_op jit(solution)/shard_map/ppermute | solution.py:201
  41.8 5.2 %collective-permute-start.18 = (bf16[24,3072]{1,0:T(8,128)(2,1)S(1)}, bf16[24,3072]{1,0:T(8,128)(2,1)S(1)}, u32[]{:S(2)}, u32[]{:S(2)}) collective-permute-start(bf16[24,3072]{1,0:T(8,128)(2,1)S(1)} %shard_map.72), channel_id=1, source_target_pairs={{0,4},{1,3},{4,8},{5,1},{8,12},{9,5},{12,14},{13,9},{14,10},{15,13... | collective-permute-start | bytes 442376 | tf_op jit(solution)/shard_map/ppermute | solution.py:201
  43.3 7.1 %collective-permute-start.21 = (bf16[24,3072]{1,0:T(8,128)(2,1)S(1)}, bf16[24,3072]{1,0:T(8,128)(2,1)S(1)}, u32[]{:S(2)}, u32[]{:S(2)}) collective-permute-start(bf16[24,3072]{1,0:T(8,128)(2,1)S(1)} %shard_map.73), channel_id=1, source_target_pairs={{0,8},{1,7},{4,12},{5,3},{8,14},{9,1},{12,10},{13,5},{14,6},{15,9}... | collective-permute-start | bytes 442376 | tf_op jit(solution)/shard_map/ppermute | solution.py:201
  46.5 4.8 %collective-permute-start.23 = (bf16[24,3072]{1,0:T(8,128)(2,1)S(1)}, bf16[24,3072]{1,0:T(8,128)(2,1)S(1)}, u32[]{:S(2)}, u32[]{:S(2)}) collective-permute-start(bf16[24,3072]{1,0:T(8,128)(2,1)S(1)} %shard_map.74), channel_id=1, source_target_pairs={{0,5},{1,2},{4,9},{5,0},{8,13},{9,4},{12,15},{13,8},{14,11},{15,12... | collective-permute-start | bytes 442376 | tf_op jit(solution)/shard_map/ppermute | solution.py:201
  (8 other events, 181.1 us)

commit v8 on v7

--- a/solution.py
+++ b/solution.py
@@ -67,7 +67,7 @@
                 )
             )
     for copy in copies:
-        copy.start()
+        copy.start(priority=1)
     copies[0].wait()
     choosers = choose(ids_here[...])
     upper_ref[...], lower_ref[...] = choosers
@@ -87,26 +87,27 @@
     out_ref[...] = in_ref[...]
 
 
+def share_kernel(ids_ref, gates_ref, out_ref):
+    share = jnp.sum(jnp.where(ids_ref[...] == 0, gates_ref[...], 0.0), axis=0, keepdims=True)
+    out_ref[...] = jnp.broadcast_to(share, out_ref.shape).T
+
+
 def hidden_kernel(blocks, *refs):
     arrays, (gate_ref, up_ref, out_ref, first, second) = refs[:-5], refs[-5:]
-    units, width = gate_ref.shape
-    half = width // 2
+    half = gate_ref.shape[1] // 2
     for j, (i, row) in enumerate(blocks):
         first[j * CAP : (j + 1) * CAP, :] = arrays[i][row : row + CAP, :]
         second[j * CAP : (j + 1) * CAP, :] = arrays[i][row + CAP : row + PAIR, :]
     contract = (((1,), (1,)), ((), ()))
 
-    def product(ref, here):
+    def product(ref):
         return lax.dot_general(
-            first[...], ref[here, :half], contract, preferred_element_type=F32
-        ) + lax.dot_general(second[...], ref[here, half:], contract, preferred_element_type=F32)
-
-    tile = 224 if units % 224 == 0 else units
-    for start in range(0, units, tile):
-        here = slice(start, start + tile)
-        gate = product(gate_ref, here)
-        up = product(up_ref, here)
-        out_ref[:, here] = (gate / (1.0 + jnp.exp(-gate)) * up).astype(BF16)
+            first[...], ref[:, :half], contract, preferred_element_type=F32
+        ) + lax.dot_general(second[...], ref[:, half:], contract, preferred_element_type=F32)
+
+    gate = product(gate_ref)
+    up = product(up_ref)
+    out_ref[...] = (gate / (1.0 + jnp.exp(-gate)) * up).astype(BF16)
 
 
 def down_kernel(places, hidden_ref, down_ref, *out_refs):
@@ -136,14 +137,11 @@
     out_ref[...] = total.astype(out_ref.dtype)
 
 
-def mix_kernel(blocks, ids_ref, gates_ref, upper_ref, lower_ref, *refs):
+def mix_kernel(blocks, share_ref, upper_ref, lower_ref, *refs):
     (*arrays, out_ref, values, written) = refs
     half = values.shape[1] // 2
     tile = half // 3
-    ids = ids_ref[...]
-    tokens = ids.shape[1]
-    share = jnp.sum(jnp.where(ids == 0, gates_ref[...], 0.0), axis=0, keepdims=True)
-    share = jnp.broadcast_to(share, (tokens, tokens)).T[:, :1]
+    share = share_ref[:, :1]
     choosers = (upper_ref[...], lower_ref[...])
     copies = []
     for step in range(3):
@@ -247,6 +245,7 @@
             blocks.append(found[kind, distance])
 
     arrays, where = distinct(blocks)
+    share = call(share_kernel, struct((count, count), F32), ids, gates.T)
     hidden = call(
         lambda *refs: hidden_kernel(where, *refs),
         struct((rows, units), BF16),
@@ -316,12 +315,14 @@
         else:
             deliver("one", cross, "cross", distance - 1)
             deliver("two", total("like", distance), "like", distance - 2)
-    arrays, mixed = distinct(arrived + terms("like", 0))
+    early = arrived[:1] + terms("like", 0)
+    arrays, where = distinct(early)
+    early = call(lambda *refs: sum_kernel(where, *refs), struct((PAIR, half), F32), *arrays)
+    arrays, mixed = distinct(arrived[1:] + [block(early)])
     return call(
         lambda *refs: mix_kernel(mixed, *refs),
         struct(tokens.shape, BF16),
-        ids,
-        gates.T,
+        share,
         *choosers,
         *arrays,
         out_specs=pl.BlockSpec(memory_space=pl.ANY),

time: 52.9 us -> 52.7 us (level)
  waiting for transfers between devices: 17.9 us -> 17.3 us
    ppermute x24, waiting for transfers between devices: 17.9 us -> 17.3 us  [move(): return lax.ppermute(a.astype(BF16), 'tensor', steps[kind])]
    pallas_call x12 -> x14, Pallas kernels: 11 us -> 11.2 us  [call(): pl.pallas_call(kernel, out_shape=out_shape, scratch_shapes=list(scratch),...]
  transfers between devices with their start and end apart: 24 -> 24, of which waited for: 12 -> 14; matrix products, arithmetic and copies ran while one was open for 0% -> 0% of each run, Pallas kernels for 1% -> 1%
where the time goes in v8:
time: 52.7 us; the launch traced here: 52.5 us
  starting transfers between devices  23.9 us (45%)
  waiting for transfers between devices  17.3 us (33%)
  Pallas kernels  11.2 us (21%)
    ppermute x24, starting transfers between devices, move(): return lax.ppermute(a.astype(BF16), 'tensor', steps[kind])  23.9 us
    ppermute x24, waiting for transfers between devices, move(): return lax.ppermute(a.astype(BF16), 'tensor', steps[kind])  17.3 us
    pallas_call x14, Pallas kernels, call(): pl.pallas_call(kernel, out_shape=out_shape, scratch_shapes=list(scratch),...  11.2 us
  transfers between devices with their start and end apart: 24, of which 14 were waited for; matrix products, arithmetic and copies ran while one was open for 0% of the time, Pallas kernels for 1%

profile of v8, /device:TPU:0, one launch (start us, length us, event | category | flops | bytes accessed | tf_op | source)
XLA Modules:
  0.0 52.5 jit_solution(11768334309767650606)
XLA Ops:
  0.0 1.9 %shard_map.65 = (bf16[24,3072]{1,0:T(8,128)(2,1)S(1)}, bf16[24,128]{1,0:T(8,128)(2,1)S(1)}, bf16[24,128]{1,0:T(8,128)(2,1)S(1)}) custom-call(s32[4,128]{1,0:T(4,128)} %bitcast.8, bf16[128,6144]{1,0:T(8,128)(2,1)} %tokens_ref.1), custom_call_target="tpu_custom_call" | custom-call | bytes 1574912 | tf_op jit(solution)/shard_map/pallas_call | solution.py:169
  2.0 2.5 %collective-permute-start.1 = (bf16[24,3072]{1,0:T(8,128)(2,1)S(1)}, bf16[24,3072]{1,0:T(8,128)(2,1)S(1)}, u32[]{:S(2)}, u32[]{:S(2)}) collective-permute-start(bf16[24,3072]{1,0:T(8,128)(2,1)S(1)} %shard_map.66.refs_0_), channel_id=1, source_target_pairs={{0,3},{1,4},{4,1},{5,8},{8,5},{9,12},{12,9},{13,14},{14,13},{15,10... | collective-permute-start | bytes 442376 | tf_op jit(solution)/shard_map/ppermute | solution.py:199
  4.5 1.7 %collective-permute-start.4 = (bf16[24,3072]{1,0:T(8,128)(2,1)S(1)}, bf16[24,3072]{1,0:T(8,128)(2,1)S(1)}, u32[]{:S(2)}, u32[]{:S(2)}) collective-permute-start(bf16[24,3072]{1,0:T(8,128)(2,1)S(1)} %shard_map.66.refs_0_), channel_id=1, source_target_pairs={{0,8},{1,7},{4,12},{5,3},{8,14},{9,1},{12,10},{13,5},{14,6},{15,9}... | collective-permute-start | bytes 442376 | tf_op jit(solution)/shard_map/ppermute | solution.py:199
  6.2 1.6 %collective-permute-start.2 = (bf16[24,3072]{1,0:T(8,128)(2,1)S(1)}, bf16[24,3072]{1,0:T(8,128)(2,1)S(1)}, u32[]{:S(2)}, u32[]{:S(2)}) collective-permute-start(bf16[24,3072]{1,0:T(8,128)(2,1)S(1)} %shard_map.66.refs_0_), channel_id=1, source_target_pairs={{0,4},{1,3},{4,8},{5,1},{8,12},{9,5},{12,14},{13,9},{14,10},{15,13... | collective-permute-start | bytes 442376 | tf_op jit(solution)/shard_map/ppermute | solution.py:199
  7.8 1.9 %collective-permute-start.3 = (bf16[24,3072]{1,0:T(8,128)(2,1)S(1)}, bf16[24,3072]{1,0:T(8,128)(2,1)S(1)}, u32[]{:S(2)}, u32[]{:S(2)}) collective-permute-start(bf16[24,3072]{1,0:T(8,128)(2,1)S(1)} %collective-permute-done.1.refs_2_), channel_id=1, source_target_pairs={{0,4},{1,3},{4,8},{5,1},{8,12},{9,5},{12,14},{13,9},{14,10},{15,13... | collective-permute-start | bytes 442376 | tf_op jit(solution)/shard_map/ppermute | solution.py:199
  9.7 2.5 %collective-permute-done.4.refs_5_ = bf16[24,3072]{1,0:T(8,128)(2,1)S(1)} collective-permute-done((bf16[24,3072]{1,0:T(8,128)(2,1)S(1)}, bf16[24,3072]{1,0:T(8,128)(2,1)S(1)}, u32[]{:S(2)}, u32[]{:S(2)}) %collective-permute-start.4) | collective-permute-done | bytes 147488 | tf_op jit(solution)/shard_map/ppermute | solution.py:199
  12.1 2.0 %collective-permute-start.6 = (bf16[24,3072]{1,0:T(8,128)(2,1)S(1)}, bf16[24,3072]{1,0:T(8,128)(2,1)S(1)}, u32[]{:S(2)}, u32[]{:S(2)}) collective-permute-start(bf16[24,3072]{1,0:T(8,128)(2,1)S(1)} %collective-permute-done.4.refs_5_), channel_id=1, source_target_pairs={{0,4},{1,3},{4,8},{5,1},{8,12},{9,5},{12,14},{13,9},{14,10},{15,13... | collective-permute-start | bytes 442376 | tf_op jit(solution)/shard_map/ppermute | solution.py:199
  14.2 1.2 %collective-permute-start.7 = (bf16[24,3072]{1,0:T(8,128)(2,1)S(1)}, bf16[24,3072]{1,0:T(8,128)(2,1)S(1)}, u32[]{:S(2)}, u32[]{:S(2)}) collective-permute-start(bf16[24,3072]{1,0:T(8,128)(2,1)S(1)} %collective-permute-done.4.refs_5_), channel_id=1, source_target_pairs={{0,8},{1,7},{4,12},{5,3},{8,14},{9,1},{12,10},{13,5},{14,6},{15,9}... | collective-permute-start | bytes 442376 | tf_op jit(solution)/shard_map/ppermute | solution.py:199
  15.9 1.5 %collective-permute-start.5 = (bf16[24,3072]{1,0:T(8,128)(2,1)S(1)}, bf16[24,3072]{1,0:T(8,128)(2,1)S(1)}, u32[]{:S(2)}, u32[]{:S(2)}) collective-permute-start(bf16[24,3072]{1,0:T(8,128)(2,1)S(1)} %collective-permute-done.3.refs_4_), channel_id=1, source_target_pairs={{0,4},{1,3},{4,8},{5,1},{8,12},{9,5},{12,14},{13,9},{14,10},{15,13... | collective-permute-start | bytes 442376 | tf_op jit(solution)/shard_map/ppermute | solution.py:199
  18.0 3.8 %collective-permute-done.7.refs_8_ = bf16[24,3072]{1,0:T(8,128)(2,1)S(1)} collective-permute-done((bf16[24,3072]{1,0:T(8,128)(2,1)S(1)}, bf16[24,3072]{1,0:T(8,128)(2,1)S(1)}, u32[]{:S(2)}, u32[]{:S(2)}) %collective-permute-start.7) | collective-permute-done | bytes 147488 | tf_op jit(solution)/shard_map/ppermute | solution.py:199
  24.0 5.2 %shard_map.67.refs_0_ = bf16[192,672]{1,0:T(8,128)(2,1)S(1)} custom-call(bf16[24,3072]{1,0:T(8,128)(2,1)S(1)} %shard_map.66.refs_0_, bf16[24,3072]{1,0:T(8,128)(2,1)S(1)} %collective-permute-done.refs_1_, bf16[24,3072]{1,0:T(8,128)(2,1)S(1)} %collective-permute-done.1.refs_2_, bf16[24,3072]{1,0:T(8,128)(2,1)S(1)} %collective-permute-done.2.refs_3_, ...), custom_call_target="tpu_custom_call" | custom-call | flops 3170893824 | bytes 18874368 | tf_op jit(solution)/shard_map/pallas_call | solution.py:169
  29.2 2.0 %shard_map.68 = (f32[192,3072]{1,0:T(8,128)S(1)}, bf16[72,3072]{1,0:T(8,128)(2,1)S(1)}, bf16[120,3072]{1,0:T(8,128)(2,1)S(1)}) custom-call(bf16[192,672]{1,0:T(8,128)(2,1)S(1)} %shard_map.67.refs_0_, bf16[672,6144]{1,0:T(8,128)(2,1)S(1)} %bitcast.7), custom_call_target="tpu_custom_call" | custom-call | flops 1585446912 | bytes 8515584 | tf_op jit(solution)/shard_map/pallas_call | solution.py:169
  31.6 1.5 %collective-permute-done.15.refs_1_ = bf16[72,3072]{1,0:T(8,128)(2,1)S(1)} collective-permute-done((bf16[72,3072]{1,0:T(8,128)(2,1)S(1)}, bf16[72,3072]{1,0:T(8,128)(2,1)S(1)}, u32[]{:S(2)}, u32[]{:S(2)}) %collective-permute-start.15) | collective-permute-done | bytes 442400 | tf_op jit(solution)/shard_map/ppermute | solution.py:199
  33.6 1.0 %collective-permute-start.20 = (bf16[24,3072]{1,0:T(8,128)(2,1)S(1)}, bf16[24,3072]{1,0:T(8,128)(2,1)S(1)}, u32[]{:S(2)}, u32[]{:S(2)}) collective-permute-start(bf16[24,3072]{1,0:T(8,128)(2,1)S(1)} %shard_map.69), channel_id=1, source_target_pairs={{0,4},{1,3},{4,8},{5,1},{8,12},{9,5},{12,14},{13,9},{14,10},{15,13... | collective-permute-start | bytes 442376 | tf_op jit(solution)/shard_map/ppermute | solution.py:199
  34.6 2.4 %collective-permute-start.17 = (bf16[24,3072]{1,0:T(8,128)(2,1)S(1)}, bf16[24,3072]{1,0:T(8,128)(2,1)S(1)}, u32[]{:S(2)}, u32[]{:S(2)}) collective-permute-start(bf16[24,3072]{1,0:T(8,128)(2,1)S(1)} %shard_map.70), channel_id=1, source_target_pairs={{0,8},{1,7},{4,12},{5,3},{8,14},{9,1},{12,10},{13,5},{14,6},{15,9}... | collective-permute-start | bytes 442376 | tf_op jit(solution)/shard_map/ppermute | solution.py:199
  37.0 0.7 %collective-permute-start.18 = (bf16[24,3072]{1,0:T(8,128)(2,1)S(1)}, bf16[24,3072]{1,0:T(8,128)(2,1)S(1)}, u32[]{:S(2)}, u32[]{:S(2)}) collective-permute-start(bf16[24,3072]{1,0:T(8,128)(2,1)S(1)} %shard_map.71), channel_id=1, source_target_pairs={{0,4},{1,3},{4,8},{5,1},{8,12},{9,5},{12,14},{13,9},{14,10},{15,13... | collective-permute-start | bytes 442376 | tf_op jit(solution)/shard_map/ppermute | solution.py:199
  37.8 1.0 %collective-permute-done.20.refs_2_ = bf16[24,3072]{1,0:T(8,128)(2,1)S(1)} collective-permute-done((bf16[24,3072]{1,0:T(8,128)(2,1)S(1)}, bf16[24,3072]{1,0:T(8,128)(2,1)S(1)}, u32[]{:S(2)}, u32[]{:S(2)}) %collective-permute-start.20) | collective-permute-done | bytes 147488 | tf_op jit(solution)/shard_map/ppermute | solution.py:199
  38.8 1.9 %collective-permute-start.21 = (bf16[24,3072]{1,0:T(8,128)(2,1)S(1)}, bf16[24,3072]{1,0:T(8,128)(2,1)S(1)}, u32[]{:S(2)}, u32[]{:S(2)}) collective-permute-start(bf16[24,3072]{1,0:T(8,128)(2,1)S(1)} %shard_map.73), channel_id=1, source_target_pairs={{0,4},{1,3},{4,8},{5,1},{8,12},{9,5},{12,14},{13,9},{14,10},{15,13... | collective-permute-start | bytes 442376 | tf_op jit(solution)/shard_map/ppermute | solution.py:199
  40.8 0.7 %collective-permute-start.23 = (bf16[24,3072]{1,0:T(8,128)(2,1)S(1)}, bf16[24,3072]{1,0:T(8,128)(2,1)S(1)}, u32[]{:S(2)}, u32[]{:S(2)}) collective-permute-start(bf16[24,3072]{1,0:T(8,128)(2,1)S(1)} %shard_map.74), channel_id=1, source_target_pairs={{0,4},{1,3},{4,8},{5,1},{8,12},{9,5},{12,14},{13,9},{14,10},{15,13... | collective-permute-start | bytes 442376 | tf_op jit(solution)/shard_map/ppermute | solution.py:199
  41.4 1.5 %collective-permute-done.17.refs_2_ = bf16[24,3072]{1,0:T(8,128)(2,1)S(1)} collective-permute-done((bf16[24,3072]{1,0:T(8,128)(2,1)S(1)}, bf16[24,3072]{1,0:T(8,128)(2,1)S(1)}, u32[]{:S(2)}, u32[]{:S(2)}) %collective-permute-start.17) | collective-permute-done | bytes 147488 | tf_op jit(solution)/shard_map/ppermute | solution.py:199
  43.1 2.5 %collective-permute-start.19 = (bf16[24,3072]{1,0:T(8,128)(2,1)S(1)}, bf16[24,3072]{1,0:T(8,128)(2,1)S(1)}, u32[]{:S(2)}, u32[]{:S(2)}) collective-permute-start(bf16[24,3072]{1,0:T(8,128)(2,1)S(1)} %shard_map.72), channel_id=1, source_target_pairs={{0,8},{1,7},{4,12},{5,3},{8,14},{9,1},{12,10},{13,5},{14,6},{15,9}... | collective-permute-start | bytes 442376 | tf_op jit(solution)/shard_map/ppermute | solution.py:199
  46.3 3.9 %collective-permute-done.19.refs_3_ = bf16[24,3072]{1,0:T(8,128)(2,1)S(1)} collective-permute-done((bf16[24,3072]{1,0:T(8,128)(2,1)S(1)}, bf16[24,3072]{1,0:T(8,128)(2,1)S(1)}, u32[]{:S(2)}, u32[]{:S(2)}) %collective-permute-start.19) | collective-permute-done | bytes 147488 | tf_op jit(solution)/shard_map/ppermute | solution.py:199
  50.2 0.9 %collective-permute-done.22.refs_4_ = bf16[24,3072]{1,0:T(8,128)(2,1)S(1)} collective-permute-done((bf16[24,3072]{1,0:T(8,128)(2,1)S(1)}, bf16[24,3072]{1,0:T(8,128)(2,1)S(1)}, u32[]{:S(2)}, u32[]{:S(2)}) %collective-permute-start.22) | collective-permute-done | bytes 147488 | tf_op jit(solution)/shard_map/ppermute | solution.py:199
  51.1 1.5 %shard_map.77 = bf16[128,6144]{1,0:T(8,128)(2,1)} custom-call(f32[128,128]{1,0:T(8,128)S(1)} %shard_map.64.refs_0_, bf16[24,128]{1,0:T(8,128)(2,1)S(1)} %get-tuple-element.18.refs_1_, bf16[24,128]{1,0:T(8,128)(2,1)S(1)} %get-tuple-element.19.refs_2_, bf16[24,3072]{1,0:T(8,128)(2,1)S(1)} %collective-permute-done.19.refs_3_, ...), custom_call_target="tpu_custom_call" | custom-call | bytes 667648 | tf_op jit(solution)/shard_map/pallas_call | solution.py:169
  (57 shorter events, 5.0 us)
Async XLA Ops:
  2.0 5.8 %collective-permute-start.1 = (bf16[24,3072]{1,0:T(8,128)(2,1)S(1)}, bf16[24,3072]{1,0:T(8,128)(2,1)S(1)}, u32[]{:S(2)}, u32[]{:S(2)}) collective-permute-start(bf16[24,3072]{1,0:T(8,128)(2,1)S(1)} %shard_map.66.refs_0_), channel_id=1, source_target_pairs={{0,3},{1,4},{4,1},{5,8},{8,5},{9,12},{12,9},{13,14},{14,13},{15,10... | collective-permute-start | bytes 442376 | tf_op jit(solution)/shard_map/ppermute | solution.py:199
  4.5 7.7 %collective-permute-start.4 = (bf16[24,3072]{1,0:T(8,128)(2,1)S(1)}, bf16[24,3072]{1,0:T(8,128)(2,1)S(1)}, u32[]{:S(2)}, u32[]{:S(2)}) collective-permute-start(bf16[24,3072]{1,0:T(8,128)(2,1)S(1)} %shard_map.66.refs_0_), channel_id=1, source_target_pairs={{0,8},{1,7},{4,12},{5,3},{8,14},{9,1},{12,10},{13,5},{14,6},{15,9}... | collective-permute-start | bytes 442376 | tf_op jit(solution)/shard_map/ppermute | solution.py:199
  6.2 9.2 %collective-permute-start.2 = (bf16[24,3072]{1,0:T(8,128)(2,1)S(1)}, bf16[24,3072]{1,0:T(8,128)(2,1)S(1)}, u32[]{:S(2)}, u32[]{:S(2)}) collective-permute-start(bf16[24,3072]{1,0:T(8,128)(2,1)S(1)} %shard_map.66.refs_0_), channel_id=1, source_target_pairs={{0,4},{1,3},{4,8},{5,1},{8,12},{9,5},{12,14},{13,9},{14,10},{15,13... | collective-permute-start | bytes 442376 | tf_op jit(solution)/shard_map/ppermute | solution.py:199
  7.8 7.6 %collective-permute-start = (bf16[24,3072]{1,0:T(8,128)(2,1)S(1)}, bf16[24,3072]{1,0:T(8,128)(2,1)S(1)}, u32[]{:S(2)}, u32[]{:S(2)}) collective-permute-start(bf16[24,3072]{1,0:T(8,128)(2,1)S(1)} %shard_map.66.refs_0_), channel_id=1, source_target_pairs={{0,1},{1,0},{4,5},{5,4},{8,9},{9,8},{12,13},{13,12},{14,15},{15,14... | collective-permute-start | bytes 442376 | tf_op jit(solution)/shard_map/ppermute | solution.py:199
  7.8 8.1 %collective-permute-start.3 = (bf16[24,3072]{1,0:T(8,128)(2,1)S(1)}, bf16[24,3072]{1,0:T(8,128)(2,1)S(1)}, u32[]{:S(2)}, u32[]{:S(2)}) collective-permute-start(bf16[24,3072]{1,0:T(8,128)(2,1)S(1)} %collective-permute-done.1.refs_2_), channel_id=1, source_target_pairs={{0,4},{1,3},{4,8},{5,1},{8,12},{9,5},{12,14},{13,9},{14,10},{15,13... | collective-permute-start | bytes 442376 | tf_op jit(solution)/shard_map/ppermute | solution.py:199
  12.1 5.8 %collective-permute-start.6 = (bf16[24,3072]{1,0:T(8,128)(2,1)S(1)}, bf16[24,3072]{1,0:T(8,128)(2,1)S(1)}, u32[]{:S(2)}, u32[]{:S(2)}) collective-permute-start(bf16[24,3072]{1,0:T(8,128)(2,1)S(1)} %collective-permute-done.4.refs_5_), channel_id=1, source_target_pairs={{0,4},{1,3},{4,8},{5,1},{8,12},{9,5},{12,14},{13,9},{14,10},{15,13... | collective-permute-start | bytes 442376 | tf_op jit(solution)/shard_map/ppermute | solution.py:199
  14.2 7.6 %collective-permute-start.7 = (bf16[24,3072]{1,0:T(8,128)(2,1)S(1)}, bf16[24,3072]{1,0:T(8,128)(2,1)S(1)}, u32[]{:S(2)}, u32[]{:S(2)}) collective-permute-start(bf16[24,3072]{1,0:T(8,128)(2,1)S(1)} %collective-permute-done.4.refs_5_), channel_id=1, source_target_pairs={{0,8},{1,7},{4,12},{5,3},{8,14},{9,1},{12,10},{13,5},{14,6},{15,9}... | collective-permute-start | bytes 442376 | tf_op jit(solution)/shard_map/ppermute | solution.py:199
  15.4 6.5 %collective-permute-start.12 = (bf16[24,3072]{1,0:T(8,128)(2,1)S(1)}, bf16[24,3072]{1,0:T(8,128)(2,1)S(1)}, u32[]{:S(2)}, u32[]{:S(2)}) collective-permute-start(bf16[24,3072]{1,0:T(8,128)(2,1)S(1)} %collective-permute-done.4.refs_5_), channel_id=1, source_target_pairs={{0,1},{1,0},{4,5},{5,4},{8,9},{9,8},{12,13},{13,12},{14,15},{15,14... | collective-permute-start | bytes 442376 | tf_op jit(solution)/shard_map/ppermute | solution.py:199
  15.4 7.0 %collective-permute-start.9 = (bf16[24,3072]{1,0:T(8,128)(2,1)S(1)}, bf16[24,3072]{1,0:T(8,128)(2,1)S(1)}, u32[]{:S(2)}, u32[]{:S(2)}) collective-permute-start(bf16[24,3072]{1,0:T(8,128)(2,1)S(1)} %collective-permute-done.1.refs_2_), channel_id=1, source_target_pairs={{0,1},{1,0},{4,5},{5,4},{8,9},{9,8},{12,13},{13,12},{14,15},{15,14... | collective-permute-start | bytes 442376 | tf_op jit(solution)/shard_map/ppermute | solution.py:199
  15.9 6.5 %collective-permute-start.5 = (bf16[24,3072]{1,0:T(8,128)(2,1)S(1)}, bf16[24,3072]{1,0:T(8,128)(2,1)S(1)}, u32[]{:S(2)}, u32[]{:S(2)}) collective-permute-start(bf16[24,3072]{1,0:T(8,128)(2,1)S(1)} %collective-permute-done.3.refs_4_), channel_id=1, source_target_pairs={{0,4},{1,3},{4,8},{5,1},{8,12},{9,5},{12,14},{13,9},{14,10},{15,13... | collective-permute-start | bytes 442376 | tf_op jit(solution)/shard_map/ppermute | solution.py:199
  18.0 4.9 %collective-permute-start.10 = (bf16[24,3072]{1,0:T(8,128)(2,1)S(1)}, bf16[24,3072]{1,0:T(8,128)(2,1)S(1)}, u32[]{:S(2)}, u32[]{:S(2)}) collective-permute-start(bf16[24,3072]{1,0:T(8,128)(2,1)S(1)} %collective-permute-done.2.refs_3_), channel_id=1, source_target_pairs={{0,1},{1,0},{4,5},{5,4},{8,9},{9,8},{12,13},{13,12},{14,15},{15,14... | collective-permute-start | bytes 442376 | tf_op jit(solution)/shard_map/ppermute | solution.py:199
  21.8 1.4 %collective-permute-start.11 = (bf16[24,3072]{1,0:T(8,128)(2,1)S(1)}, bf16[24,3072]{1,0:T(8,128)(2,1)S(1)}, u32[]{:S(2)}, u32[]{:S(2)}) collective-permute-start(bf16[24,3072]{1,0:T(8,128)(2,1)S(1)} %collective-permute-done.3.refs_4_), channel_id=1, source_target_pairs={{0,1},{1,0},{4,5},{5,4},{8,9},{9,8},{12,13},{13,12},{14,15},{15,14... | collective-permute-start | bytes 442376 | tf_op jit(solution)/shard_map/ppermute | solution.py:199
  21.8 1.6 %collective-permute-start.14 = (bf16[24,3072]{1,0:T(8,128)(2,1)S(1)}, bf16[24,3072]{1,0:T(8,128)(2,1)S(1)}, u32[]{:S(2)}, u32[]{:S(2)}) collective-permute-start(bf16[24,3072]{1,0:T(8,128)(2,1)S(1)} %collective-permute-done.6.refs_7_), channel_id=1, source_target_pairs={{0,1},{1,0},{4,5},{5,4},{8,9},{9,8},{12,13},{13,12},{14,15},{15,14... | collective-permute-start | bytes 442376 | tf_op jit(solution)/shard_map/ppermute | solution.py:199
  22.3 1.4 %collective-permute-start.8 = (bf16[24,3072]{1,0:T(8,128)(2,1)S(1)}, bf16[24,3072]{1,0:T(8,128)(2,1)S(1)}, u32[]{:S(2)}, u32[]{:S(2)}) collective-permute-start(bf16[24,3072]{1,0:T(8,128)(2,1)S(1)} %collective-permute-done.7.refs_8_), channel_id=1, source_target_pairs={{0,1},{1,0},{4,5},{5,4},{8,9},{9,8},{12,13},{13,12},{14,15},{15,14... | collective-permute-start | bytes 442376 | tf_op jit(solution)/shard_map/ppermute | solution.py:199
  22.4 1.5 %collective-permute-start.13 = (bf16[24,3072]{1,0:T(8,128)(2,1)S(1)}, bf16[24,3072]{1,0:T(8,128)(2,1)S(1)}, u32[]{:S(2)}, u32[]{:S(2)}) collective-permute-start(bf16[24,3072]{1,0:T(8,128)(2,1)S(1)} %collective-permute-done.5.refs_6_), channel_id=1, source_target_pairs={{0,1},{1,0},{4,5},{5,4},{8,9},{9,8},{12,13},{13,12},{14,15},{15,14... | collective-permute-start | bytes 442376 | tf_op jit(solution)/shard_map/ppermute | solution.py:199
  31.3 1.9 %collective-permute-start.15 = (bf16[72,3072]{1,0:T(8,128)(2,1)S(1)}, bf16[72,3072]{1,0:T(8,128)(2,1)S(1)}, u32[]{:S(2)}, u32[]{:S(2)}) collective-permute-start(bf16[72,3072]{1,0:T(8,128)(2,1)S(1)} %get-tuple-element.23), channel_id=1, source_target_pairs={{0,1},{1,0},{4,5},{5,4},{8,9},{9,8},{12,13},{13,12},{14,15},{15,14... | collective-permute-start | bytes 1327112 | tf_op jit(solution)/shard_map/ppermute | solution.py:199
  33.1 4.6 %collective-permute-start.16 = (bf16[120,3072]{1,0:T(8,128)(2,1)S(1)}, bf16[120,3072]{1,0:T(8,128)(2,1)S(1)}, u32[]{:S(2)}, u32[]{:S(2)}) collective-permute-start(bf16[120,3072]{1,0:T(8,128)(2,1)S(1)} %get-tuple-element.24), channel_id=1, source_target_pairs={{0,1},{1,0},{4,5},{5,4},{8,9},{9,8},{12,13},{13,12},{14,15},{15,14... | collective-permute-start | bytes 2211848 | tf_op jit(solution)/shard_map/ppermute | solution.py:199
  33.6 5.2 %collective-permute-start.20 = (bf16[24,3072]{1,0:T(8,128)(2,1)S(1)}, bf16[24,3072]{1,0:T(8,128)(2,1)S(1)}, u32[]{:S(2)}, u32[]{:S(2)}) collective-permute-start(bf16[24,3072]{1,0:T(8,128)(2,1)S(1)} %shard_map.69), channel_id=1, source_target_pairs={{0,4},{1,3},{4,8},{5,1},{8,12},{9,5},{12,14},{13,9},{14,10},{15,13... | collective-permute-start | bytes 442376 | tf_op jit(solution)/shard_map/ppermute | solution.py:199
  34.6 8.3 %collective-permute-start.17 = (bf16[24,3072]{1,0:T(8,128)(2,1)S(1)}, bf16[24,3072]{1,0:T(8,128)(2,1)S(1)}, u32[]{:S(2)}, u32[]{:S(2)}) collective-permute-start(bf16[24,3072]{1,0:T(8,128)(2,1)S(1)} %shard_map.70), channel_id=1, source_target_pairs={{0,8},{1,7},{4,12},{5,3},{8,14},{9,1},{12,10},{13,5},{14,6},{15,9}... | collective-permute-start | bytes 442376 | tf_op jit(solution)/shard_map/ppermute | solution.py:199
  37.0 6.0 %collective-permute-start.18 = (bf16[24,3072]{1,0:T(8,128)(2,1)S(1)}, bf16[24,3072]{1,0:T(8,128)(2,1)S(1)}, u32[]{:S(2)}, u32[]{:S(2)}) collective-permute-start(bf16[24,3072]{1,0:T(8,128)(2,1)S(1)} %shard_map.71), channel_id=1, source_target_pairs={{0,4},{1,3},{4,8},{5,1},{8,12},{9,5},{12,14},{13,9},{14,10},{15,13... | collective-permute-start | bytes 442376 | tf_op jit(solution)/shard_map/ppermute | solution.py:199
  38.8 6.8 %collective-permute-start.21 = (bf16[24,3072]{1,0:T(8,128)(2,1)S(1)}, bf16[24,3072]{1,0:T(8,128)(2,1)S(1)}, u32[]{:S(2)}, u32[]{:S(2)}) collective-permute-start(bf16[24,3072]{1,0:T(8,128)(2,1)S(1)} %shard_map.73), channel_id=1, source_target_pairs={{0,4},{1,3},{4,8},{5,1},{8,12},{9,5},{12,14},{13,9},{14,10},{15,13... | collective-permute-start | bytes 442376 | tf_op jit(solution)/shard_map/ppermute | solution.py:199
  40.8 5.4 %collective-permute-start.23 = (bf16[24,3072]{1,0:T(8,128)(2,1)S(1)}, bf16[24,3072]{1,0:T(8,128)(2,1)S(1)}, u32[]{:S(2)}, u32[]{:S(2)}) collective-permute-start(bf16[24,3072]{1,0:T(8,128)(2,1)S(1)} %shard_map.74), channel_id=1, source_target_pairs={{0,4},{1,3},{4,8},{5,1},{8,12},{9,5},{12,14},{13,9},{14,10},{15,13... | collective-permute-start | bytes 442376 | tf_op jit(solution)/shard_map/ppermute | solution.py:199
  43.1 7.1 %collective-permute-start.19 = (bf16[24,3072]{1,0:T(8,128)(2,1)S(1)}, bf16[24,3072]{1,0:T(8,128)(2,1)S(1)}, u32[]{:S(2)}, u32[]{:S(2)}) collective-permute-start(bf16[24,3072]{1,0:T(8,128)(2,1)S(1)} %shard_map.72), channel_id=1, source_target_pairs={{0,8},{1,7},{4,12},{5,3},{8,14},{9,1},{12,10},{13,5},{14,6},{15,9}... | collective-permute-start | bytes 442376 | tf_op jit(solution)/shard_map/ppermute | solution.py:199
  45.7 5.4 %collective-permute-start.22 = (bf16[24,3072]{1,0:T(8,128)(2,1)S(1)}, bf16[24,3072]{1,0:T(8,128)(2,1)S(1)}, u32[]{:S(2)}, u32[]{:S(2)}) collective-permute-start(bf16[24,3072]{1,0:T(8,128)(2,1)S(1)} %shard_map.75), channel_id=1, source_target_pairs={{0,5},{1,2},{4,9},{5,0},{8,13},{9,4},{12,15},{13,8},{14,11},{15,12... | collective-permute-start | bytes 442376 | tf_op jit(solution)/shard_map/ppermute | solution.py:199
  (8 other events, 170.8 us)
